TPU v7x, 32 devices: a whole 2x2x4 slice. The times are simulated.
32 devices in a mesh: rows: 16 (over z, y, x), cols: 2 (over core).
Axes of the slice: x: 2, y: 2, z: 4, core: 2. Of those that a mesh axis runs over, the one named last changes fastest.
Arguments:
- features: bfloat16 [64, 512, 2048], P('rows', 'cols'), may hold values from -6 to 6
- reduce_weight: bfloat16 [2048, 512], replicated, may hold values from -0.125 to 0.125
- dilated_weight: bfloat16 [9, 512, 512], replicated, may hold values from -0.09375 to 0.09375
- expand_weight: bfloat16 [512, 2048], replicated, may hold values from -0.25 to 0.25
- mid_gain: float32 [2, 512], replicated, may hold values from 0.5 to 1.5
- mid_shift: float32 [2, 512], replicated, may hold values from -2 to 2
- out_gain: float32 [2048], replicated, may hold values from 0.5 to 1.5
- out_shift: float32 [2048], replicated, may hold values from -2 to 2
- aspp_point: bfloat16 [2048, 256], replicated, may hold values from -0.125 to 0.125
- sep_depth: bfloat16 [3, 9, 2048], replicated, may hold values from -2 to 2
- sep_point: bfloat16 [3, 2048, 256], replicated, may hold values from -0.125 to 0.125
- pool_weight: bfloat16 [2048, 256], replicated, may hold values from -0.125 to 0.125
- proj_weight: bfloat16 [1280, 256], replicated, may hold values from -0.15625 to 0.15625
- aspp_gain: float32 [5, 256], replicated, may hold values from 0.5 to 1.5
- aspp_shift: float32 [5, 256], replicated, may hold values from -2 to 2
- head_weight: bfloat16 [256, 17], replicated, may hold values from -0.75 to 0.75
- head_bias: float32 [17], replicated, may hold values from -3 to 3
- task_scales: float32 [3], replicated, may hold values from -1 to 1
- crop_ids: int32 [64, 512], P('rows', 'cols'), may hold values from 0 to 15, as said below
- labels: int32 [64, 512], P('rows', 'cols'), may hold values from 0 to 12
- boundary_mask: int32 [64, 512], P('rows', 'cols'), may hold values from 0 to 1, as said below
- valid_mask: int32 [64, 512], P('rows', 'cols'), may hold values from 0 to 1
- geometry_target: float32 [4, 64, 512], P(None, 'rows', 'cols'), may hold values from -6 to 6
Outputs:
- objective: float32 [], replicated
- grad_features: bfloat16 [64, 512, 2048], P('rows', 'cols')
- grad_reduce_weight: float32 [2048, 512], replicated
- grad_dilated_weight: float32 [9, 512, 512], replicated
- grad_expand_weight: float32 [512, 2048], replicated
- grad_mid_gain: float32 [2, 512], replicated
- grad_mid_shift: float32 [2, 512], replicated
- grad_out_gain: float32 [2048], replicated
- grad_out_shift: float32 [2048], replicated
- grad_aspp_point: float32 [2048, 256], replicated
- grad_sep_depth: float32 [3, 9, 2048], replicated
- grad_sep_point: float32 [3, 2048, 256], replicated
- grad_pool_weight: float32 [2048, 256], replicated
- grad_proj_weight: float32 [1280, 256], replicated
- grad_aspp_gain: float32 [5, 256], replicated
- grad_aspp_shift: float32 [5, 256], replicated
- grad_head_weight: float32 [256, 17], replicated
- grad_head_bias: float32 [17], replicated
- grad_task_scales: float32 [3], replicated
Inputs may be any that keep to these rules, and one draw needn't show every extreme that they name: `crop_ids`: each crop covers a rectangle of the canvas and has pixels; crop 0 covers all 64 rows. `boundary_mask`: the first canvas row has no ones, so the semantic loss always has pixels.
All inputs are finite; a program needn't handle non-finite values.
Results may differ from a plain program's by a relative error of at most 0.03.
Values may be sent and summed in bfloat16 or wider, within the bound.
A program may use at most 448 MiB of HBM per device.

v0:
```python
import jax
import jax.numpy as jnp
from jax import lax
from jax.sharding import PartitionSpec as P

CLASSES = 13
CROPS = 16
MID_RATE = 4
BASE_RATE = 12


EPS = 1e-05


def extended(block, sides, width):
    for axis, dim in sides:
        count = lax.axis_size(axis)
        forward = [(i, i + 1) for i in range(count - 1)]
        backward = [(target, source) for source, target in forward]
        low = lax.ppermute(
            lax.slice_in_dim(block, block.shape[dim] - width, None, axis=dim), axis, forward
        )
        high = lax.ppermute(lax.slice_in_dim(block, 0, width, axis=dim), axis, backward)
        block = jnp.concatenate([low, block, high], axis=dim)
    return block


def from_behind(value, axis, steps):
    count = lax.axis_size(axis)
    initial, last = (max(0, -steps), min(count, count - steps))
    return lax.ppermute(value, axis, [(source, source + steps) for source in range(initial, last)])


def sigmoid_linear(value):
    return value * jax.nn.sigmoid(value)


def gate_slope(value):
    sigma = jax.nn.sigmoid(value)
    return sigma * (1.0 + value * (1.0 - sigma))


def matmul(left, right):
    return jnp.dot(left, right, preferred_element_type=jnp.float32)


def fetch(block, rate):
    step = rate // block.shape[0]
    widened = extended(block, (("cols", 1),), rate)
    moved = {}
    for sign in (1, -1):
        moved[sign] = from_behind(widened, "rows", sign * step)
    return (moved[1], widened, moved[-1])


def offset_piece(near, index, rate, width):
    start = rate + (index % 3 - 1) * rate
    rows_part = near[index // 3]
    return rows_part[:, start : start + width, :].reshape(-1, rows_part.shape[2])


def norm_forward(value, count):
    totals = lax.psum(jnp.sum(value, axis=1), ("rows", "cols"))
    center = totals / count
    centered = value - center[:, None, :]
    spread = lax.psum(jnp.sum(centered * centered, axis=1), ("rows", "cols")) / count
    scale = lax.rsqrt(spread + EPS)
    return (centered * scale[:, None, :], scale)


def norm_backward(upstream, normed, scale, gain, count):
    shift_grad, gain_grad = lax.psum(
        (jnp.sum(upstream, axis=1), jnp.sum(upstream * normed, axis=1)), ("rows", "cols")
    )
    inner = upstream - shift_grad[:, None, :] / count - normed * (gain_grad / count)[:, None, :]
    return (inner * (gain * scale)[:, None, :], gain_grad, shift_grad)


def on_device(
    features,
    reduce_weight,
    dilated_weight,
    expand_weight,
    mid_gain,
    mid_shift,
    out_gain,
    out_shift,
    aspp_point,
    sep_depth,
    sep_point,
    pool_weight,
    proj_weight,
    aspp_gain,
    aspp_shift,
    head_weight,
    head_bias,
    task_scales,
    crop_ids,
    labels,
    boundary_mask,
    valid_mask,
    geometry_target,
):
    height, width, channels = features.shape
    pixels = height * width
    count = float(pixels * lax.axis_size("rows") * lax.axis_size("cols"))
    highest = lax.Precision.HIGHEST
    flat = features.reshape(pixels, channels)
    reduced = matmul(flat, reduce_weight)
    normed_one, scale_one = norm_forward(reduced[None], count)
    gated_one = normed_one[0] * mid_gain[0] + mid_shift[0]
    first_act = sigmoid_linear(gated_one).astype(jnp.bfloat16)
    first_field = first_act.reshape(height, width, -1)
    first_near = fetch(first_field, MID_RATE)
    dilated = jnp.zeros((pixels, dilated_weight.shape[2]), jnp.float32)
    for index in range(9):
        dilated = dilated + matmul(
            offset_piece(first_near, index, MID_RATE, width), dilated_weight[index]
        )
    normed_two, scale_two = norm_forward(dilated[None], count)
    gated_two = normed_two[0] * mid_gain[1] + mid_shift[1]
    second_act = sigmoid_linear(gated_two).astype(jnp.bfloat16)
    expanded = matmul(second_act, expand_weight)
    normed_three, scale_three = norm_forward(expanded[None], count)
    pre_trunk = normed_three[0] * out_gain + out_shift + flat.astype(jnp.float32)
    trunk = sigmoid_linear(pre_trunk).astype(jnp.bfloat16)
    field = trunk.reshape(height, width, channels)
    branch_pre = [matmul(trunk, aspp_point)]
    trunk_near = []
    separable = []
    for index in range(3):
        rate = BASE_RATE * (index + 1)
        near = fetch(field, rate)
        trunk_near.append(near)
        mixed = jnp.zeros((pixels, channels), jnp.float32)
        for tap in range(9):
            mixed = mixed + offset_piece(near, tap, rate, width).astype(jnp.float32) * sep_depth[
                index, tap
            ].astype(jnp.float32)
        separable.append(mixed.astype(jnp.bfloat16))
        branch_pre.append(matmul(separable[index], sep_point[index]))
    stacked = jnp.stack(branch_pre)
    normed_branch, scale_branch = norm_forward(stacked, count)
    gated_branch = normed_branch * aspp_gain[:4, None, :] + aspp_shift[:4, None, :]
    branch_act = sigmoid_linear(gated_branch).astype(jnp.bfloat16)
    crop_flat = crop_ids.reshape(pixels)
    members = (crop_flat[:, None] == jnp.arange(CROPS)[None, :]).astype(jnp.bfloat16)
    members_wide = members.astype(jnp.float32)
    keep = (1 - boundary_mask.reshape(pixels)).astype(jnp.float32)
    valid = valid_mask.reshape(pixels).astype(jnp.float32)
    local_sums = jnp.einsum("pk,pc->kc", members, trunk, preferred_element_type=jnp.float32)
    crop_sums, crop_count, keep_count, valid_count = lax.psum(
        (local_sums, jnp.sum(members_wide, axis=0), jnp.sum(keep), jnp.sum(valid)), ("rows", "cols")
    )
    pooled = (crop_sums / crop_count[:, None]).astype(jnp.bfloat16)
    crop_pre = matmul(pooled, pool_weight)
    crop_act = sigmoid_linear(crop_pre).astype(jnp.bfloat16)
    crop_spread = matmul(members, crop_act).astype(jnp.bfloat16)
    joined = jnp.concatenate(
        [branch_act[0], branch_act[1], branch_act[2], branch_act[3], crop_spread], axis=1
    )
    projected = matmul(joined, proj_weight)
    normed_proj, scale_proj = norm_forward(projected[None], count)
    gated_proj = normed_proj[0] * aspp_gain[4] + aspp_shift[4]
    united = sigmoid_linear(gated_proj).astype(jnp.bfloat16)
    heads = matmul(united, head_weight) + head_bias
    logits = heads[:, :CLASSES]
    top = jnp.max(logits, axis=1, keepdims=True)
    exps = jnp.exp(logits - top)
    totals = jnp.sum(exps, axis=1)
    label_hot = (labels.reshape(pixels)[:, None] == jnp.arange(CLASSES)[None, :]).astype(
        jnp.float32
    )
    picked = jnp.sum(logits * label_hot, axis=1)
    target = geometry_target.reshape(4, pixels)
    depth_error = heads[:, CLASSES] - target[0]
    root = jnp.sqrt(depth_error * depth_error + 1.0)
    normal_error = heads[:, CLASSES + 1 :] - target[1:].T
    local_losses = jnp.stack(
        [
            jnp.sum(keep * (top[:, 0] + jnp.log(totals) - picked)),
            jnp.sum(valid * (root - 1.0)),
            jnp.sum(valid * jnp.sum(normal_error * normal_error, axis=1)),
        ]
    )
    loss_sums = lax.psum(local_losses, ("rows", "cols"))
    counts = jnp.stack([keep_count, valid_count, valid_count])
    losses = loss_sums / counts
    scale_exp = jnp.exp(task_scales)
    objective = jnp.sum(scale_exp * losses - task_scales)
    grad_scales = scale_exp * losses - 1.0
    factor = scale_exp / counts
    logit_grad = factor[0] * keep[:, None] * (exps / totals[:, None] - label_hot)
    depth_grad = factor[1] * valid * depth_error / root
    normal_grad = factor[2] * valid[:, None] * 2.0 * normal_error
    head_grad = jnp.concatenate([logit_grad, depth_grad[:, None], normal_grad], axis=1)
    grad_head_bias = jnp.sum(head_grad, axis=0)
    head_low = head_grad.astype(jnp.bfloat16)
    grad_head_weight = jnp.einsum("pc,pk->ck", united, head_low, preferred_element_type=jnp.float32)
    united_grad = jnp.einsum("pk,ck->pc", head_low, head_weight, preferred_element_type=jnp.float32)
    proj_grad, proj_gain_grad, proj_shift_grad = norm_backward(
        (united_grad * gate_slope(gated_proj))[None], normed_proj, scale_proj, aspp_gain[4:5], count
    )
    proj_low = proj_grad[0].astype(jnp.bfloat16)
    grad_proj_weight = jnp.einsum("pc,pd->cd", joined, proj_low, preferred_element_type=jnp.float32)
    joined_grad = jnp.einsum("pd,cd->pc", proj_low, proj_weight, preferred_element_type=jnp.float32)
    aspp_width = proj_weight.shape[1]
    branch_up = jnp.stack(
        [joined_grad[:, branch * aspp_width : (branch + 1) * aspp_width] for branch in range(4)]
    )
    branch_grad, branch_gain_grad, branch_shift_grad = norm_backward(
        branch_up * gate_slope(gated_branch), normed_branch, scale_branch, aspp_gain[:4], count
    )
    branch_low = branch_grad.astype(jnp.bfloat16)
    crop_local = jnp.einsum(
        "pk,pc->kc", members_wide, joined_grad[:, 4 * aspp_width :], precision=highest
    )
    crop_total = lax.psum(crop_local, ("rows", "cols"))
    crop_low = (crop_total * gate_slope(crop_pre)).astype(jnp.bfloat16)
    grad_pool_weight = jnp.einsum("kc,kd->cd", pooled, crop_low, preferred_element_type=jnp.float32)
    pooled_grad = (
        jnp.einsum("kd,cd->kc", crop_low, pool_weight, preferred_element_type=jnp.float32)
        / crop_count[:, None]
    )
    trunk_grad = jnp.einsum(
        "pd,cd->pc", branch_low[0], aspp_point, preferred_element_type=jnp.float32
    )
    trunk_grad = trunk_grad + jnp.dot(members_wide, pooled_grad, precision=highest)
    grad_aspp_point = jnp.einsum(
        "pc,pd->cd", trunk, branch_low[0], preferred_element_type=jnp.float32
    )
    point_grads = []
    depth_grads = []
    for index in range(3):
        rate = BASE_RATE * (index + 1)
        point_grads.append(
            jnp.einsum(
                "pc,pd->cd",
                separable[index],
                branch_low[index + 1],
                preferred_element_type=jnp.float32,
            )
        )
        tap_grads = []
        sep_low = jnp.einsum(
            "pd,cd->pc", branch_low[index + 1], sep_point[index], preferred_element_type=jnp.float32
        ).astype(jnp.bfloat16)
        sep_wide = sep_low.astype(jnp.float32)
        near = trunk_near[index]
        grad_near = fetch(sep_low.reshape(height, width, channels), rate)
        for tap in range(9):
            tap_grads.append(
                jnp.sum(offset_piece(near, tap, rate, width).astype(jnp.float32) * sep_wide, axis=0)
            )
            trunk_grad = trunk_grad + offset_piece(grad_near, 8 - tap, rate, width).astype(
                jnp.float32
            ) * sep_depth[index, tap].astype(jnp.float32)
        depth_grads.append(jnp.stack(tap_grads))
    pre_grad = trunk_grad * gate_slope(pre_trunk)
    expand_grad, out_gain_grad, out_shift_grad = norm_backward(
        pre_grad[None], normed_three, scale_three, out_gain[None], count
    )
    expand_low = expand_grad[0].astype(jnp.bfloat16)
    grad_expand_weight = jnp.einsum(
        "pc,pd->cd", second_act, expand_low, preferred_element_type=jnp.float32
    )
    second_grad = jnp.einsum(
        "pd,cd->pc", expand_low, expand_weight, preferred_element_type=jnp.float32
    )
    dilated_grad, two_gain_grad, two_shift_grad = norm_backward(
        (second_grad * gate_slope(gated_two))[None], normed_two, scale_two, mid_gain[1:2], count
    )
    dilated_low = dilated_grad[0].astype(jnp.bfloat16)
    dilated_near = fetch(dilated_low.reshape(height, width, -1), MID_RATE)
    first_grad = jnp.zeros((pixels, dilated_weight.shape[1]), jnp.float32)
    dilated_grads = []
    for tap in range(9):
        dilated_grads.append(
            jnp.einsum(
                "pc,pd->cd",
                offset_piece(first_near, tap, MID_RATE, width),
                dilated_low,
                preferred_element_type=jnp.float32,
            )
        )
        first_grad = first_grad + jnp.einsum(
            "pd,cd->pc",
            offset_piece(dilated_near, 8 - tap, MID_RATE, width),
            dilated_weight[tap],
            preferred_element_type=jnp.float32,
        )
    reduced_grad, one_gain_grad, one_shift_grad = norm_backward(
        (first_grad * gate_slope(gated_one))[None], normed_one, scale_one, mid_gain[0:1], count
    )
    reduced_low = reduced_grad[0].astype(jnp.bfloat16)
    grad_reduce_weight = jnp.einsum(
        "pc,pd->cd", flat, reduced_low, preferred_element_type=jnp.float32
    )
    input_grad = (
        jnp.einsum("pd,cd->pc", reduced_low, reduce_weight, preferred_element_type=jnp.float32)
        + pre_grad
    )
    grad_features = input_grad.astype(jnp.bfloat16).reshape(height, width, channels)
    summed = lax.psum(
        (
            grad_reduce_weight,
            jnp.stack(dilated_grads),
            grad_expand_weight,
            grad_aspp_point,
            jnp.stack(depth_grads),
            jnp.stack(point_grads),
            grad_proj_weight,
            grad_head_weight,
            grad_head_bias,
        ),
        ("rows", "cols"),
    )
    grad_mid_gain = jnp.concatenate([one_gain_grad, two_gain_grad], axis=0)
    grad_mid_shift = jnp.concatenate([one_shift_grad, two_shift_grad], axis=0)
    grad_aspp_gain = jnp.concatenate([branch_gain_grad, proj_gain_grad], axis=0)
    grad_aspp_shift = jnp.concatenate([branch_shift_grad, proj_shift_grad], axis=0)
    return (
        objective,
        grad_features,
        summed[0],
        summed[1],
        summed[2],
        grad_mid_gain,
        grad_mid_shift,
        out_gain_grad[0],
        out_shift_grad[0],
        summed[3],
        summed[4],
        summed[5],
        grad_pool_weight,
        summed[6],
        grad_aspp_gain,
        grad_aspp_shift,
        summed[7],
        summed[8],
        grad_scales,
    )


def solution(mesh):
    in_specs = (
        P("rows", "cols", None),
        P(),
        P(),
        P(),
        P(),
        P(),
        P(),
        P(),
        P(),
        P(),
        P(),
        P(),
        P(),
        P(),
        P(),
        P(),
        P(),
        P(),
        P("rows", "cols"),
        P("rows", "cols"),
        P("rows", "cols"),
        P("rows", "cols"),
        P(None, "rows", "cols"),
    )
    out_specs = (
        P(),
        P("rows", "cols", None),
        P(),
        P(),
        P(),
        P(),
        P(),
        P(),
        P(),
        P(),
        P(),
        P(),
        P(),
        P(),
        P(),
        P(),
        P(),
        P(),
        P(),
    )
    return jax.shard_map(
        on_device, mesh=mesh, in_specs=in_specs, out_specs=out_specs, check_vma=False
    )
```

profile of v0, /device:TPU:11, one launch (start us, length us, event | category | flops | bytes accessed | tf_op | source)
XLA Modules:
  0.0 2927.6 jit_solution(61339337665500397)
XLA Ops:
  13.9 39.5 %psum.245 = f32[1,512]{1,0:T(1,128)S(1)} all-reduce(f32[1,512]{1,0:T(1,128)S(1)} %bitcast.787), channel_id=1, replica_groups=mesh['rows'=16,'cols'=2] {'rows','cols'}, use_global_device_ids=true, to_apply=%region_1.0 | all-reduce | flops 512 | bytes 4096 | tf_op jit(solution)/shard_map/psum | solution.py:63
  55.3 40.0 %psum.246 = f32[1,512]{1,0:T(1,128)S(1)} all-reduce(f32[1,512]{1,0:T(1,128)S(1)} %bitcast.772), channel_id=1, replica_groups=mesh['rows'=16,'cols'=2] {'rows','cols'}, use_global_device_ids=true, to_apply=%region_3.0 | all-reduce | flops 512 | bytes 4096 | tf_op jit(solution)/shard_map/psum | solution.py:66
  112.8 19.1 collective-permute-done.3
  133.7 23.1 collective-permute-done.2
  161.8 39.0 %psum.247 = f32[1,512]{1,0:T(1,128)S(1)} all-reduce(f32[1,512]{1,0:T(1,128)S(1)} %bitcast.774), channel_id=1, replica_groups=mesh['rows'=16,'cols'=2] {'rows','cols'}, use_global_device_ids=true, to_apply=%region_5.0 | all-reduce | flops 512 | bytes 4096 | tf_op jit(solution)/shard_map/psum | solution.py:63
  202.7 39.0 %psum.248 = f32[1,512]{1,0:T(1,128)S(1)} all-reduce(f32[1,512]{1,0:T(1,128)S(1)} %bitcast.773), channel_id=1, replica_groups=mesh['rows'=16,'cols'=2] {'rows','cols'}, use_global_device_ids=true, to_apply=%region_7.0 | all-reduce | flops 512 | bytes 4096 | tf_op jit(solution)/shard_map/psum | solution.py:66
  249.9 41.5 %psum.249 = f32[1,2048]{1,0:T(1,128)S(1)} all-reduce(f32[1,2048]{1,0:T(1,128)S(1)} %bitcast.771), channel_id=1, replica_groups=mesh['rows'=16,'cols'=2] {'rows','cols'}, use_global_device_ids=true, to_apply=%region_9.0 | all-reduce | flops 2048 | bytes 16384 | tf_op jit(solution)/shard_map/psum | solution.py:63
  295.7 38.8 %psum.250 = f32[1,2048]{1,0:T(1,128)S(1)} all-reduce(f32[1,2048]{1,0:T(1,128)S(1)} %bitcast.727), channel_id=1, replica_groups=mesh['rows'=16,'cols'=2] {'rows','cols'}, use_global_device_ids=true, to_apply=%region_11.0 | all-reduce | flops 2048 | bytes 16384 | tf_op jit(solution)/shard_map/psum | solution.py:66
  424.8 33.9 %collective-permute-done.7 = bf16[4,280,2048]{2,1,0:T(8,128)(2,1)} collective-permute-done((bf16[4,280,2048]{2,1,0:T(8,128)(2,1)}, bf16[4,280,2048]{2,1,0:T(8,128)(2,1)}, u32[]{:S(2)}, u32[]{:S(2)}) %collective-permute-start.7) | collective-permute-done | bytes 4587552 | tf_op jit(solution)/shard_map/ppermute | solution.py:31
  472.2 91.1 %collective-permute-done.6 = bf16[4,280,2048]{2,1,0:T(8,128)(2,1)} collective-permute-done((bf16[4,280,2048]{2,1,0:T(8,128)(2,1)}, bf16[4,280,2048]{2,1,0:T(8,128)(2,1)}, u32[]{:S(2)}, u32[]{:S(2)}) %collective-permute-start.6) | collective-permute-done | bytes 4587552 | tf_op jit(solution)/shard_map/ppermute | solution.py:31
  596.1 65.7 %collective-permute-done.10 = bf16[4,304,2048]{2,1,0:T(8,128)(2,1)S(1)} collective-permute-done((bf16[4,304,2048]{2,1,0:T(8,128)(2,1)}, bf16[4,304,2048]{2,1,0:T(8,128)(2,1)S(1)}, u32[]{:S(2)}, u32[]{:S(2)}) %collective-permute-start.10) | collective-permute-done | bytes 4980768 | tf_op jit(solution)/shard_map/ppermute | solution.py:31
  699.6 193.0 %collective-permute-done.14 = bf16[4,328,2048]{2,1,0:T(8,128)(2,1)} collective-permute-done((bf16[4,328,2048]{2,1,0:T(8,128)(2,1)}, bf16[4,328,2048]{2,1,0:T(8,128)(2,1)}, u32[]{:S(2)}, u32[]{:S(2)}) %collective-permute-start.14) | collective-permute-done | bytes 5373984 | tf_op jit(solution)/shard_map/ppermute | solution.py:31
  913.2 175.3 %psum.251 = f32[4,256]{1,0:T(4,128)S(1)} all-reduce(f32[4,256]{1,0:T(4,128)S(1)} %fusion.195), channel_id=1, replica_groups=mesh['rows'=16,'cols'=2] {'rows','cols'}, use_global_device_ids=true, to_apply=%region_13.0 | all-reduce | flops 1024 | bytes 8192 | tf_op jit(solution)/shard_map/psum | solution.py:63
  1090.8 40.0 %all-reduce.6 = (f32[4,256]{1,0:T(4,128)S(1)}, f32[16]{0:T(128)S(1)}) all-reduce(f32[4,256]{1,0:T(4,128)S(1)} %multiply_reduce_fusion.3, f32[16]{0:T(128)S(1)} %copy-done.181), channel_id=1, replica_groups=mesh['rows'=16,'cols'=2] {'rows','cols'}, use_global_device_ids=true, to_apply=%region_15.0 | all-reduce | flops 1040 | bytes 8320 | tf_op jit(solution)/shard_map/psum | solution.py:66
  1143.6 40.2 %psum.255 = f32[1,256]{1,0:T(1,128)S(1)} all-reduce(f32[1,256]{1,0:T(1,128)S(1)} %bitcast.796), channel_id=1, replica_groups=mesh['rows'=16,'cols'=2] {'rows','cols'}, use_global_device_ids=true, to_apply=%region_20.0 | all-reduce | flops 256 | bytes 2048 | tf_op jit(solution)/shard_map/psum | solution.py:63
  1185.2 39.7 %psum.256 = f32[1,256]{1,0:T(1,128)S(1)} all-reduce(f32[1,256]{1,0:T(1,128)S(1)} %bitcast.784), channel_id=1, replica_groups=mesh['rows'=16,'cols'=2] {'rows','cols'}, use_global_device_ids=true, to_apply=%region_22.0 | all-reduce | flops 256 | bytes 2048 | tf_op jit(solution)/shard_map/psum | solution.py:66
  1229.7 41.1 %all-reduce.5 = (f32[1]{0:T(128)}, f32[1]{0:T(128)}) all-reduce(f32[1]{0:T(128)} %bitcast.89, f32[1]{0:T(128)} %bitcast.88), channel_id=1, replica_groups=mesh['rows'=16,'cols'=2] {'rows','cols'}, use_global_device_ids=true, to_apply=%region_34.0 | all-reduce | flops 2 | bytes 16 | tf_op jit(solution)/shard_map/psum | solution.py:152
  1277.8 39.5 %all-reduce.4 = (f32[1,256]{1,0:T(1,128)S(1)}, f32[1,256]{1,0:T(1,128)S(1)}) all-reduce(f32[1,256]{1,0:T(1,128)S(1)} %bitcast.795, f32[1,256]{1,0:T(1,128)S(1)} %bitcast.794), channel_id=1, replica_groups=mesh['rows'=16,'cols'=2] {'rows','cols'}, use_global_device_ids=true, to_apply=%region_39.0 | all-reduce | flops 512 | bytes 4096 | tf_op jit(solution)/shard_map/psum | solution.py:72
  1328.0 40.7 %all-reduce.3 = (f32[4,256]{1,0:T(4,128)S(1)}, f32[4,256]{1,0:T(4,128)S(1)}, f32[16,256]{1,0:T(8,128)S(1)}) all-reduce(f32[4,256]{1,0:T(4,128)S(1)} %get-tuple-element.125, f32[4,256]{1,0:T(4,128)S(1)} %get-tuple-element.124, f32[16,256]{1,0:T(8,128)S(1)} %fusion.89), channel_id=1, replica_groups=mesh['rows'=16,'cols'=2] {'rows','cols'}, use_global_device_ids=true, to_apply=%region_43.0 | all-reduce | flops 6144 | bytes 49152 | tf_op jit(solution)/shard_map/psum | solution.py:72
  1403.8 20.0 fusion.66
  1423.8 47.3 %fusion.50 = (f32[2048]{0:T(1024)}, f32[2048]{0:T(1024)}, f32[2048]{0:T(1024)}, f32[2048]{0:T(1024)}, f32[2048]{0:T(1024)}, /*index=5*/f32[2048]{0:T(1024)}, f32...) fusion(f32[4,256,2048]{2,1,0:T(8,128)} %get-tuple-element.199, ...), kind=kOutput, calls=%fused_computation.83 | convolution fusion | flops 1159688192 | bytes 144326656 | tf_op jit(solution)/shard_map/pd,cd->pc/dot_general | solution.py:245
  1564.8 37.1 %collective-permute-done.18 = bf16[4,280,2048]{2,1,0:T(8,128)(2,1)} collective-permute-done((bf16[4,280,2048]{2,1,0:T(8,128)(2,1)}, bf16[4,280,2048]{2,1,0:T(8,128)(2,1)}, u32[]{:S(2)}, u32[]{:S(2)}) %collective-permute-start.18) | collective-permute-done | bytes 4587552 | tf_op jit(solution)/shard_map/ppermute | solution.py:31
  1601.9 65.3 %collective-permute-start.27 = (bf16[4,328,2048]{2,1,0:T(8,128)(2,1)}, bf16[4,328,2048]{2,1,0:T(8,128)(2,1)S(1)}, u32[]{:S(2)}, u32[]{:S(2)}) collective-permute-start(bf16[4,328,2048]{2,1,0:T(8,128)(2,1)} %pad_maximum_fusion.2), channel_id=1, source_target_pairs={{0,18},{2,20},{4,22},{6,24},{8,26},{10,28},{12,30},{1,19},{3,21},{... | collective-permute-start | bytes 16121864 | tf_op jit(solution)/shard_map/ppermute | solution.py:31
  1690.1 25.3 collective-permute-done.19
  1739.3 65.3 %collective-permute-done.23 = bf16[4,304,2048]{2,1,0:T(8,128)(2,1)} collective-permute-done((bf16[4,304,2048]{2,1,0:T(8,128)(2,1)}, bf16[4,304,2048]{2,1,0:T(8,128)(2,1)}, u32[]{:S(2)}, u32[]{:S(2)}) %collective-permute-start.23) | collective-permute-done | bytes 4980768 | tf_op jit(solution)/shard_map/ppermute | solution.py:31
  1813.4 206.4 %collective-permute-done.26 = bf16[4,328,2048]{2,1,0:T(8,128)(2,1)S(1)} collective-permute-done((bf16[4,328,2048]{2,1,0:T(8,128)(2,1)}, bf16[4,328,2048]{2,1,0:T(8,128)(2,1)S(1)}, u32[]{:S(2)}, u32[]{:S(2)}) %collective-permute-start.26) | collective-permute-done | bytes 5373984 | tf_op jit(solution)/shard_map/ppermute | solution.py:31
  2039.9 52.3 %fusion.196 = (f32[2048]{0:T(1024)S(1)}, f32[2048]{0:T(1024)S(1)}, f32[1024,2048]{1,0:T(8,128)}) fusion(f32[1024,2048]{1,0:T(8,128)} %copy-done.7, bf16[4,256,2048]{2,1,0:T(8,128)(2,1)} %param.23, f32[2048]{0:T(1024)S(1)} %copy-done.84, f32[2048]{0:T(1024)S(1)} %copy-done.80, f32[2048]{0:T(1024)S(1)} %bitcast.659, ...), kind=kOutput, calls=%fused_computation.459 | convolution fusion | flops 1277161472 | bytes 144433152 | tf_op jit(solution)/shard_map/pd,cd->pc/dot_general | solution.py:225
  2092.2 184.1 %all-reduce.2 = (f32[1,2048]{1,0:T(1,128)S(1)}, f32[2048]{0:T(1024)S(1)}) all-reduce(f32[1,2048]{1,0:T(1,128)S(1)} %bitcast.770, f32[2048]{0:T(1024)S(1)} %get-tuple-element.95), channel_id=1, replica_groups=mesh['rows'=16,'cols'=2] {'rows','cols'}, use_global_device_ids=true, to_apply=%region_48.0 | all-reduce | flops 4096 | bytes 32768 | tf_op jit(solution)/shard_map/psum | solution.py:72
  2298.1 39.6 %all-reduce.1 = (f32[1,512]{1,0:T(1,128)S(1)}, f32[1,512]{1,0:T(1,128)S(1)}) all-reduce(f32[1,512]{1,0:T(1,128)S(1)} %bitcast.786, f32[1,512]{1,0:T(1,128)S(1)} %bitcast.785), channel_id=1, replica_groups=mesh['rows'=16,'cols'=2] {'rows','cols'}, use_global_device_ids=true, to_apply=%region_52.0 | all-reduce | flops 1024 | bytes 8192 | tf_op jit(solution)/shard_map/psum | solution.py:72
  2363.1 42.9 %collective-permute-done.31 = bf16[4,264,512]{2,1,0:T(8,128)(2,1)S(1)} collective-permute-done((bf16[4,264,512]{2,1,0:T(8,128)(2,1)S(1)}, bf16[4,264,512]{2,1,0:T(8,128)(2,1)S(1)}, u32[]{:S(2)}, u32[]{:S(2)}) %collective-permute-start.31) | collective-permute-done | bytes 1081376 | tf_op jit(solution)/shard_map/ppermute | solution.py:31
  2413.6 40.4 %all-reduce = (f32[3]{0:T(128)S(1)}, f32[1,512]{1,0:T(1,128)S(1)}, f32[1,512]{1,0:T(1,128)S(1)}, f32[256,17]{0,1:T(8,128)}, f32[17]{0:T(128)}) all-reduce(f32[3]{0:T(128)S(1)} %copy-done.188, f32[1,512]{1,0:T(1,128)S(1)} %bitcast.768, f32[1,512]{1,0:T(1,128)S(1)} %bitcast.767, ...), channel_id=1, replica_groups=mesh['rows'=16,'cols'=2] {'rows','cols'}, use_global_device_ids=true, to_apply=%region_30.0 | all-reduce | flops 5396 | bytes 43168 | tf_op jit(solution)/shard_map/psum | solution.py:186
  2477.4 419.2 %all-reduce.13.cloned.1.call-done = (f32[2048,512]{0,1:T(8,128)}, f32[9,512,512]{2,1,0:T(8,128)}, f32[512,2048]{1,0:T(8,128)}, f32[2048,256]{1,0:T(8,128)}, f32[...) async-done(((f32[2048,512]{0,1:T(8,128)}, f32[9,512,512]{2,1,0:T(8,128)}, f32[512,2048]{1,0:T(8,128)}, f32[2048,256]{1,0:T(8,128)}, ...) | async-done | bytes 27746320 | tf_op jit(solution)/shard_map/psum | solution.py:304
  (655 shorter events, 585.0 us)
Async XLA Ops:
  7.2 1129.8 %all-reduce.11.cloned.1.call-start = ((), (), s32[]{:S(2)}) async-start(), calls=%async_computation | async-start | bytes 262144 | tf_op jit(solution)/shard_map/psum | solution.py:152
  104.0 27.9 collective-permute-start.3
  106.5 50.2 %collective-permute-start.2 = (bf16[4,264,512]{2,1,0:T(8,128)(2,1)S(1)}, bf16[4,264,512]{2,1,0:T(8,128)(2,1)S(1)}, u32[]{:S(2)}, u32[]{:S(2)}) collective-permute-start(bf16[4,264,512]{2,1,0:T(8,128)(2,1)S(1)} %pad_maximum_fusion.20), channel_id=1, source_target_pairs={{0,2},{2,4},{4,6},{6,8},{8,10},{10,12},{12,14},{14,16},{16,18},{18... | collective-permute-start | bytes 3244040 | tf_op jit(solution)/shard_map/ppermute | solution.py:31
  345.0 6.1 collective-permute-start.4
  346.3 5.9 collective-permute-start.5
  355.1 103.6 %collective-permute-start.7 = (bf16[4,280,2048]{2,1,0:T(8,128)(2,1)}, bf16[4,280,2048]{2,1,0:T(8,128)(2,1)}, u32[]{:S(2)}, u32[]{:S(2)}) collective-permute-start(bf16[4,280,2048]{2,1,0:T(8,128)(2,1)} %pad_maximum_fusion.5), channel_id=1, source_target_pairs={{6,0},{8,2},{10,4},{12,6},{14,8},{16,10},{18,12},{20,14},{22,16},{... | collective-permute-start | bytes 13762568 | tf_op jit(solution)/shard_map/ppermute | solution.py:31
  362.7 11.4 collective-permute-start.8
  364.0 199.3 %collective-permute-start.6 = (bf16[4,280,2048]{2,1,0:T(8,128)(2,1)}, bf16[4,280,2048]{2,1,0:T(8,128)(2,1)}, u32[]{:S(2)}, u32[]{:S(2)}) collective-permute-start(bf16[4,280,2048]{2,1,0:T(8,128)(2,1)} %pad_maximum_fusion.5), channel_id=1, source_target_pairs={{0,6},{2,8},{4,10},{6,12},{8,14},{10,16},{12,18},{14,20},{16,22},{... | collective-permute-start | bytes 13762568 | tf_op jit(solution)/shard_map/ppermute | solution.py:31
  367.3 15.5 collective-permute-start.9
  371.4 20.8 collective-permute-start.12
  374.0 2522.6 %all-reduce.13.cloned.1.call-start = ((), (), s32[]{:S(2)}) async-start(), calls=%async_computation.1 | async-start | bytes 55836672 | tf_op jit(solution)/shard_map/psum | solution.py:304
  374.1 19.4 collective-permute-start.13
  387.2 274.6 %collective-permute-start.10 = (bf16[4,304,2048]{2,1,0:T(8,128)(2,1)}, bf16[4,304,2048]{2,1,0:T(8,128)(2,1)S(1)}, u32[]{:S(2)}, u32[]{:S(2)}) collective-permute-start(bf16[4,304,2048]{2,1,0:T(8,128)(2,1)} %pad_maximum_fusion.3), channel_id=1, source_target_pairs={{0,12},{2,14},{4,16},{6,18},{8,20},{10,22},{12,24},{14,26},{16,28}... | collective-permute-start | bytes 14942216 | tf_op jit(solution)/shard_map/ppermute | solution.py:31
  392.3 269.6 %collective-permute-start.11 = (bf16[4,304,2048]{2,1,0:T(8,128)(2,1)}, bf16[4,304,2048]{2,1,0:T(8,128)(2,1)}, u32[]{:S(2)}, u32[]{:S(2)}) collective-permute-start(bf16[4,304,2048]{2,1,0:T(8,128)(2,1)} %pad_maximum_fusion.3), channel_id=1, source_target_pairs={{12,0},{14,2},{16,4},{18,6},{20,8},{22,10},{24,12},{26,14},{28,16}... | collective-permute-start | bytes 14942216 | tf_op jit(solution)/shard_map/ppermute | solution.py:31
  399.2 493.4 %collective-permute-start.14 = (bf16[4,328,2048]{2,1,0:T(8,128)(2,1)}, bf16[4,328,2048]{2,1,0:T(8,128)(2,1)}, u32[]{:S(2)}, u32[]{:S(2)}) collective-permute-start(bf16[4,328,2048]{2,1,0:T(8,128)(2,1)} %pad_maximum_fusion.1), channel_id=1, source_target_pairs={{0,18},{2,20},{4,22},{6,24},{8,26},{10,28},{12,30},{1,19},{3,21},{... | collective-permute-start | bytes 16121864 | tf_op jit(solution)/shard_map/ppermute | solution.py:31
  458.7 433.9 %collective-permute-start.15 = (bf16[4,328,2048]{2,1,0:T(8,128)(2,1)}, bf16[4,328,2048]{2,1,0:T(8,128)(2,1)S(1)}, u32[]{:S(2)}, u32[]{:S(2)}) collective-permute-start(bf16[4,328,2048]{2,1,0:T(8,128)(2,1)} %pad_maximum_fusion.1), channel_id=1, source_target_pairs={{18,0},{20,2},{22,4},{24,6},{26,8},{28,10},{30,12},{19,1},{21,3},{... | collective-permute-start | bytes 16121864 | tf_op jit(solution)/shard_map/ppermute | solution.py:31
  1472.3 17.4 collective-permute-start.16
  1473.8 20.1 collective-permute-start.17
  1479.5 36.7 %collective-permute-start.20 = (bf16[4,24,2048]{2,1,0:T(8,128)(2,1)S(1)}, bf16[4,24,2048]{2,1,0:T(8,128)(2,1)S(1)}, u32[]{:S(2)}, u32[]{:S(2)}) collective-permute-start(bf16[4,24,2048]{2,1,0:T(8,128)(2,1)S(1)} %get-tuple-element.222), channel_id=1, source_target_pairs={{0,1},{2,3},{4,5},{6,7},{8,9},{10,11},{12,13},{14,15},{16,17},{18,... | collective-permute-start | bytes 1179656 | tf_op jit(solution)/shard_map/ppermute | solution.py:20
  1480.8 39.3 %collective-permute-start.21 = (bf16[4,24,2048]{2,1,0:T(8,128)(2,1)S(1)}, bf16[4,24,2048]{2,1,0:T(8,128)(2,1)S(1)}, u32[]{:S(2)}, u32[]{:S(2)}) collective-permute-start(bf16[4,24,2048]{2,1,0:T(8,128)(2,1)S(1)} %get-tuple-element.223), channel_id=1, source_target_pairs={{1,0},{3,2},{5,4},{7,6},{9,8},{11,10},{13,12},{15,14},{17,16},{19,... | collective-permute-start | bytes 1179656 | tf_op jit(solution)/shard_map/ppermute | solution.py:23
  1486.6 50.8 %collective-permute-start.24 = (bf16[4,36,2048]{2,0,1:T(4,128)(2,1)}, bf16[4,36,2048]{2,0,1:T(4,128)(2,1)S(1)}, u32[]{:S(2)}, u32[]{:S(2)}) collective-permute-start(bf16[4,36,2048]{2,0,1:T(4,128)(2,1)} %copy.66), channel_id=1, source_target_pairs={{0,1},{2,3},{4,5},{6,7},{8,9},{10,11},{12,13},{14,15},{16,17},{18,... | collective-permute-start | bytes 1769480 | tf_op jit(solution)/shard_map/ppermute | solution.py:20
  1489.7 58.3 %collective-permute-start.25 = (bf16[4,36,2048]{2,0,1:T(4,128)(2,1)}, bf16[4,36,2048]{2,0,1:T(4,128)(2,1)}, u32[]{:S(2)}, u32[]{:S(2)}) collective-permute-start(bf16[4,36,2048]{2,0,1:T(4,128)(2,1)} %copy.67), channel_id=1, source_target_pairs={{1,0},{3,2},{5,4},{7,6},{9,8},{11,10},{13,12},{15,14},{17,16},{19,... | collective-permute-start | bytes 1769480 | tf_op jit(solution)/shard_map/ppermute | solution.py:23
  1496.9 105.0 %collective-permute-start.18 = (bf16[4,280,2048]{2,1,0:T(8,128)(2,1)}, bf16[4,280,2048]{2,1,0:T(8,128)(2,1)}, u32[]{:S(2)}, u32[]{:S(2)}) collective-permute-start(bf16[4,280,2048]{2,1,0:T(8,128)(2,1)} %pad_maximum_fusion.6), channel_id=1, source_target_pairs={{6,0},{8,2},{10,4},{12,6},{14,8},{16,10},{18,12},{20,14},{22,16},{... | collective-permute-start | bytes 13762568 | tf_op jit(solution)/shard_map/ppermute | solution.py:31
  1516.1 199.2 %collective-permute-start.19 = (bf16[4,280,2048]{2,1,0:T(8,128)(2,1)}, bf16[4,280,2048]{2,1,0:T(8,128)(2,1)}, u32[]{:S(2)}, u32[]{:S(2)}) collective-permute-start(bf16[4,280,2048]{2,1,0:T(8,128)(2,1)} %pad_maximum_fusion.6), channel_id=1, source_target_pairs={{0,6},{2,8},{4,10},{6,12},{8,14},{10,16},{12,18},{14,20},{16,22},{... | collective-permute-start | bytes 13762568 | tf_op jit(solution)/shard_map/ppermute | solution.py:31
  1522.7 207.7 %collective-permute-start.22 = (bf16[4,304,2048]{2,1,0:T(8,128)(2,1)}, bf16[4,304,2048]{2,1,0:T(8,128)(2,1)}, u32[]{:S(2)}, u32[]{:S(2)}) collective-permute-start(bf16[4,304,2048]{2,1,0:T(8,128)(2,1)} %pad_maximum_fusion.4), channel_id=1, source_target_pairs={{12,0},{14,2},{16,4},{18,6},{20,8},{22,10},{24,12},{26,14},{28,16}... | collective-permute-start | bytes 14942216 | tf_op jit(solution)/shard_map/ppermute | solution.py:31
  1537.4 267.2 %collective-permute-start.23 = (bf16[4,304,2048]{2,1,0:T(8,128)(2,1)}, bf16[4,304,2048]{2,1,0:T(8,128)(2,1)}, u32[]{:S(2)}, u32[]{:S(2)}) collective-permute-start(bf16[4,304,2048]{2,1,0:T(8,128)(2,1)} %pad_maximum_fusion.4), channel_id=1, source_target_pairs={{0,12},{2,14},{4,16},{6,18},{8,20},{10,22},{12,24},{14,26},{16,28}... | collective-permute-start | bytes 14942216 | tf_op jit(solution)/shard_map/ppermute | solution.py:31
  1556.4 463.4 %collective-permute-start.26 = (bf16[4,328,2048]{2,1,0:T(8,128)(2,1)}, bf16[4,328,2048]{2,1,0:T(8,128)(2,1)S(1)}, u32[]{:S(2)}, u32[]{:S(2)}) collective-permute-start(bf16[4,328,2048]{2,1,0:T(8,128)(2,1)} %pad_maximum_fusion.2), channel_id=1, source_target_pairs={{18,0},{20,2},{22,4},{24,6},{26,8},{28,10},{30,12},{19,1},{21,3},{... | collective-permute-start | bytes 16121864 | tf_op jit(solution)/shard_map/ppermute | solution.py:31
  1601.9 432.6 %collective-permute-start.27 = (bf16[4,328,2048]{2,1,0:T(8,128)(2,1)}, bf16[4,328,2048]{2,1,0:T(8,128)(2,1)S(1)}, u32[]{:S(2)}, u32[]{:S(2)}) collective-permute-start(bf16[4,328,2048]{2,1,0:T(8,128)(2,1)} %pad_maximum_fusion.2), channel_id=1, source_target_pairs={{0,18},{2,20},{4,22},{6,24},{8,26},{10,28},{12,30},{1,19},{3,21},{... | collective-permute-start | bytes 16121864 | tf_op jit(solution)/shard_map/ppermute | solution.py:31
  2343.3 11.4 collective-permute-start.28
  2344.6 10.1 collective-permute-start.29
  2355.0 51.1 %collective-permute-start.31 = (bf16[4,264,512]{2,1,0:T(8,128)(2,1)S(1)}, bf16[4,264,512]{2,1,0:T(8,128)(2,1)S(1)}, u32[]{:S(2)}, u32[]{:S(2)}) collective-permute-start(bf16[4,264,512]{2,1,0:T(8,128)(2,1)S(1)} %pad_maximum_fusion.21), channel_id=1, source_target_pairs={{0,2},{2,4},{4,6},{6,8},{8,10},{10,12},{12,14},{14,16},{16,18},{18... | collective-permute-start | bytes 3244040 | tf_op jit(solution)/shard_map/ppermute | solution.py:31
  2359.1 48.8 %collective-permute-start.30 = (bf16[4,264,512]{2,1,0:T(8,128)(2,1)S(1)}, bf16[4,264,512]{2,1,0:T(8,128)(2,1)S(1)}, u32[]{:S(2)}, u32[]{:S(2)}) collective-permute-start(bf16[4,264,512]{2,1,0:T(8,128)(2,1)S(1)} %pad_maximum_fusion.21), channel_id=1, source_target_pairs={{2,0},{4,2},{6,4},{8,6},{10,8},{12,10},{14,12},{16,14},{18,16},{20... | collective-permute-start | bytes 3244040 | tf_op jit(solution)/shard_map/ppermute | solution.py:31
  (201 other events, 8303.8 us)
Sparse Core Ops, SparseCore 0:
  374.2 715.5 all-reduce.10
  2462.0 434.6 all-reduce.12
where the time goes:
time: 2950 us; the launch traced here: 2930 us
  waiting for transfers between devices  1240 us (42%)
  blocking collectives  918 us (31%)
  other arithmetic  247 us (8%)
  matrix products  241 us (8%)
  starting transfers between devices  161 us (5%)
  local copies, waits for them, and re-layouts  105 us (4%)
    ppermute x16, waiting for transfers between devices, from_behind(): lax.ppermute(value, axis, [(source, source + steps) for source in range(i...  818 us
    psum x1, waiting for transfers between devices, on_device(): lax.psum((grad_reduce_weight, jnp.stack(dilated_grads), grad_expand_weigh...  419 us
    psum x5, blocking collectives, norm_forward(): totals = lax.psum(jnp.sum(value, axis=1), ('rows', 'cols'))  336 us
    psum x4, blocking collectives, norm_backward(): lax.psum((jnp.sum(upstream, axis=1), jnp.sum(upstream * normed, axis=1)),...  304 us
    psum x5, blocking collectives, norm_forward(): lax.psum(jnp.sum(centered * centered, axis=1), ('rows', 'cols')) / count  198 us
    ppermute x16, starting transfers between devices, from_behind(): lax.ppermute(value, axis, [(source, source + steps) for source in range(i...  118 us
    convert_element_type x7, other arithmetic, on_device(): offset_piece(near, tap, rate, width).astype(jnp.float32)  82.4 us
    dot_general x3, matrix products, on_device(): jnp.einsum('pd,cd->pc', branch_low[index + 1], sep_point[index], preferre...  72.6 us
  transfers between devices with their start and end apart: 34, of which 15 were waited for; matrix products, arithmetic and copies ran while one was open for 10% of the time, Pallas kernels for 0%

commit v1 on v0

v1 whole, which is shorter than its diff:
```python
import functools

import jax
import jax.numpy as jnp
from jax import lax
from jax.experimental import pallas as pl
from jax.experimental.pallas import tpu as pltpu
from jax.sharding import PartitionSpec as P

CLASSES = 13
CROPS = 16
MID_RATE = 4
BASE_RATE = 12
LANES = 128

EPS = 1e-05
MESH = pl.DeviceIdType.MESH


def gather_kernel(rows, cols, x_ref, out_ref, send, recv):
    devices = rows * cols
    me = lax.axis_index("rows") * cols + lax.axis_index("cols")
    barrier = pltpu.get_barrier_semaphore()

    def peer(step):
        other = lax.rem(me + step, devices)
        return (other // cols, lax.rem(other, cols))

    def greet(step, carry):
        pl.semaphore_signal(barrier, inc=1, device_id=peer(step), device_id_type=MESH)
        return carry

    lax.fori_loop(1, devices, greet, 0)
    out_ref[me] = x_ref[...]
    pl.semaphore_wait(barrier, devices - 1)

    def go(step, carry):
        pltpu.make_async_remote_copy(
            x_ref, out_ref.at[me], send, recv, device_id=peer(step), device_id_type=MESH
        ).start()
        return carry

    lax.fori_loop(1, devices, go, 0)
    others = out_ref.at[pl.ds(0, devices - 1)]
    pltpu.make_async_remote_copy(
        others, others, send, recv, device_id=peer(1), device_id_type=MESH
    ).wait()


def gather_all(value, collective):
    rows, cols = lax.axis_size("rows"), lax.axis_size("cols")
    flat = value.reshape(-1, LANES)
    gathered = pl.pallas_call(
        functools.partial(gather_kernel, rows, cols),
        out_shape=jax.ShapeDtypeStruct((rows * cols,) + flat.shape, flat.dtype),
        in_specs=[pl.BlockSpec(memory_space=pltpu.VMEM)],
        out_specs=pl.BlockSpec(memory_space=pltpu.VMEM),
        scratch_shapes=[pltpu.SemaphoreType.DMA, pltpu.SemaphoreType.DMA],
        compiler_params=pltpu.CompilerParams(collective_id=collective, has_side_effects=True),
        name="gather_all",
    )(flat)
    return gathered.reshape((rows * cols,) + value.shape)


def extended(block, sides, width):
    for axis, dim in sides:
        count = lax.axis_size(axis)
        forward = [(i, i + 1) for i in range(count - 1)]
        backward = [(target, source) for source, target in forward]
        low = lax.ppermute(
            lax.slice_in_dim(block, block.shape[dim] - width, None, axis=dim), axis, forward
        )
        high = lax.ppermute(lax.slice_in_dim(block, 0, width, axis=dim), axis, backward)
        block = jnp.concatenate([low, block, high], axis=dim)
    return block


def from_behind(value, axis, steps):
    count = lax.axis_size(axis)
    initial, last = (max(0, -steps), min(count, count - steps))
    return lax.ppermute(value, axis, [(source, source + steps) for source in range(initial, last)])


def sigmoid_linear(value):
    return value * jax.nn.sigmoid(value)


def gate_slope(value):
    sigma = jax.nn.sigmoid(value)
    return sigma * (1.0 + value * (1.0 - sigma))


def matmul(left, right):
    return jnp.dot(left, right, preferred_element_type=jnp.float32)


def fetch(block, rate):
    step = rate // block.shape[0]
    widened = extended(block, (("cols", 1),), rate)
    moved = {}
    for sign in (1, -1):
        moved[sign] = from_behind(widened, "rows", sign * step)
    return (moved[1], widened, moved[-1])


def offset_piece(near, index, rate, width):
    start = rate + (index % 3 - 1) * rate
    rows_part = near[index // 3]
    return rows_part[:, start : start + width, :].reshape(-1, rows_part.shape[2])


def local_stats(value):
    mean = jnp.mean(value, axis=1)
    centered = value - mean[:, None, :]
    return mean, jnp.sum(centered * centered, axis=1)


def merged_stats(means, squares, share, count):
    center = jnp.mean(means, axis=0)
    apart = means - center
    spread = (jnp.sum(squares, axis=0) + share * jnp.sum(apart * apart, axis=0)) / count
    return center, lax.rsqrt(spread + EPS)


def pack(*values):
    flat = jnp.concatenate([value.reshape(-1) for value in values])
    unit = 8 * LANES
    short = -flat.shape[0] % unit
    return jnp.pad(flat, (0, short)) if short else flat


def unpack(flat, *shapes):
    out, at = [], 0
    for shape in shapes:
        size = 1
        for extent in shape:
            size *= extent
        out.append(flat[..., at : at + size].reshape(flat.shape[:-1] + tuple(shape)))
        at += size
    return out


def shared_sums(collective, *values):
    flat = jnp.sum(gather_all(pack(*values), collective), axis=0)
    return unpack(flat, *[value.shape for value in values])


def normalize(value, center, scale):
    return (value - center[:, None, :]) * scale[:, None, :]


def norm_backward(upstream, normed, scale, gain, count, collective, *extra):
    shift_grad, gain_grad, *extra = shared_sums(
        collective, jnp.sum(upstream, axis=1), jnp.sum(upstream * normed, axis=1), *extra
    )
    inner = upstream - shift_grad[:, None, :] / count - normed * (gain_grad / count)[:, None, :]
    return (inner * (gain * scale)[:, None, :], gain_grad, shift_grad, *extra)


def on_device(
    features,
    reduce_weight,
    dilated_weight,
    expand_weight,
    mid_gain,
    mid_shift,
    out_gain,
    out_shift,
    aspp_point,
    sep_depth,
    sep_point,
    pool_weight,
    proj_weight,
    aspp_gain,
    aspp_shift,
    head_weight,
    head_bias,
    task_scales,
    crop_ids,
    labels,
    boundary_mask,
    valid_mask,
    geometry_target,
):
    height, width, channels = features.shape
    pixels = height * width
    share = float(pixels)
    count = float(pixels * lax.axis_size("rows") * lax.axis_size("cols"))
    highest = lax.Precision.HIGHEST
    low = jnp.bfloat16
    aspp_width = proj_weight.shape[1]
    crop_flat = crop_ids.reshape(pixels)
    members = (crop_flat[:, None] == jnp.arange(CROPS)[None, :]).astype(low)
    members_wide = members.astype(jnp.float32)
    keep = (1 - boundary_mask.reshape(pixels)).astype(jnp.float32)
    valid = valid_mask.reshape(pixels).astype(jnp.float32)
    flat = features.reshape(pixels, channels)
    reduced = matmul(flat, reduce_weight)[None]
    mean, square = local_stats(reduced)
    own_counts = (jnp.sum(members_wide, axis=0), jnp.sum(keep)[None], jnp.sum(valid)[None])
    gathered = gather_all(pack(mean, square, *own_counts), 0)
    means, squares, crop_counts, keeps, valids = unpack(
        gathered, mean.shape, square.shape, (CROPS,), (1,), (1,)
    )
    center, scale_one = merged_stats(means, squares, share, count)
    crop_count, keep_count, valid_count = (
        jnp.sum(crop_counts, axis=0), jnp.sum(keeps), jnp.sum(valids)
    )
    normed_one = normalize(reduced, center, scale_one)
    gated_one = normed_one[0] * mid_gain[0] + mid_shift[0]
    first_act = sigmoid_linear(gated_one).astype(low)
    first_field = first_act.reshape(height, width, -1)
    first_near = fetch(first_field, MID_RATE)
    dilated = jnp.zeros((pixels, dilated_weight.shape[2]), jnp.float32)
    for index in range(9):
        dilated = dilated + matmul(
            offset_piece(first_near, index, MID_RATE, width), dilated_weight[index]
        )
    dilated = dilated[None]
    mean, square = local_stats(dilated)
    means, squares = unpack(gather_all(pack(mean, square), 1), mean.shape, square.shape)
    center, scale_two = merged_stats(means, squares, share, count)
    normed_two = normalize(dilated, center, scale_two)
    gated_two = normed_two[0] * mid_gain[1] + mid_shift[1]
    second_act = sigmoid_linear(gated_two).astype(low)
    expanded = matmul(second_act, expand_weight)[None]
    mean, square = local_stats(expanded)
    means, squares = unpack(gather_all(pack(mean, square), 2), mean.shape, square.shape)
    center, scale_three = merged_stats(means, squares, share, count)
    normed_three = normalize(expanded, center, scale_three)
    pre_trunk = normed_three[0] * out_gain + out_shift + flat.astype(jnp.float32)
    trunk = sigmoid_linear(pre_trunk).astype(low)
    taps = sep_depth.astype(jnp.float32)[:, :, :, None] * sep_point.astype(jnp.float32)[:, None, :, :]
    taps = jnp.transpose(taps.astype(low), (0, 2, 1, 3)).reshape(3, channels, 9 * aspp_width)
    branch_pre = [matmul(trunk, aspp_point)]
    for index in range(3):
        rate = BASE_RATE * (index + 1)
        step = rate // height
        made = matmul(trunk, taps[index]).astype(low).reshape(height, width, 3, 3, aspp_width)
        side = lax.axis_size("cols")
        up = [(i, i + 1) for i in range(side - 1)]
        down = [(i + 1, i) for i in range(side - 1)]
        before = lax.ppermute(made[:, width - rate :, :, 0, :], "cols", up)
        after = lax.ppermute(made[:, :rate, :, 2, :], "cols", down)
        wide = jnp.float32
        rows_sum = (
            made[:, :, :, 1].astype(wide)
            + jnp.concatenate([before, made[:, : width - rate, :, 0]], axis=1).astype(wide)
            + jnp.concatenate([made[:, rate:, :, 2], after], axis=1).astype(wide)
        )
        above = from_behind(rows_sum[:, :, 0].astype(low), "rows", step).astype(wide)
        below = from_behind(rows_sum[:, :, 2].astype(low), "rows", -step).astype(wide)
        branch_pre.append((rows_sum[:, :, 1] + above + below).reshape(pixels, aspp_width))
    stacked = jnp.stack(branch_pre)
    local_sums = jnp.einsum("pk,pc->kc", members, trunk, preferred_element_type=jnp.float32)
    mean, square = local_stats(stacked)
    crop_part = jnp.dot(local_sums, pool_weight.astype(jnp.float32), precision=highest)
    means, squares, crop_parts = unpack(
        gather_all(pack(mean, square, crop_part), 3), mean.shape, square.shape, crop_part.shape
    )
    center, scale_branch = merged_stats(means, squares, share, count)
    normed_branch = normalize(stacked, center, scale_branch)
    gated_branch = normed_branch * aspp_gain[:4, None, :] + aspp_shift[:4, None, :]
    branch_act = sigmoid_linear(gated_branch).astype(low)
    crop_pre = jnp.sum(crop_parts, axis=0) / crop_count[:, None]
    crop_act = sigmoid_linear(crop_pre).astype(low)
    crop_spread = matmul(members, crop_act).astype(low)
    joined = jnp.concatenate(
        [branch_act[0], branch_act[1], branch_act[2], branch_act[3], crop_spread], axis=1
    )
    projected = matmul(joined, proj_weight)[None]
    mean, square = local_stats(projected)
    means, squares = unpack(gather_all(pack(mean, square), 4), mean.shape, square.shape)
    center, scale_proj = merged_stats(means, squares, share, count)
    normed_proj = normalize(projected, center, scale_proj)
    gated_proj = normed_proj[0] * aspp_gain[4] + aspp_shift[4]
    united = sigmoid_linear(gated_proj).astype(low)
    heads = matmul(united, head_weight) + head_bias
    logits = heads[:, :CLASSES]
    top = jnp.max(logits, axis=1, keepdims=True)
    exps = jnp.exp(logits - top)
    totals = jnp.sum(exps, axis=1)
    label_hot = (labels.reshape(pixels)[:, None] == jnp.arange(CLASSES)[None, :]).astype(
        jnp.float32
    )
    picked = jnp.sum(logits * label_hot, axis=1)
    target = geometry_target.reshape(4, pixels)
    depth_error = heads[:, CLASSES] - target[0]
    root = jnp.sqrt(depth_error * depth_error + 1.0)
    normal_error = heads[:, CLASSES + 1 :] - target[1:].T
    local_losses = jnp.stack(
        [
            jnp.sum(keep * (top[:, 0] + jnp.log(totals) - picked)),
            jnp.sum(valid * (root - 1.0)),
            jnp.sum(valid * jnp.sum(normal_error * normal_error, axis=1)),
        ]
    )
    counts = jnp.stack([keep_count, valid_count, valid_count])
    scale_exp = jnp.exp(task_scales)
    factor = scale_exp / counts
    logit_grad = factor[0] * keep[:, None] * (exps / totals[:, None] - label_hot)
    depth_grad = factor[1] * valid * depth_error / root
    normal_grad = factor[2] * valid[:, None] * 2.0 * normal_error
    head_grad = jnp.concatenate([logit_grad, depth_grad[:, None], normal_grad], axis=1)
    head_low = head_grad.astype(low)
    head_weight_part = jnp.einsum("pc,pk->ck", united, head_low, preferred_element_type=jnp.float32)
    united_grad = jnp.einsum("pk,ck->pc", head_low, head_weight, preferred_element_type=jnp.float32)
    proj_grad, proj_gain_grad, proj_shift_grad, loss_sums, grad_head_bias = norm_backward(
        (united_grad * gate_slope(gated_proj))[None], normed_proj, scale_proj, aspp_gain[4:5], count,
        5, local_losses, jnp.sum(head_grad, axis=0),
    )
    losses = loss_sums / counts
    objective = jnp.sum(scale_exp * losses - task_scales)
    grad_scales = scale_exp * losses - 1.0
    proj_low = proj_grad[0].astype(low)
    grad_proj_weight = jnp.einsum("pc,pd->cd", joined, proj_low, preferred_element_type=jnp.float32)
    joined_grad = jnp.einsum("pd,cd->pc", proj_low, proj_weight, preferred_element_type=jnp.float32)
    branch_up = jnp.stack(
        [joined_grad[:, branch * aspp_width : (branch + 1) * aspp_width] for branch in range(4)]
    )
    crop_local = jnp.einsum(
        "pk,pc->kc", members_wide, joined_grad[:, 4 * aspp_width :], precision=highest
    )
    branch_grad, branch_gain_grad, branch_shift_grad, crop_total = norm_backward(
        branch_up * gate_slope(gated_branch), normed_branch, scale_branch, aspp_gain[:4], count,
        6, crop_local,
    )
    branch_low = branch_grad.astype(low)
    crop_low = (crop_total * gate_slope(crop_pre)).astype(low)
    pooled = (lax.psum(local_sums, ("rows", "cols")) / crop_count[:, None]).astype(low)
    grad_pool_weight = jnp.einsum("kc,kd->cd", pooled, crop_low, preferred_element_type=jnp.float32)
    pooled_grad = (
        jnp.einsum("kd,cd->kc", crop_low, pool_weight, preferred_element_type=jnp.float32)
        / crop_count[:, None]
    )
    trunk_grad = jnp.einsum(
        "pd,cd->pc", branch_low[0], aspp_point, preferred_element_type=jnp.float32
    )
    trunk_grad = trunk_grad + jnp.dot(members_wide, pooled_grad, precision=highest)
    grad_aspp_point = jnp.einsum(
        "pc,pd->cd", trunk, branch_low[0], preferred_element_type=jnp.float32
    )
    point_grads = []
    depth_grads = []
    for index in range(3):
        rate = BASE_RATE * (index + 1)
        near = fetch(branch_low[index + 1].reshape(height, width, aspp_width), rate)
        moved = jnp.concatenate(
            [offset_piece(near, 8 - tap, rate, width) for tap in range(9)], axis=1
        )
        trunk_grad = trunk_grad + jnp.einsum(
            "pd,cd->pc", moved, taps[index], preferred_element_type=jnp.float32
        )
        whole = jnp.einsum("pc,pd->cd", trunk, moved, preferred_element_type=jnp.float32)
        whole = whole.reshape(channels, 9, aspp_width)
        point_grads.append(jnp.sum(whole * sep_depth[index].T.astype(jnp.float32)[:, :, None], axis=1))
        depth_grads.append(
            jnp.sum(whole * sep_point[index].astype(jnp.float32)[:, None, :], axis=2).T
        )
    pre_grad = trunk_grad * gate_slope(pre_trunk)
    expand_grad, out_gain_grad, out_shift_grad = norm_backward(
        pre_grad[None], normed_three, scale_three, out_gain[None], count, 7
    )
    expand_low = expand_grad[0].astype(low)
    grad_expand_weight = jnp.einsum(
        "pc,pd->cd", second_act, expand_low, preferred_element_type=jnp.float32
    )
    second_grad = jnp.einsum(
        "pd,cd->pc", expand_low, expand_weight, preferred_element_type=jnp.float32
    )
    dilated_grad, two_gain_grad, two_shift_grad = norm_backward(
        (second_grad * gate_slope(gated_two))[None], normed_two, scale_two, mid_gain[1:2], count, 8
    )
    dilated_low = dilated_grad[0].astype(low)
    dilated_near = fetch(dilated_low.reshape(height, width, -1), MID_RATE)
    first_grad = jnp.zeros((pixels, dilated_weight.shape[1]), jnp.float32)
    dilated_grads = []
    for tap in range(9):
        dilated_grads.append(
            jnp.einsum(
                "pc,pd->cd",
                offset_piece(first_near, tap, MID_RATE, width),
                dilated_low,
                preferred_element_type=jnp.float32,
            )
        )
        first_grad = first_grad + jnp.einsum(
            "pd,cd->pc",
            offset_piece(dilated_near, 8 - tap, MID_RATE, width),
            dilated_weight[tap],
            preferred_element_type=jnp.float32,
        )
    reduced_grad, one_gain_grad, one_shift_grad = norm_backward(
        (first_grad * gate_slope(gated_one))[None], normed_one, scale_one, mid_gain[0:1], count, 9
    )
    reduced_low = reduced_grad[0].astype(low)
    grad_reduce_weight = jnp.einsum(
        "pc,pd->cd", flat, reduced_low, preferred_element_type=jnp.float32
    )
    input_grad = (
        jnp.einsum("pd,cd->pc", reduced_low, reduce_weight, preferred_element_type=jnp.float32)
        + pre_grad
    )
    grad_features = input_grad.astype(low).reshape(height, width, channels)
    parts = (
        grad_reduce_weight,
        jnp.stack(dilated_grads),
        grad_expand_weight,
        grad_aspp_point,
        jnp.stack(depth_grads),
        jnp.stack(point_grads),
        grad_proj_weight,
        jnp.pad(head_weight_part, ((0, 0), (0, LANES - head_weight_part.shape[1]))),
    )
    summed = lax.psum(tuple(part.astype(low) for part in parts), ("rows", "cols"))
    summed = [part.astype(jnp.float32) for part in summed]
    grad_mid_gain = jnp.concatenate([one_gain_grad, two_gain_grad], axis=0)
    grad_mid_shift = jnp.concatenate([one_shift_grad, two_shift_grad], axis=0)
    grad_aspp_gain = jnp.concatenate([branch_gain_grad, proj_gain_grad], axis=0)
    grad_aspp_shift = jnp.concatenate([branch_shift_grad, proj_shift_grad], axis=0)
    return (
        objective,
        grad_features,
        summed[0],
        summed[1],
        summed[2],
        grad_mid_gain,
        grad_mid_shift,
        out_gain_grad[0],
        out_shift_grad[0],
        summed[3],
        summed[4],
        summed[5],
        grad_pool_weight,
        summed[6],
        grad_aspp_gain,
        grad_aspp_shift,
        summed[7][:, : head_weight.shape[1]],
        grad_head_bias,
        grad_scales,
    )


def solution(mesh):
    in_specs = (
        P("rows", "cols", None),
        P(),
        P(),
        P(),
        P(),
        P(),
        P(),
        P(),
        P(),
        P(),
        P(),
        P(),
        P(),
        P(),
        P(),
        P(),
        P(),
        P(),
        P("rows", "cols"),
        P("rows", "cols"),
        P("rows", "cols"),
        P("rows", "cols"),
        P(None, "rows", "cols"),
    )
    out_specs = (
        P(),
        P("rows", "cols", None),
        P(),
        P(),
        P(),
        P(),
        P(),
        P(),
        P(),
        P(),
        P(),
        P(),
        P(),
        P(),
        P(),
        P(),
        P(),
        P(),
        P(),
    )
    return jax.shard_map(
        on_device, mesh=mesh, in_specs=in_specs, out_specs=out_specs, check_vma=False
    )
```

time: 2950 us -> 1230 us (0.42)
  blocking collectives: 918 us -> 0 us
  waiting for transfers between devices: 1240 us -> 356 us
  Pallas kernels: 0 us -> 167 us
  other arithmetic: 247 us -> 136 us
  local copies, waits for them, and re-layouts: 105 us -> 209 us
  starting transfers between devices: 161 us -> 91.4 us
    psum x16 -> x0, blocking collectives: 918 us -> none  [the longest x5 336 us: norm_forward(): totals = lax.psum(jnp.sum(value, axis=1), ('rows', 'cols'))]
    ppermute x16, waiting for transfers between devices: 818 us -> 121 us  [from_behind(): lax.ppermute(value, axis, [(source, source + steps) for source in range(i...]
    psum x2, waiting for transfers between devices: 419 us -> 235 us  [the longest x1 235 us: on_device(): lax.psum(tuple((part.astype(low) for part in parts)), ('rows', 'cols'))]
    pallas_call x0 -> x10, Pallas kernels: none -> 167 us  [gather_all(): pl.pallas_call(functools.partial(gather_kernel, rows, cols), out_shape=ja...]
    convert_element_type x23 -> x17, other arithmetic: 162 us -> 60.6 us  [the longest x4 15.2 us: on_device(): summed = [part.astype(jnp.float32) for part in summed]]
    ppermute x16, starting transfers between devices: 118 us -> 55.4 us  [from_behind(): lax.ppermute(value, axis, [(source, source + steps) for source in range(i...]
    dot_general x1, matrix products: 52.3 us -> 4.55 us  [on_device(): jnp.einsum('pd,cd->pc', branch_low[0], aspp_point, preferred_element_type...]
    slice x10, local copies, waits for them, and re-layouts: 47.7 us -> 5.48 us  [offset_piece(): return rows_part[:, start:start + width, :].reshape(-1, rows_part.shape[2])]
  transfers between devices with their start and end apart: 34 -> 34, of which waited for: 15 -> 10; matrix products, arithmetic and copies ran while one was open for 10% -> 36% of each run, Pallas kernels for 0% -> 10%
where the time goes in v1:
time: 1230 us; the launch traced here: 1220 us
  waiting for transfers between devices  356 us (29%)
  matrix products  244 us (20%)
  local copies, waits for them, and re-layouts  209 us (17%)
  Pallas kernels  167 us (14%)
  other arithmetic  136 us (11%)
  starting transfers between devices  91.4 us (7%)
  between operations  17 us (1%)
    psum x1, waiting for transfers between devices, on_device(): lax.psum(tuple((part.astype(low) for part in parts)), ('rows', 'cols'))  235 us
    pallas_call x10, Pallas kernels, gather_all(): pl.pallas_call(functools.partial(gather_kernel, rows, cols), out_shape=ja...  167 us
    ppermute x16, waiting for transfers between devices, from_behind(): lax.ppermute(value, axis, [(source, source + steps) for source in range(i...  121 us
    dot_general x18, matrix products, matmul(): return jnp.dot(left, right, preferred_element_type=jnp.float32)  73.5 us
    ppermute x16, starting transfers between devices, from_behind(): lax.ppermute(value, axis, [(source, source + steps) for source in range(i...  55.4 us
    dot_general x3, matrix products, on_device(): jnp.einsum('pd,cd->pc', moved, taps[index], preferred_element_type=jnp.fl...  52.6 us
    unnamed x351, local copies, waits for them, and re-layouts  45.3 us
    dot_general x3, matrix products, on_device(): jnp.einsum('pc,pd->cd', trunk, moved, preferred_element_type=jnp.float32)  44 us
  transfers between devices with their start and end apart: 34, of which 10 were waited for; matrix products, arithmetic and copies ran while one was open for 36% of the time, Pallas kernels for 10%

profile of v1, /device:TPU:11, one launch (start us, length us, event | category | flops | bytes accessed | tf_op | source)
XLA Modules:
  0.0 1219.9 jit_solution(17037711904869154110)
XLA Ops:
  16.5 12.8 %gather_all.10 = f32[32,16,128]{2,1,0:T(8,128)} custom-call(f32[16,128]{1,0:T(8,128)} %pad_bitcast_fusion.x_ref), custom_call_target="tpu_custom_call" | custom-call | tf_op jit(solution)/shard_map/gather_all/pallas_call | solution.py:53
  54.6 9.1 multiply_convert_fusion
  63.7 10.0 fusion.140
  115.8 20.5 %collective-permute-done.2 = bf16[4,264,512]{2,1,0:T(8,128)(2,1)S(1)} collective-permute-done((bf16[4,264,512]{2,1,0:T(8,128)(2,1)}, bf16[4,264,512]{2,1,0:T(8,128)(2,1)S(1)}, u32[]{:S(2)}, u32[]{:S(2)}) %collective-permute-start.2) | collective-permute-done | bytes 1081376 | tf_op jit(solution)/shard_map/ppermute | solution.py:81
  142.8 10.8 gather_all.11
  163.4 17.6 %gather_all.12 = f32[32,32,128]{2,1,0:T(8,128)} custom-call(f32[32,128]{1,0:T(8,128)} %pad_maximum_fusion.19.x_ref), custom_call_target="tpu_custom_call" | custom-call | tf_op jit(solution)/shard_map/gather_all/pallas_call | solution.py:53
  191.4 13.4 %convolution_convert_fusion.2 = bf16[1024,2304]{1,0:T(8,128)(2,1)} fusion(bf16[1024,2048]{1,0:T(8,128)(2,1)S(1)} %multiply_convert_fusion.2, bf16[2048,2304]{0,1:T(8,128)(2,1)} %bitcast.603), kind=kOutput, calls=%fused_computation.18 | convolution fusion | flops 9666035712 | bytes 18350080 | tf_op jit(solution)/shard_map/dot_general | solution.py:94
  211.5 8.9 reshape.1117
  228.8 13.5 %convolution_convert_fusion.1 = bf16[1024,2304]{1,0:T(8,128)(2,1)} fusion(bf16[1024,2048]{1,0:T(8,128)(2,1)S(1)} %copy-done.17, bf16[2048,2304]{0,1:T(8,128)(2,1)} %bitcast.599), kind=kOutput, calls=%fused_computation.17 | convolution fusion | flops 9666035712 | bytes 18350080 | tf_op jit(solution)/shard_map/dot_general | solution.py:94
  249.0 8.9 reshape.1118
  279.2 16.1 %convolution_convert_fusion = bf16[1024,2304]{1,0:T(8,128)(2,1)} fusion(bf16[1024,2048]{1,0:T(8,128)(2,1)} %copy-done.16, bf16[2048,2304]{0,1:T(8,128)(2,1)} %bitcast.597), kind=kOutput, calls=%fused_computation.16 | convolution fusion | flops 9666035712 | bytes 18350080 | tf_op jit(solution)/shard_map/dot_general | solution.py:94
  302.0 8.9 reshape.1119
  380.9 8.6 collective-permute-start.14
  400.4 11.6 collective-permute-done.14
  421.3 29.6 %gather_all.13 = f32[32,48,128]{2,1,0:T(8,128)} custom-call(f32[48,128]{1,0:T(8,128)} %maximum_bitcast_fusion.x_ref), custom_call_target="tpu_custom_call" | custom-call | tf_op jit(solution)/shard_map/gather_all/pallas_call | solution.py:53
  466.2 9.4 gather_all.14
  487.7 9.6 gather_all.15
  509.6 22.5 %gather_all.16 = f32[32,48,128]{2,1,0:T(8,128)} custom-call(f32[48,128]{1,0:T(8,128)} %maximum_bitcast_fusion.1.x_ref), custom_call_target="tpu_custom_call" | custom-call | tf_op jit(solution)/shard_map/gather_all/pallas_call | solution.py:53
  596.2 7.5 collective-permute-done.19
  613.0 22.7 %collective-permute-done.26 = bf16[4,328,256]{2,1,0:T(8,128)(2,1)S(1)} collective-permute-done((bf16[4,328,256]{2,1,0:T(8,128)(2,1)}, bf16[4,328,256]{2,1,0:T(8,128)(2,1)S(1)}, u32[]{:S(2)}, u32[]{:S(2)}) %collective-permute-start.26) | collective-permute-done | bytes 671776 | tf_op jit(solution)/shard_map/ppermute | solution.py:81
  640.3 12.5 %fusion.169 = f32[1024,2048]{1,0:T(8,128)} fusion(bf16[1024,2304]{1,0:T(8,128)(2,1)S(1)} %constant_dynamic-update-slice_fusion, bf16[2048,2304]{0,1:T(8,128)(2,1)S(1)} %bitcast.606), kind=kOutput, calls=%fused_computation.435 | convolution fusion | flops 9663676416 | bytes 22544384 | tf_op jit(solution)/shard_map/pd,cd->pc/dot_general | solution.py:351
  656.2 12.1 fusion.170
  671.9 27.9 %fusion.129 = (f32[2048]{0:T(1024)S(1)}, f32[2048]{0:T(1024)S(1)}, f32[1024,2048]{1,0:T(8,128)}) fusion(f32[2048]{0:T(1024)S(1)} %copy-done.78, f32[1024,2048]{1,0:T(8,128)} %copy-done.1, f32[2048]{0:T(1024)S(1)} %copy-done.72, bf16[4,256,2048]{2,1,0:T(8,128)(2,1)} %param.23, f32[2048]{0:T(1024)S(1)} %copy-done.119, f32[2048]{0:T(1024)S(1)} %copy-done.94, ...), kind=kOutput, calls=%fused_computation.398 | convolution fusion | flops 9707712512 | bytes 68730880 | tf_op jit(solution)/shard_map/pd,cd->pc/dot_general | solution.py:351
  700.4 37.1 %gather_all.17 = f32[32,32,128]{2,1,0:T(8,128)} custom-call(f32[32,128]{1,0:T(8,128)} %pad_maximum_fusion.20.x_ref), custom_call_target="tpu_custom_call" | custom-call | tf_op jit(solution)/shard_map/gather_all/pallas_call | solution.py:53
  755.9 8.9 gather_all.18
  809.2 16.4 %multiply_reduce_fusion = (bf16[2048,256]{0,1:T(8,128)(2,1)S(1)}, bf16[2048,9]{0,1:T(8,128)(2,1)S(1)}) fusion(f32[2048,9]{0,1:T(8,128)S(1)} %copy-done.74, f32[2048,256]{0,1:T(8,128)} %copy.166, bf16[9,256,1024]{2,1,0:T(8,128)(2,1)} %bitcast.622, bf16[1024,2048]{1,0:T(8,128)(2,1)} %copy-done.16), kind=kOutput, calls=%fused_computation.1 | convolution fusion | flops 9682008064 | bytes 12169216 | tf_op jit(solution)/shard_map/pc,pd->cd/dot_general | solution.py:354
  825.6 14.0 %multiply_reduce_fusion.2 = (bf16[2048,256]{0,1:T(8,128)(2,1)S(1)}, bf16[2048,9]{0,1:T(8,128)(2,1)S(1)}) fusion(f32[2048,9]{0,1:T(8,128)S(1)} %copy-done.75, f32[2048,256]{0,1:T(8,128)S(1)} %copy-done.56, bf16[9,256,1024]{2,1,0:T(8,128)(2,1)S(1)} %bitcast.621, bf16[1024,2048]{1,0:T(8,128)(2,1)S(1)} %copy-done.20), kind=kOutput, calls=%fused_computation.3 | convolution fusion | flops 9682008064 | bytes 12169216 | tf_op jit(solution)/shard_map/pc,pd->cd/dot_general | solution.py:354
  839.7 13.6 %multiply_reduce_fusion.1 = (bf16[2048,256]{0,1:T(8,128)(2,1)S(1)}, bf16[2048,9]{0,1:T(8,128)(2,1)S(1)}) fusion(f32[2048,9]{0,1:T(8,128)S(1)} %copy-done.73, f32[2048,256]{0,1:T(8,128)S(1)} %copy-done.55, bf16[9,256,1024]{2,1,0:T(8,128)(2,1)S(1)} %bitcast.620, bf16[1024,2048]{1,0:T(8,128)(2,1)S(1)} %copy-done.20), kind=kOutput, calls=%fused_computation.2 | convolution fusion | flops 9682008064 | bytes 12169216 | tf_op jit(solution)/shard_map/pc,pd->cd/dot_general | solution.py:354
  865.6 41.8 %collective-permute-done.31 = bf16[4,264,512]{2,1,0:T(8,128)(2,1)S(1)} collective-permute-done((bf16[4,264,512]{2,1,0:T(8,128)(2,1)S(1)}, bf16[4,264,512]{2,1,0:T(8,128)(2,1)S(1)}, u32[]{:S(2)}, u32[]{:S(2)}) %collective-permute-start.31) | collective-permute-done | bytes 1081376 | tf_op jit(solution)/shard_map/ppermute | solution.py:81
  916.3 9.2 gather_all.19
  942.7 8.6 add_convert_fusion
  951.3 234.5 %all-reduce.10.cloned.1.call-done = (bf16[2048,512]{0,1:T(8,128)(2,1)}, bf16[3,9,2048]{2,1,0:T(8,128)(2,1)}, bf16[3,2048,256]{1,2,0:T(8,128)(2,1)}, bf16[9,512,5...) async-done(((bf16[2048,512]{0,1:T(8,128)(2,1)}, ...) | async-done | bytes 13938704 | tf_op jit(solution)/shard_map/psum | solution.py:415
  (659 shorter events, 494.2 us)
Async XLA Ops:
  35.0 46.9 %collective-permute-start = (bf16[4,4,512]{2,1,0:T(4,128)(2,1)}, bf16[4,4,512]{2,1,0:T(4,128)(2,1)S(1)}, u32[]{:S(2)}, u32[]{:S(2)}) collective-permute-start(bf16[4,4,512]{2,1,0:T(4,128)(2,1)} %get-tuple-element.203), channel_id=1, source_target_pairs={{0,1},{2,3},{4,5},{6,7},{8,9},{10,11},{12,13},{14,15},{16,17},{18,... | collective-permute-start | bytes 49160 | tf_op jit(solution)/shard_map/ppermute | solution.py:70
  36.3 45.6 %collective-permute-start.1 = (bf16[4,4,512]{2,1,0:T(4,128)(2,1)}, bf16[4,4,512]{2,1,0:T(4,128)(2,1)S(1)}, u32[]{:S(2)}, u32[]{:S(2)}) collective-permute-start(bf16[4,4,512]{2,1,0:T(4,128)(2,1)} %get-tuple-element.204), channel_id=1, source_target_pairs={{1,0},{3,2},{5,4},{7,6},{9,8},{11,10},{13,12},{15,14},{17,16},{19,... | collective-permute-start | bytes 49160 | tf_op jit(solution)/shard_map/ppermute | solution.py:73
  83.1 28.7 %collective-permute-start.3 = (bf16[4,264,512]{2,1,0:T(8,128)(2,1)}, bf16[4,264,512]{2,1,0:T(8,128)(2,1)}, u32[]{:S(2)}, u32[]{:S(2)}) collective-permute-start(bf16[4,264,512]{2,1,0:T(8,128)(2,1)} %pad_maximum_fusion.2), channel_id=1, source_target_pairs={{2,0},{4,2},{6,4},{8,6},{10,8},{12,10},{14,12},{16,14},{18,16},{20... | collective-permute-start | bytes 3244040 | tf_op jit(solution)/shard_map/ppermute | solution.py:81
  95.7 40.6 %collective-permute-start.2 = (bf16[4,264,512]{2,1,0:T(8,128)(2,1)}, bf16[4,264,512]{2,1,0:T(8,128)(2,1)S(1)}, u32[]{:S(2)}, u32[]{:S(2)}) collective-permute-start(bf16[4,264,512]{2,1,0:T(8,128)(2,1)} %pad_maximum_fusion.2), channel_id=1, source_target_pairs={{0,2},{2,4},{4,6},{6,8},{8,10},{10,12},{12,14},{14,16},{16,18},{18... | collective-permute-start | bytes 3244040 | tf_op jit(solution)/shard_map/ppermute | solution.py:81
  267.5 671.2 %all-reduce.8.cloned.1.call-start = ((), (), s32[]{:S(2)}) async-start(), calls=%async_computation | async-start | bytes 262144 | tf_op jit(solution)/shard_map/psum | solution.py:330
  268.3 917.6 %all-reduce.10.cloned.1.call-start = ((), (), s32[]{:S(2)}) async-start(), calls=%async_computation.1 | async-start | bytes 28049408 | tf_op jit(solution)/shard_map/psum | solution.py:415
  269.9 63.0 %collective-permute-start.4 = (bf16[4,12,3,256]{3,0,2,1:T(4,128)(2,1)S(1)}, bf16[4,12,3,256]{3,0,2,1:T(4,128)(2,1)S(1)}, u32[]{:S(2)}, u32[]{:S(2)}) collective-permute-start(bf16[4,12,3,256]{3,0,2,1:T(4,128)(2,1)S(1)} %copy.138), channel_id=1, source_target_pairs={{0,1},{2,3},{4,5},{6,7},{8,9},{10,11},{12,13},{14,15},{16,17},{18,... | collective-permute-start | bytes 221192 | tf_op jit(solution)/shard_map/ppermute | solution.py:243
  272.9 62.6 %collective-permute-start.5 = (bf16[4,12,3,256]{3,0,2,1:T(4,128)(2,1)S(1)}, bf16[4,12,3,256]{3,0,2,1:T(4,128)(2,1)S(1)}, u32[]{:S(2)}, u32[]{:S(2)}) collective-permute-start(bf16[4,12,3,256]{3,0,2,1:T(4,128)(2,1)S(1)} %copy.141), channel_id=1, source_target_pairs={{1,0},{3,2},{5,4},{7,6},{9,8},{11,10},{13,12},{15,14},{17,16},{19,... | collective-permute-start | bytes 221192 | tf_op jit(solution)/shard_map/ppermute | solution.py:244
  277.9 69.4 %collective-permute-start.8 = (bf16[4,24,3,256]{3,1,2,0:T(8,128)(2,1)}, bf16[4,24,3,256]{3,1,2,0:T(8,128)(2,1)}, u32[]{:S(2)}, u32[]{:S(2)}) collective-permute-start(bf16[4,24,3,256]{3,1,2,0:T(8,128)(2,1)} %copy.146), channel_id=1, source_target_pairs={{0,1},{2,3},{4,5},{6,7},{8,9},{10,11},{12,13},{14,15},{16,17},{18,... | collective-permute-start | bytes 442376 | tf_op jit(solution)/shard_map/ppermute | solution.py:243
  315.1 52.9 %collective-permute-start.12 = (bf16[4,36,3,256]{3,0,2,1:T(4,128)(2,1)}, bf16[4,36,3,256]{3,0,2,1:T(4,128)(2,1)}, u32[]{:S(2)}, u32[]{:S(2)}) collective-permute-start(bf16[4,36,3,256]{3,0,2,1:T(4,128)(2,1)} %copy.154), channel_id=1, source_target_pairs={{0,1},{2,3},{4,5},{6,7},{8,9},{10,11},{12,13},{14,15},{16,17},{18,... | collective-permute-start | bytes 663560 | tf_op jit(solution)/shard_map/ppermute | solution.py:243
  325.7 28.1 %collective-permute-start.9 = (bf16[4,24,3,256]{3,1,2,0:T(8,128)(2,1)}, bf16[4,24,3,256]{3,1,2,0:T(8,128)(2,1)}, u32[]{:S(2)}, u32[]{:S(2)}) collective-permute-start(bf16[4,24,3,256]{3,1,2,0:T(8,128)(2,1)} %copy.149), channel_id=1, source_target_pairs={{1,0},{3,2},{5,4},{7,6},{9,8},{11,10},{13,12},{15,14},{17,16},{19,... | collective-permute-start | bytes 442376 | tf_op jit(solution)/shard_map/ppermute | solution.py:244
  332.9 37.8 %collective-permute-start.13 = (bf16[4,36,3,256]{3,0,2,1:T(4,128)(2,1)}, bf16[4,36,3,256]{3,0,2,1:T(4,128)(2,1)}, u32[]{:S(2)}, u32[]{:S(2)}) collective-permute-start(bf16[4,36,3,256]{3,0,2,1:T(4,128)(2,1)} %copy.157), channel_id=1, source_target_pairs={{1,0},{3,2},{5,4},{7,6},{9,8},{11,10},{13,12},{15,14},{17,16},{19,... | collective-permute-start | bytes 663560 | tf_op jit(solution)/shard_map/ppermute | solution.py:244
  344.8 44.7 %collective-permute-start.6 = (bf16[4,256,256]{1,0,2:T(4,128)(2,1)}, bf16[4,256,256]{1,0,2:T(4,128)(2,1)S(1)}, u32[]{:S(2)}, u32[]{:S(2)}) collective-permute-start(bf16[4,256,256]{1,0,2:T(4,128)(2,1)} %get-tuple-element.179), channel_id=1, source_target_pairs={{0,6},{2,8},{4,10},{6,12},{8,14},{10,16},{12,18},{14,20},{16,22},{... | collective-permute-start | bytes 1572872 | tf_op jit(solution)/shard_map/ppermute | solution.py:81
  347.4 43.4 %collective-permute-start.7 = (bf16[4,256,256]{1,0,2:T(4,128)(2,1)}, bf16[4,256,256]{1,0,2:T(4,128)(2,1)}, u32[]{:S(2)}, u32[]{:S(2)}) collective-permute-start(bf16[4,256,256]{1,0,2:T(4,128)(2,1)} %get-tuple-element.180), channel_id=1, source_target_pairs={{6,0},{8,2},{10,4},{12,6},{14,8},{16,10},{18,12},{20,14},{22,16},{... | collective-permute-start | bytes 1572872 | tf_op jit(solution)/shard_map/ppermute | solution.py:81
  363.9 31.1 %collective-permute-start.10 = (bf16[4,256,256]{1,0,2:T(4,128)(2,1)}, bf16[4,256,256]{1,0,2:T(4,128)(2,1)}, u32[]{:S(2)}, u32[]{:S(2)}) collective-permute-start(bf16[4,256,256]{1,0,2:T(4,128)(2,1)} %get-tuple-element.181), channel_id=1, source_target_pairs={{0,12},{2,14},{4,16},{6,18},{8,20},{10,22},{12,24},{14,26},{16,28}... | collective-permute-start | bytes 1572872 | tf_op jit(solution)/shard_map/ppermute | solution.py:81
  367.9 27.1 %collective-permute-start.11 = (bf16[4,256,256]{1,0,2:T(4,128)(2,1)}, bf16[4,256,256]{1,0,2:T(4,128)(2,1)}, u32[]{:S(2)}, u32[]{:S(2)}) collective-permute-start(bf16[4,256,256]{1,0,2:T(4,128)(2,1)} %get-tuple-element.182), channel_id=1, source_target_pairs={{12,0},{14,2},{16,4},{18,6},{20,8},{22,10},{24,12},{26,14},{28,16}... | collective-permute-start | bytes 1572872 | tf_op jit(solution)/shard_map/ppermute | solution.py:81
  380.9 31.1 %collective-permute-start.14 = (bf16[4,256,256]{1,0,2:T(4,128)(2,1)}, bf16[4,256,256]{1,0,2:T(4,128)(2,1)}, u32[]{:S(2)}, u32[]{:S(2)}) collective-permute-start(bf16[4,256,256]{1,0,2:T(4,128)(2,1)} %get-tuple-element.183), channel_id=1, source_target_pairs={{0,18},{2,20},{4,22},{6,24},{8,26},{10,28},{12,30},{1,19},{3,21},{... | collective-permute-start | bytes 1572872 | tf_op jit(solution)/shard_map/ppermute | solution.py:81
  389.4 22.6 %collective-permute-start.15 = (bf16[4,256,256]{1,0,2:T(4,128)(2,1)}, bf16[4,256,256]{1,0,2:T(4,128)(2,1)}, u32[]{:S(2)}, u32[]{:S(2)}) collective-permute-start(bf16[4,256,256]{1,0,2:T(4,128)(2,1)} %get-tuple-element.184), channel_id=1, source_target_pairs={{18,0},{20,2},{22,4},{24,6},{26,8},{28,10},{30,12},{19,1},{21,3},{... | collective-permute-start | bytes 1572872 | tf_op jit(solution)/shard_map/ppermute | solution.py:81
  548.7 30.5 %collective-permute-start.24 = (bf16[4,36,256]{2,1,0:T(8,128)(2,1)}, bf16[4,36,256]{2,1,0:T(8,128)(2,1)S(1)}, u32[]{:S(2)}, u32[]{:S(2)}) collective-permute-start(bf16[4,36,256]{2,1,0:T(8,128)(2,1)} %get-tuple-element.233), channel_id=1, source_target_pairs={{0,1},{2,3},{4,5},{6,7},{8,9},{10,11},{12,13},{14,15},{16,17},{18,... | collective-permute-start | bytes 221192 | tf_op jit(solution)/shard_map/ppermute | solution.py:70
  550.0 34.1 %collective-permute-start.25 = (bf16[4,36,256]{2,1,0:T(8,128)(2,1)S(1)}, bf16[4,36,256]{2,1,0:T(8,128)(2,1)S(1)}, u32[]{:S(2)}, u32[]{:S(2)}) collective-permute-start(bf16[4,36,256]{2,1,0:T(8,128)(2,1)S(1)} %get-tuple-element.234), channel_id=1, source_target_pairs={{1,0},{3,2},{5,4},{7,6},{9,8},{11,10},{13,12},{15,14},{17,16},{19,... | collective-permute-start | bytes 221192 | tf_op jit(solution)/shard_map/ppermute | solution.py:73
  553.7 13.7 %collective-permute-start.16 = (bf16[4,12,256]{2,1,0:T(8,128)(2,1)}, bf16[4,12,256]{2,1,0:T(8,128)(2,1)S(1)}, u32[]{:S(2)}, u32[]{:S(2)}) collective-permute-start(bf16[4,12,256]{2,1,0:T(8,128)(2,1)} %get-tuple-element.225), channel_id=1, source_target_pairs={{0,1},{2,3},{4,5},{6,7},{8,9},{10,11},{12,13},{14,15},{16,17},{18,... | collective-permute-start | bytes 73736 | tf_op jit(solution)/shard_map/ppermute | solution.py:70
  555.0 15.5 %collective-permute-start.17 = (bf16[4,12,256]{2,1,0:T(8,128)(2,1)}, bf16[4,12,256]{2,1,0:T(8,128)(2,1)S(1)}, u32[]{:S(2)}, u32[]{:S(2)}) collective-permute-start(bf16[4,12,256]{2,1,0:T(8,128)(2,1)} %get-tuple-element.226), channel_id=1, source_target_pairs={{1,0},{3,2},{5,4},{7,6},{9,8},{11,10},{13,12},{15,14},{17,16},{19,... | collective-permute-start | bytes 73736 | tf_op jit(solution)/shard_map/ppermute | solution.py:73
  570.6 18.8 %collective-permute-start.18 = (bf16[4,280,256]{2,1,0:T(8,128)(2,1)S(1)}, bf16[4,280,256]{2,1,0:T(8,128)(2,1)S(1)}, u32[]{:S(2)}, u32[]{:S(2)}) collective-permute-start(bf16[4,280,256]{2,1,0:T(8,128)(2,1)S(1)} %pad_maximum_fusion.10), channel_id=1, source_target_pairs={{6,0},{8,2},{10,4},{12,6},{14,8},{16,10},{18,12},{20,14},{22,16},{... | collective-permute-start | bytes 1720328 | tf_op jit(solution)/shard_map/ppermute | solution.py:81
  572.7 31.0 %collective-permute-start.19 = (bf16[4,280,256]{2,1,0:T(8,128)(2,1)S(1)}, bf16[4,280,256]{2,1,0:T(8,128)(2,1)S(1)}, u32[]{:S(2)}, u32[]{:S(2)}) collective-permute-start(bf16[4,280,256]{2,1,0:T(8,128)(2,1)S(1)} %pad_maximum_fusion.10), channel_id=1, source_target_pairs={{0,6},{2,8},{4,10},{6,12},{8,14},{10,16},{12,18},{14,20},{16,22},{... | collective-permute-start | bytes 1720328 | tf_op jit(solution)/shard_map/ppermute | solution.py:81
  577.0 29.0 %collective-permute-start.22 = (bf16[4,304,256]{2,1,0:T(8,128)(2,1)S(1)}, bf16[4,304,256]{2,1,0:T(8,128)(2,1)S(1)}, u32[]{:S(2)}, u32[]{:S(2)}) collective-permute-start(bf16[4,304,256]{2,1,0:T(8,128)(2,1)S(1)} %pad_maximum_fusion.9), channel_id=1, source_target_pairs={{12,0},{14,2},{16,4},{18,6},{20,8},{22,10},{24,12},{26,14},{28,16}... | collective-permute-start | bytes 1867784 | tf_op jit(solution)/shard_map/ppermute | solution.py:81
  579.2 32.6 %collective-permute-start.23 = (bf16[4,304,256]{2,1,0:T(8,128)(2,1)S(1)}, bf16[4,304,256]{2,1,0:T(8,128)(2,1)S(1)}, u32[]{:S(2)}, u32[]{:S(2)}) collective-permute-start(bf16[4,304,256]{2,1,0:T(8,128)(2,1)S(1)} %pad_maximum_fusion.9), channel_id=1, source_target_pairs={{0,12},{2,14},{4,16},{6,18},{8,20},{10,22},{12,24},{14,26},{16,28}... | collective-permute-start | bytes 1867784 | tf_op jit(solution)/shard_map/ppermute | solution.py:81
  585.1 50.5 %collective-permute-start.26 = (bf16[4,328,256]{2,1,0:T(8,128)(2,1)}, bf16[4,328,256]{2,1,0:T(8,128)(2,1)S(1)}, u32[]{:S(2)}, u32[]{:S(2)}) collective-permute-start(bf16[4,328,256]{2,1,0:T(8,128)(2,1)} %pad_maximum_fusion.8), channel_id=1, source_target_pairs={{18,0},{20,2},{22,4},{24,6},{26,8},{28,10},{30,12},{19,1},{21,3},{... | collective-permute-start | bytes 2015240 | tf_op jit(solution)/shard_map/ppermute | solution.py:81
  589.4 79.8 %collective-permute-start.27 = (bf16[4,328,256]{2,1,0:T(8,128)(2,1)}, bf16[4,328,256]{2,1,0:T(8,128)(2,1)S(1)}, u32[]{:S(2)}, u32[]{:S(2)}) collective-permute-start(bf16[4,328,256]{2,1,0:T(8,128)(2,1)} %pad_maximum_fusion.8), channel_id=1, source_target_pairs={{0,18},{2,20},{4,22},{6,24},{8,26},{10,28},{12,30},{1,19},{3,21},{... | collective-permute-start | bytes 2015240 | tf_op jit(solution)/shard_map/ppermute | solution.py:81
  773.4 82.6 %collective-permute-start.28 = (bf16[4,4,512]{2,1,0:T(4,128)(2,1)S(1)}, bf16[4,4,512]{2,1,0:T(4,128)(2,1)S(1)}, u32[]{:S(2)}, u32[]{:S(2)}) collective-permute-start(bf16[4,4,512]{2,1,0:T(4,128)(2,1)S(1)} %get-tuple-element.199), channel_id=1, source_target_pairs={{0,1},{2,3},{4,5},{6,7},{8,9},{10,11},{12,13},{14,15},{16,17},{18,... | collective-permute-start | bytes 49160 | tf_op jit(solution)/shard_map/ppermute | solution.py:70
  774.8 81.2 %collective-permute-start.29 = (bf16[4,4,512]{2,1,0:T(4,128)(2,1)S(1)}, bf16[4,4,512]{2,1,0:T(4,128)(2,1)S(1)}, u32[]{:S(2)}, u32[]{:S(2)}) collective-permute-start(bf16[4,4,512]{2,1,0:T(4,128)(2,1)S(1)} %get-tuple-element.200), channel_id=1, source_target_pairs={{1,0},{3,2},{5,4},{7,6},{9,8},{11,10},{13,12},{15,14},{17,16},{19,... | collective-permute-start | bytes 49160 | tf_op jit(solution)/shard_map/ppermute | solution.py:73
  856.3 51.1 %collective-permute-start.31 = (bf16[4,264,512]{2,1,0:T(8,128)(2,1)S(1)}, bf16[4,264,512]{2,1,0:T(8,128)(2,1)S(1)}, u32[]{:S(2)}, u32[]{:S(2)}) collective-permute-start(bf16[4,264,512]{2,1,0:T(8,128)(2,1)S(1)} %pad_maximum_fusion.3), channel_id=1, source_target_pairs={{0,2},{2,4},{4,6},{6,8},{8,10},{10,12},{12,14},{14,16},{16,18},{18... | collective-permute-start | bytes 3244040 | tf_op jit(solution)/shard_map/ppermute | solution.py:81
  861.9 47.3 %collective-permute-start.30 = (bf16[4,264,512]{2,1,0:T(8,128)(2,1)S(1)}, bf16[4,264,512]{2,1,0:T(8,128)(2,1)S(1)}, u32[]{:S(2)}, u32[]{:S(2)}) collective-permute-start(bf16[4,264,512]{2,1,0:T(8,128)(2,1)S(1)} %pad_maximum_fusion.3), channel_id=1, source_target_pairs={{2,0},{4,2},{6,4},{8,6},{10,8},{12,10},{14,12},{16,14},{18,16},{20... | collective-permute-start | bytes 3244040 | tf_op jit(solution)/shard_map/ppermute | solution.py:81
  (154 other events, 1726.9 us)
Sparse Core Ops, SparseCore 0:
  273.9 143.3 all-reduce.7
  933.9 251.9 all-reduce.9

commit v2 on v1

--- a/solution.py
+++ b/solution.py
@@ -155,6 +155,506 @@
     )
     inner = upstream - shift_grad[:, None, :] / count - normed * (gain_grad / count)[:, None, :]
     return (inner * (gain * scale)[:, None, :], gain_grad, shift_grad, *extra)
+
+
+PAD = 48
+VMEM_BYTES = 60 * 1024 * 1024
+
+
+def place():
+    rows, cols = lax.axis_size("rows"), lax.axis_size("cols")
+    row, col = lax.axis_index("rows"), lax.axis_index("cols")
+    return rows, cols, row, col, row * cols + col
+
+
+def greet_all():
+    rows, cols, row, col, me = place()
+    barrier = pltpu.get_barrier_semaphore()
+
+    def greet(step, carry):
+        other = lax.rem(me + step, rows * cols)
+        pl.semaphore_signal(
+            barrier, inc=1, device_id=(other // cols, lax.rem(other, cols)), device_id_type=MESH
+        )
+        return carry
+
+    lax.fori_loop(1, rows * cols, greet, 0)
+
+
+def await_all():
+    rows, cols = lax.axis_size("rows"), lax.axis_size("cols")
+    pl.semaphore_wait(pltpu.get_barrier_semaphore(), rows * cols - 1)
+
+
+def share(slots, sems):
+    rows, cols, row, col, me = place()
+
+    def go(step, carry):
+        other = lax.rem(me + step, rows * cols)
+        pltpu.make_async_remote_copy(
+            slots.at[me],
+            slots.at[me],
+            sems.at[0],
+            sems.at[1],
+            device_id=(other // cols, lax.rem(other, cols)),
+            device_id_type=MESH,
+        ).start()
+        return carry
+
+    lax.fori_loop(1, rows * cols, go, 0)
+
+
+def shared(slots, sems):
+    rows, cols, row, col, me = place()
+    others = slots.at[pl.ds(0, rows * cols - 1)]
+    pltpu.make_async_remote_copy(
+        others,
+        others,
+        sems.at[0],
+        sems.at[1],
+        device_id=(row, lax.rem(col + 1, cols)),
+        device_id_type=MESH,
+    ).wait()
+
+
+def put_row(slots, me, at, vector):
+    for part in range(vector.shape[1] // LANES):
+        slots[me, at + part : at + part + 1, :] = vector[:, part * LANES : (part + 1) * LANES]
+
+
+def take_row(table, at, width):
+    parts = [table[at + part : at + part + 1, :] for part in range(width // LANES)]
+    return parts[0] if len(parts) == 1 else jnp.concatenate(parts, axis=1)
+
+
+def merged(slots, half, share_size, count):
+    center = jnp.mean(slots[:, :half, :], axis=0)
+    apart = slots[:, :half, :] - center[None]
+    spread = jnp.sum(slots[:, half : 2 * half, :], axis=0) + share_size * jnp.sum(apart * apart, axis=0)
+    return center, lax.rsqrt(spread / count + EPS)
+
+
+def sigmoid(value):
+    return 1.0 / (1.0 + jnp.exp(-value))
+
+
+def across(left, right):
+    return lax.dot_general(left, right, (((1,), (1,)), ((), ())), preferred_element_type=jnp.float32)
+
+
+def down(left, right):
+    return lax.dot_general(left, right, (((0,), (0,)), ((), ())), preferred_element_type=jnp.float32)
+
+
+def pyramid_kernel(
+    height,
+    trunk,
+    depth,
+    sep_point,
+    aspp_point,
+    crop_part,
+    crop_count,
+    members,
+    proj_weight,
+    gains,
+    shifts,
+    head_weight,
+    head_bias,
+    factors,
+    info,
+    branch_low,
+    proj_part,
+    head_part,
+    crop_local,
+    crop_pre,
+    sums_five,
+    sums_four,
+    field,
+    send_main,
+    recv_main,
+    send_side,
+    recv_side,
+    pre,
+    joined,
+    crop_act,
+    projected,
+    united,
+    head_low,
+    upstream,
+    proj_low,
+    branch_up,
+    crop_slots,
+    four_slots,
+    five_slots,
+    back_five,
+    back_four,
+    main_sems,
+    side_sems,
+    crop_sems,
+    four_sems,
+    five_sems,
+    back_five_sems,
+    back_four_sems,
+):
+    rows, cols, row, col, me = place()
+    low, wide = jnp.bfloat16, jnp.float32
+    pixels = trunk.shape[0]
+    width = pixels // height
+    share_size = float(pixels)
+    count = float(pixels * rows * cols)
+    aspp = sep_point.shape[2]
+    greet_all()
+
+    def exists(target):
+        return jnp.logical_and(target >= 0, target < rows)
+
+    for index in range(3):
+        step = BASE_RATE * (index + 1) // height
+        for way in (0, 2):
+
+            @pl.when(jnp.logical_not(exists(row - (1 - way) * step)))
+            def _():
+                recv_main[index, way] = jnp.zeros(recv_main.shape[2:], low)
+                recv_side[index, way] = jnp.zeros(recv_side.shape[2:], low)
+
+    half = crop_part.shape[0]
+    crop_slots[me, :half, :] = crop_part[:, :LANES]
+    crop_slots[me, half:, :] = crop_part[:, LANES:]
+    pre[0] = jnp.dot(trunk[...], aspp_point[...], preferred_element_type=wide)
+    await_all()
+    share(crop_slots, crop_sems)
+    side_from = pl.multiple_of((1 - col) * (PAD + width), 16)
+    side_to = pl.multiple_of((1 - col) * (width - PAD), 16)
+
+    def main_copy(index, way, step):
+        return pltpu.make_async_remote_copy(
+            send_main.at[index, way],
+            recv_main.at[index, way],
+            main_sems.at[0, index, way],
+            main_sems.at[1, index, way],
+            device_id=(row + (1 - way) * step, col),
+            device_id_type=MESH,
+        )
+
+    def side_copy(index, way, step):
+        return pltpu.make_async_remote_copy(
+            send_side.at[index, way],
+            recv_side.at[index, way],
+            side_sems.at[0, index, way],
+            side_sems.at[1, index, way],
+            device_id=(row + (1 - way) * step, 1 - col),
+            device_id_type=MESH,
+        )
+
+    for index in (2, 1, 0):
+        rate = BASE_RATE * (index + 1)
+        step = rate // height
+
+        def one_way(turn, carry):
+            way = lax.rem(2 * turn, 3)
+            for sign in (0, 1, -1):
+                tap = depth[pl.ds(index * 9 + 3 * way + 1 - sign, 1), :].astype(low)
+                made = jnp.dot(trunk[...] * tap, sep_point[index], preferred_element_type=wide)
+                for line in range(height):
+                    part = made[line * width : (line + 1) * width, :]
+                    if sign == 0:
+                        field[line, PAD : PAD + width, :] = part
+                        field[line, :PAD, :] = jnp.zeros((PAD, aspp), wide)
+                        field[line, PAD + width :, :] = jnp.zeros((PAD, aspp), wide)
+                    else:
+                        at = PAD + sign * rate
+                        field[line, at : at + width, :] += part
+            send_side[index, way] = field[:, pl.ds(side_from, PAD), :].astype(low)
+
+            @pl.when(way == 1)
+            def _():
+                for line in range(height):
+                    pre[index + 1, line * width : (line + 1) * width, :] = field[
+                        line, PAD : PAD + width, :
+                    ]
+
+            @pl.when(way != 1)
+            def _():
+                send_main[index, way] = field[:, PAD : PAD + width, :].astype(low)
+
+                @pl.when(exists(row + (1 - way) * step))
+                def _():
+                    main_copy(index, way, step).start()
+
+            @pl.when(exists(row + (1 - way) * step))
+            def _():
+                side_copy(index, way, step).start()
+
+            return carry
+
+        lax.fori_loop(0, 3, one_way, 0)
+
+    def lines(body, carry=0):
+        def run(line, carry):
+            return body(line, pl.ds(pl.multiple_of(line * width, width), width), carry)
+
+        return lax.fori_loop(0, height, run, carry)
+
+    zero_row = jnp.zeros((1, aspp), wide)
+
+    def statistics(value_of, slots, at, half_rows):
+        total = lines(
+            lambda line, span, acc: acc + jnp.sum(value_of(span), axis=0, keepdims=True), zero_row
+        )
+        mean = total / share_size
+
+        def squares(line, span, acc):
+            apart = value_of(span) - mean
+            return acc + jnp.sum(apart * apart, axis=0, keepdims=True)
+
+        put_row(slots, me, at, mean)
+        put_row(slots, me, half_rows + at, lines(squares, zero_row))
+
+    per = aspp // LANES
+    statistics(lambda span: pre[0, span, :], four_slots, 0, 4 * per)
+    for index in (2, 1, 0):
+        step = BASE_RATE * (index + 1) // height
+        for way in (0, 2, 1):
+
+            @pl.when(exists(row - (1 - way) * step))
+            def _():
+                if way != 1:
+                    main_copy(index, way, step).wait_recv()
+                side_copy(index, way, step).wait_recv()
+
+        def assemble(line, span, carry):
+            pre[index + 1, span, :] += recv_main[index, 0, line].astype(wide) + recv_main[
+                index, 2, line
+            ].astype(wide)
+            edge = pl.ds(pl.multiple_of(line * width + side_to, 16), PAD)
+            pre[index + 1, edge, :] += (
+                recv_side[index, 0, line].astype(wide)
+                + recv_side[index, 1, line].astype(wide)
+                + recv_side[index, 2, line].astype(wide)
+            )
+            return carry
+
+        lines(assemble)
+        statistics(lambda span: pre[index + 1, span, :], four_slots, per * (index + 1), 4 * per)
+    share(four_slots, four_sems)
+    shared(crop_slots, crop_sems)
+    crop_total = jnp.sum(crop_slots[...], axis=0)
+    crop_value = jnp.concatenate([crop_total[:half], crop_total[half:]], axis=1) / crop_count[...]
+    crop_pre[...] = crop_value
+    crop_act[...] = jnp.zeros(crop_act.shape, low)
+    crop_act[:half, :] = (crop_value * sigmoid(crop_value)).astype(low)
+
+    def spread(line, span, carry):
+        joined[span, 4 * aspp :] = jnp.dot(
+            members[span, :], crop_act[...], preferred_element_type=wide
+        ).astype(low)
+        return carry
+
+    lines(spread)
+    shared(four_slots, four_sems)
+    center_four, scale_four = merged(four_slots, 4 * per, share_size, count)
+    centers = [take_row(center_four, per * part, aspp) for part in range(4)]
+    scales = [take_row(scale_four, per * part, aspp) for part in range(4)]
+
+    def activate(line, span, carry):
+        for part in range(4):
+            normed = (pre[part, span, :] - centers[part]) * scales[part]
+            gated = normed * gains[part : part + 1, :] + shifts[part : part + 1, :]
+            joined[span, part * aspp : (part + 1) * aspp] = (gated * sigmoid(gated)).astype(low)
+        return carry
+
+    lines(activate)
+    projected[...] = jnp.dot(joined[...], proj_weight[...], preferred_element_type=wide)
+    five_slots[me] = jnp.zeros(five_slots.shape[1:], wide)
+    statistics(lambda span: projected[span, :], five_slots, 0, per)
+    share(five_slots, five_sems)
+    shared(five_slots, five_sems)
+    center_five, scale_five = merged(five_slots, per, share_size, count)
+    center_five, scale_five = take_row(center_five, 0, aspp), take_row(scale_five, 0, aspp)
+    gain_five, shift_five = gains[4:5, :], shifts[4:5, :]
+    lane = lax.broadcasted_iota(jnp.int32, (width, LANES), 1)
+
+    def heads_of(line, span, carry):
+        losses, bias_sum, shift_sum, gain_sum = carry
+        normed = (projected[span, :] - center_five) * scale_five
+        gated = normed * gain_five + shift_five
+        sigma = sigmoid(gated)
+        act = (gated * sigma).astype(low)
+        united[span, :] = act
+        heads = jnp.dot(act, head_weight[...], preferred_element_type=wide) + head_bias[0:1, :]
+        facts = info[span, :]
+        label, keep, valid = facts[:, 0:1], facts[:, 1:2], facts[:, 2:3]
+        is_class = lane < CLASSES
+        hot = jnp.where(lane.astype(wide) == label, 1.0, 0.0)
+        target = jnp.zeros((width, LANES), wide)
+        for part in range(4):
+            target = jnp.where(lane == CLASSES + part, facts[:, 3 + part : 4 + part], target)
+        top = jnp.max(jnp.where(is_class, heads, -jnp.inf), axis=1, keepdims=True)
+        exps = jnp.where(is_class, jnp.exp(heads - top), 0.0)
+        totals = jnp.sum(exps, axis=1, keepdims=True)
+        picked = jnp.sum(jnp.where(is_class, heads, 0.0) * hot, axis=1, keepdims=True)
+        error = jnp.where(is_class, 0.0, heads - target)
+        root = jnp.sqrt(error * error + 1.0)
+        is_depth, is_normal = lane == CLASSES, jnp.logical_and(lane > CLASSES, lane < CLASSES + 4)
+        semantic = keep * (top + jnp.log(totals) - picked)
+        terms = jnp.where(lane == 0, semantic, 0.0)
+        terms = jnp.where(is_depth, valid * (root - 1.0), terms)
+        terms = jnp.where(is_normal, valid * error * error, terms)
+        grad = jnp.where(is_class, keep * (exps / totals - hot), 0.0)
+        grad = jnp.where(is_depth, valid * error / root, grad)
+        grad = jnp.where(is_normal, valid * error, grad)
+        grad = grad * factors[0:1, :]
+        grad_low = grad.astype(low)
+        head_low[span, :] = grad_low
+        up = across(grad_low, head_weight[...]) * (sigma * (1.0 + gated * (1.0 - sigma)))
+        upstream[span, :] = up
+        return (
+            losses + jnp.sum(terms, axis=0, keepdims=True),
+            bias_sum + jnp.sum(grad, axis=0, keepdims=True),
+            shift_sum + jnp.sum(up, axis=0, keepdims=True),
+            gain_sum + jnp.sum(up * normed, axis=0, keepdims=True),
+        )
+
+    zero_lane = jnp.zeros((1, LANES), wide)
+    losses, bias_sum, shift_sum, gain_sum = lines(
+        heads_of, (zero_lane, zero_lane, zero_row, zero_row)
+    )
+    back_five[me] = jnp.zeros(back_five.shape[1:], wide)
+    put_row(back_five, me, 0, shift_sum)
+    put_row(back_five, me, per, gain_sum)
+    put_row(back_five, me, 2 * per, losses)
+    put_row(back_five, me, 2 * per + 1, bias_sum)
+    share(back_five, back_five_sems)
+    head_part[...] = down(united[...], head_low[...]).astype(low)
+    shared(back_five, back_five_sems)
+    total_five = jnp.sum(back_five[...], axis=0)
+    sums_five[...] = total_five
+    shift_mean = take_row(total_five, 0, aspp) / count
+    gain_mean = take_row(total_five, per, aspp) / count
+
+    def project_back(line, span, carry):
+        normed = (projected[span, :] - center_five) * scale_five
+        inner = upstream[span, :] - shift_mean - normed * gain_mean
+        proj_low[span, :] = (inner * (gain_five * scale_five)).astype(low)
+        return carry
+
+    lines(project_back)
+    for part in range(4):
+        branch_up[part] = across(
+            proj_low[...], proj_weight[part * aspp : (part + 1) * aspp, :]
+        )
+    crop_up = across(proj_low[...], proj_weight[4 * aspp :, :])
+    crop_high = crop_up.astype(low)
+    crop_rest = (crop_up - crop_high.astype(wide)).astype(low)
+    crop_sum = down(members[...], crop_high) + down(members[...], crop_rest)
+    crop_local[...] = crop_sum[:half, :]
+
+    for part in range(4):
+
+        def branch_sums(line, span, carry):
+            shift_sum, gain_sum = carry
+            normed = (pre[part, span, :] - centers[part]) * scales[part]
+            gated = normed * gains[part : part + 1, :] + shifts[part : part + 1, :]
+            sigma = sigmoid(gated)
+            up = branch_up[part, span, :] * (sigma * (1.0 + gated * (1.0 - sigma)))
+            branch_up[part, span, :] = up
+            return (
+                shift_sum + jnp.sum(up, axis=0, keepdims=True),
+                gain_sum + jnp.sum(up * normed, axis=0, keepdims=True),
+            )
+
+        shift_sum, gain_sum = lines(branch_sums, (zero_row, zero_row))
+        put_row(back_four, me, per * part, shift_sum)
+        put_row(back_four, me, per * (4 + part), gain_sum)
+    share(back_four, back_four_sems)
+    proj_part[...] = down(joined[...], proj_low[...]).astype(low)
+    shared(back_four, back_four_sems)
+    total_four = jnp.sum(back_four[...], axis=0)
+    sums_four[...] = total_four
+    for part in range(4):
+        shift_mean = take_row(total_four, per * part, aspp) / count
+        gain_mean = take_row(total_four, per * (4 + part), aspp) / count
+        factor = gains[part : part + 1, :] * scales[part]
+
+        def branch_back(line, span, carry):
+            normed = (pre[part, span, :] - centers[part]) * scales[part]
+            inner = branch_up[part, span, :] - shift_mean - normed * gain_mean
+            branch_low[part, span, :] = (inner * factor).astype(low)
+            return carry
+
+        lines(branch_back)
+    for index in range(3):
+        step = BASE_RATE * (index + 1) // height
+        for way in range(3):
+
+            @pl.when(exists(row + (1 - way) * step))
+            def _():
+                if way != 1:
+                    main_copy(index, way, step).wait_send()
+                side_copy(index, way, step).wait_send()
+
+
+def pyramid(height, trunk, depth, sep_point, aspp_point, crop_part, crop_count, members, proj_weight,
+            gains, shifts, head_weight, head_bias, factors, info):
+    devices = lax.axis_size("rows") * lax.axis_size("cols")
+    pixels = trunk.shape[0]
+    width = pixels // height
+    aspp = sep_point.shape[2]
+    crops = crop_part.shape[0]
+    low, wide = jnp.bfloat16, jnp.float32
+    shape = jax.ShapeDtypeStruct
+    whole = pl.BlockSpec(memory_space=pltpu.VMEM)
+    joined = proj_weight.shape[0]
+    per = aspp // LANES
+    outs = (
+        shape((4, pixels, aspp), low),
+        shape((joined, aspp), low),
+        shape((aspp, LANES), low),
+        shape((crops, aspp), wide),
+        shape((crops, aspp), wide),
+        shape((8, LANES), wide),
+        shape((8 * per, LANES), wide),
+    )
+    sems = pltpu.SemaphoreType.DMA
+    return pl.pallas_call(
+        functools.partial(pyramid_kernel, height),
+        out_shape=outs,
+        in_specs=[whole] * 14,
+        out_specs=(whole,) * len(outs),
+        scratch_shapes=[
+            pltpu.VMEM((height, width + 2 * PAD, aspp), wide),
+            pltpu.VMEM((3, 3, height, width, aspp), low),
+            pltpu.VMEM((3, 3, height, width, aspp), low),
+            pltpu.VMEM((3, 3, height, PAD, aspp), low),
+            pltpu.VMEM((3, 3, height, PAD, aspp), low),
+            pltpu.VMEM((4, pixels, aspp), wide),
+            pltpu.VMEM((pixels, joined), low),
+            pltpu.VMEM((LANES, aspp), low),
+            pltpu.VMEM((pixels, aspp), wide),
+            pltpu.VMEM((pixels, aspp), low),
+            pltpu.VMEM((pixels, LANES), low),
+            pltpu.VMEM((pixels, aspp), wide),
+            pltpu.VMEM((pixels, aspp), low),
+            pltpu.VMEM((4, pixels, aspp), wide),
+            pltpu.VMEM((devices, 2 * crops, LANES), wide),
+            pltpu.VMEM((devices, 8 * per, LANES), wide),
+            pltpu.VMEM((devices, 8, LANES), wide),
+            pltpu.VMEM((devices, 8, LANES), wide),
+            pltpu.VMEM((devices, 8 * per, LANES), wide),
+            sems((2, 3, 3)),
+            sems((2, 3, 3)),
+            sems((2,)),
+            sems((2,)),
+            sems((2,)),
+            sems((2,)),
+            sems((2,)),
+        ],
+        compiler_params=pltpu.CompilerParams(
+            collective_id=10, has_side_effects=True, vmem_limit_bytes=VMEM_BYTES
+        ),
+        name="pyramid",
+    )(trunk, depth, sep_point, aspp_point, crop_part, crop_count, members, proj_weight, gains, shifts,
+      head_weight, head_bias, factors, info)
 
 
 def on_device(
@@ -230,102 +730,54 @@
     normed_three = normalize(expanded, center, scale_three)
     pre_trunk = normed_three[0] * out_gain + out_shift + flat.astype(jnp.float32)
     trunk = sigmoid_linear(pre_trunk).astype(low)
-    taps = sep_depth.astype(jnp.float32)[:, :, :, None] * sep_point.astype(jnp.float32)[:, None, :, :]
-    taps = jnp.transpose(taps.astype(low), (0, 2, 1, 3)).reshape(3, channels, 9 * aspp_width)
-    branch_pre = [matmul(trunk, aspp_point)]
-    for index in range(3):
-        rate = BASE_RATE * (index + 1)
-        step = rate // height
-        made = matmul(trunk, taps[index]).astype(low).reshape(height, width, 3, 3, aspp_width)
-        side = lax.axis_size("cols")
-        up = [(i, i + 1) for i in range(side - 1)]
-        down = [(i + 1, i) for i in range(side - 1)]
-        before = lax.ppermute(made[:, width - rate :, :, 0, :], "cols", up)
-        after = lax.ppermute(made[:, :rate, :, 2, :], "cols", down)
-        wide = jnp.float32
-        rows_sum = (
-            made[:, :, :, 1].astype(wide)
-            + jnp.concatenate([before, made[:, : width - rate, :, 0]], axis=1).astype(wide)
-            + jnp.concatenate([made[:, rate:, :, 2], after], axis=1).astype(wide)
-        )
-        above = from_behind(rows_sum[:, :, 0].astype(low), "rows", step).astype(wide)
-        below = from_behind(rows_sum[:, :, 2].astype(low), "rows", -step).astype(wide)
-        branch_pre.append((rows_sum[:, :, 1] + above + below).reshape(pixels, aspp_width))
-    stacked = jnp.stack(branch_pre)
     local_sums = jnp.einsum("pk,pc->kc", members, trunk, preferred_element_type=jnp.float32)
-    mean, square = local_stats(stacked)
     crop_part = jnp.dot(local_sums, pool_weight.astype(jnp.float32), precision=highest)
-    means, squares, crop_parts = unpack(
-        gather_all(pack(mean, square, crop_part), 3), mean.shape, square.shape, crop_part.shape
-    )
-    center, scale_branch = merged_stats(means, squares, share, count)
-    normed_branch = normalize(stacked, center, scale_branch)
-    gated_branch = normed_branch * aspp_gain[:4, None, :] + aspp_shift[:4, None, :]
-    branch_act = sigmoid_linear(gated_branch).astype(low)
-    crop_pre = jnp.sum(crop_parts, axis=0) / crop_count[:, None]
-    crop_act = sigmoid_linear(crop_pre).astype(low)
-    crop_spread = matmul(members, crop_act).astype(low)
-    joined = jnp.concatenate(
-        [branch_act[0], branch_act[1], branch_act[2], branch_act[3], crop_spread], axis=1
-    )
-    projected = matmul(joined, proj_weight)[None]
-    mean, square = local_stats(projected)
-    means, squares = unpack(gather_all(pack(mean, square), 4), mean.shape, square.shape)
-    center, scale_proj = merged_stats(means, squares, share, count)
-    normed_proj = normalize(projected, center, scale_proj)
-    gated_proj = normed_proj[0] * aspp_gain[4] + aspp_shift[4]
-    united = sigmoid_linear(gated_proj).astype(low)
-    heads = matmul(united, head_weight) + head_bias
-    logits = heads[:, :CLASSES]
-    top = jnp.max(logits, axis=1, keepdims=True)
-    exps = jnp.exp(logits - top)
-    totals = jnp.sum(exps, axis=1)
-    label_hot = (labels.reshape(pixels)[:, None] == jnp.arange(CLASSES)[None, :]).astype(
-        jnp.float32
-    )
-    picked = jnp.sum(logits * label_hot, axis=1)
-    target = geometry_target.reshape(4, pixels)
-    depth_error = heads[:, CLASSES] - target[0]
-    root = jnp.sqrt(depth_error * depth_error + 1.0)
-    normal_error = heads[:, CLASSES + 1 :] - target[1:].T
-    local_losses = jnp.stack(
-        [
-            jnp.sum(keep * (top[:, 0] + jnp.log(totals) - picked)),
-            jnp.sum(valid * (root - 1.0)),
-            jnp.sum(valid * jnp.sum(normal_error * normal_error, axis=1)),
-        ]
-    )
+    scale_exp = jnp.exp(task_scales)
     counts = jnp.stack([keep_count, valid_count, valid_count])
-    scale_exp = jnp.exp(task_scales)
     factor = scale_exp / counts
-    logit_grad = factor[0] * keep[:, None] * (exps / totals[:, None] - label_hot)
-    depth_grad = factor[1] * valid * depth_error / root
-    normal_grad = factor[2] * valid[:, None] * 2.0 * normal_error
-    head_grad = jnp.concatenate([logit_grad, depth_grad[:, None], normal_grad], axis=1)
-    head_low = head_grad.astype(low)
-    head_weight_part = jnp.einsum("pc,pk->ck", united, head_low, preferred_element_type=jnp.float32)
-    united_grad = jnp.einsum("pk,ck->pc", head_low, head_weight, preferred_element_type=jnp.float32)
-    proj_grad, proj_gain_grad, proj_shift_grad, loss_sums, grad_head_bias = norm_backward(
-        (united_grad * gate_slope(gated_proj))[None], normed_proj, scale_proj, aspp_gain[4:5], count,
-        5, local_losses, jnp.sum(head_grad, axis=0),
+    lane = jnp.arange(LANES)
+    factors = jnp.where(
+        lane < CLASSES, factor[0], jnp.where(lane == CLASSES, factor[1], 2.0 * factor[2])
+    )
+    outs = head_weight.shape[1]
+    wide_row = ((0, 0), (0, LANES - outs))
+    info = jnp.stack(
+        [labels.reshape(pixels).astype(jnp.float32), keep, valid, *geometry_target.reshape(4, pixels)],
+        axis=1,
+    )
+    branch_low, proj_part, head_part, crop_local, crop_pre, sums_five, sums_four = pyramid(
+        height,
+        trunk,
+        jnp.pad(sep_depth.reshape(27, channels).astype(jnp.float32), ((0, 5), (0, 0))),
+        sep_point,
+        aspp_point,
+        crop_part,
+        jnp.broadcast_to(crop_count[:, None], (CROPS, aspp_width)),
+        jnp.pad(members, ((0, 0), (0, LANES - CROPS))),
+        proj_weight,
+        jnp.pad(aspp_gain, ((0, 3), (0, 0))),
+        jnp.pad(aspp_shift, ((0, 3), (0, 0))),
+        jnp.pad(head_weight, wide_row),
+        jnp.pad(jnp.broadcast_to(head_bias, (8, outs)), wide_row),
+        jnp.broadcast_to(factors, (8, LANES)),
+        jnp.pad(info, ((0, 0), (0, 1))),
+    )
+    per = aspp_width // LANES
+    proj_shift_grad = sums_five[:per].reshape(1, aspp_width)
+    proj_gain_grad = sums_five[per : 2 * per].reshape(1, aspp_width)
+    loss_row = sums_five[2 * per]
+    grad_head_bias = sums_five[2 * per + 1, :outs]
+    branch_shift_grad = sums_four[: 4 * per].reshape(4, aspp_width)
+    branch_gain_grad = sums_four[4 * per :].reshape(4, aspp_width)
+    loss_sums = jnp.stack(
+        [loss_row[0], loss_row[CLASSES], jnp.sum(loss_row[CLASSES + 1 : CLASSES + 4])]
     )
     losses = loss_sums / counts
     objective = jnp.sum(scale_exp * losses - task_scales)
     grad_scales = scale_exp * losses - 1.0
-    proj_low = proj_grad[0].astype(low)
-    grad_proj_weight = jnp.einsum("pc,pd->cd", joined, proj_low, preferred_element_type=jnp.float32)
-    joined_grad = jnp.einsum("pd,cd->pc", proj_low, proj_weight, preferred_element_type=jnp.float32)
-    branch_up = jnp.stack(
-        [joined_grad[:, branch * aspp_width : (branch + 1) * aspp_width] for branch in range(4)]
-    )
-    crop_local = jnp.einsum(
-        "pk,pc->kc", members_wide, joined_grad[:, 4 * aspp_width :], precision=highest
-    )
-    branch_grad, branch_gain_grad, branch_shift_grad, crop_total = norm_backward(
-        branch_up * gate_slope(gated_branch), normed_branch, scale_branch, aspp_gain[:4], count,
-        6, crop_local,
-    )
-    branch_low = branch_grad.astype(low)
+    (crop_total,) = shared_sums(3, crop_local)
+    taps = sep_depth.astype(jnp.float32)[:, :, :, None] * sep_point.astype(jnp.float32)[:, None, :, :]
+    taps = jnp.transpose(taps.astype(low), (0, 2, 1, 3)).reshape(3, channels, 9 * aspp_width)
     crop_low = (crop_total * gate_slope(crop_pre)).astype(low)
     pooled = (lax.psum(local_sums, ("rows", "cols")) / crop_count[:, None]).astype(low)
     grad_pool_weight = jnp.einsum("kc,kd->cd", pooled, crop_low, preferred_element_type=jnp.float32)
@@ -409,8 +861,8 @@
         grad_aspp_point,
         jnp.stack(depth_grads),
         jnp.stack(point_grads),
-        grad_proj_weight,
-        jnp.pad(head_weight_part, ((0, 0), (0, LANES - head_weight_part.shape[1]))),
+        proj_part,
+        head_part,
     )
     summed = lax.psum(tuple(part.astype(low) for part in parts), ("rows", "cols"))
     summed = [part.astype(jnp.float32) for part in summed]

time: 1230 us -> 1050 us (0.85)
  local copies, waits for them, and re-layouts: 209 us -> 99.9 us
  Pallas kernels: 167 us -> 260 us
  matrix products: 244 us -> 186 us
  other arithmetic: 136 us -> 83 us
  starting transfers between devices: 91.4 us -> 53.8 us
  waiting for transfers between devices: 356 us -> 334 us
    pallas_call x0 -> x1, Pallas kernels: none -> 145 us  [pyramid(): pl.pallas_call(functools.partial(pyramid_kernel, height), out_shape=outs,...]
    pallas_call x10 -> x7, Pallas kernels: 167 us -> 115 us  [gather_all(): pl.pallas_call(functools.partial(gather_kernel, rows, cols), out_shape=ja...]
    dot_general x18 -> x11, matrix products: 73.5 us -> 21.5 us  [matmul(): return jnp.dot(left, right, preferred_element_type=jnp.float32)]
    squeeze x13 -> x1, local copies, waits for them, and re-layouts: 32.9 us -> 0.51 us  [on_device(): grad_head_bias = sums_five[2 * per + 1, :outs]]
    reshape x3, local copies, waits for them, and re-layouts: 26.6 us -> 0.03 us  [the longest x1 0.01 us: on_device(): branch_gain_grad = sums_four[4 * per:].reshape(4, aspp_width)]
    convert_element_type x6 -> x1, local copies, waits for them, and re-layouts: 24 us -> 0.04 us  [on_device(): sep_depth.reshape(27, channels).astype(jnp.float32)]
    ppermute x16 -> x10, starting transfers between devices: 55.4 us -> 32.7 us  [from_behind(): lax.ppermute(value, axis, [(source, source + steps) for source in range(i...]
    another operation x3 -> x0, other arithmetic: 19.8 us -> none
  transfers between devices with their start and end apart: 34 -> 22, of which waited for: 10 -> 8; matrix products, arithmetic and copies ran while one was open for 36% -> 27% of each run, Pallas kernels for 10% -> 7%
where the time goes in v2:
time: 1050 us; the launch traced here: 1030 us
  waiting for transfers between devices  334 us (32%)
  Pallas kernels  260 us (25%)
  matrix products  186 us (18%)
  local copies, waits for them, and re-layouts  99.9 us (10%)
  other arithmetic  83 us (8%)
  starting transfers between devices  53.8 us (5%)
  between operations  17.1 us (2%)
    psum x1, waiting for transfers between devices, on_device(): lax.psum(tuple((part.astype(low) for part in parts)), ('rows', 'cols'))  232 us
    pallas_call x1, Pallas kernels, pyramid(): pl.pallas_call(functools.partial(pyramid_kernel, height), out_shape=outs,...  145 us
    pallas_call x7, Pallas kernels, gather_all(): pl.pallas_call(functools.partial(gather_kernel, rows, cols), out_shape=ja...  115 us
    ppermute x10, waiting for transfers between devices, from_behind(): lax.ppermute(value, axis, [(source, source + steps) for source in range(i...  102 us
    dot_general x3, matrix products, on_device(): jnp.einsum('pd,cd->pc', moved, taps[index], preferred_element_type=jnp.fl...  52.4 us
    dot_general x3, matrix products, on_device(): jnp.einsum('pc,pd->cd', trunk, moved, preferred_element_type=jnp.float32)  43.9 us
    ppermute x10, starting transfers between devices, from_behind(): lax.ppermute(value, axis, [(source, source + steps) for source in range(i...  32.7 us
    unnamed x249, local copies, waits for them, and re-layouts  29.9 us
  transfers between devices with their start and end apart: 22, of which 8 were waited for; matrix products, arithmetic and copies ran while one was open for 27% of the time, Pallas kernels for 7%

profile of v2, /device:TPU:11, one launch (start us, length us, event | category | flops | bytes accessed | tf_op | source)
XLA Modules:
  0.0 1034.0 jit_solution(16008133777902464788)
XLA Ops:
  16.6 12.8 %gather_all.7 = f32[32,16,128]{2,1,0:T(8,128)} custom-call(f32[16,128]{1,0:T(8,128)} %pad_bitcast_fusion.x_ref), custom_call_target="tpu_custom_call" | custom-call | tf_op jit(solution)/shard_map/gather_all/pallas_call | solution.py:53
  55.7 9.1 multiply_convert_fusion
  64.8 9.9 fusion.104
  114.3 18.3 %collective-permute-done.2 = bf16[4,264,512]{2,1,0:T(8,128)(2,1)S(1)} collective-permute-done((bf16[4,264,512]{2,1,0:T(8,128)(2,1)}, bf16[4,264,512]{2,1,0:T(8,128)(2,1)S(1)}, u32[]{:S(2)}, u32[]{:S(2)}) %collective-permute-start.2) | collective-permute-done | bytes 1081376 | tf_op jit(solution)/shard_map/ppermute | solution.py:81
  139.1 8.8 gather_all.8
  157.6 17.9 %gather_all.9 = f32[32,32,128]{2,1,0:T(8,128)} custom-call(f32[32,128]{1,0:T(8,128)} %pad_maximum_fusion.17.x_ref), custom_call_target="tpu_custom_call" | custom-call | tf_op jit(solution)/shard_map/gather_all/pallas_call | solution.py:53
  177.7 6.3 multiply_convert_fusion.2.trunk
  190.2 145.3 %pyramid.1 = (bf16[4,1024,256]{2,1,0:T(8,128)(2,1)}, bf16[1280,256]{1,0:T(8,128)(2,1)}, bf16[256,128]{1,0:T(8,128)(2,1)}, f32[16,256]{1,0:T(8,128)}, f32[16,256]...) custom-call(bf16[1024,2048]{1,0:T(8,128)(2,1)} %copy-done.3, f32[32,2048]{1,0:T(8,128)} %pad_convert_fusion.depth, ...), custom_call_target="tpu_custom_call" | custom-call | tf_op jit(solution)/shard_map/pyramid/pallas_call | solution.py:619
  337.8 6.1 fusion.26
  360.7 16.8 %gather_all.10 = f32[32,32,128]{2,1,0:T(8,128)} custom-call(f32[32,128]{1,0:T(8,128)} %reshape_reshape.3.x_ref), custom_call_target="tpu_custom_call" | custom-call | tf_op jit(solution)/shard_map/gather_all/pallas_call | solution.py:53
  381.0 5.8 fusion.68
  408.2 7.1 collective-permute-start.15
  415.6 6.9 collective-permute-done.7
  431.6 23.2 %collective-permute-done.14 = bf16[4,328,256]{2,1,0:T(8,128)(2,1)S(1)} collective-permute-done((bf16[4,328,256]{2,1,0:T(8,128)(2,1)S(1)}, bf16[4,328,256]{2,1,0:T(8,128)(2,1)S(1)}, u32[]{:S(2)}, u32[]{:S(2)}) %collective-permute-start.14) | collective-permute-done | bytes 671776 | tf_op jit(solution)/shard_map/ppermute | solution.py:81
  460.0 12.3 %fusion.132 = f32[1024,2048]{1,0:T(8,128)} fusion(bf16[1024,2304]{1,0:T(8,128)(2,1)S(1)} %constant_dynamic-update-slice_fusion, bf16[2048,2304]{0,1:T(8,128)(2,1)S(1)} %bitcast.407), kind=kOutput, calls=%fused_computation.302 | convolution fusion | flops 9663676416 | bytes 22544384 | tf_op jit(solution)/shard_map/pd,cd->pc/dot_general | solution.py:803
  473.6 12.1 %fusion.133 = f32[1024,2048]{1,0:T(8,128)} fusion(bf16[1024,2304]{1,0:T(8,128)(2,1)S(1)} %constant_dynamic-update-slice_fusion.8, bf16[2048,2304]{0,1:T(8,128)(2,1)S(1)} %bitcast.404), kind=kOutput, calls=%fused_computation.303 | convolution fusion | flops 9663676416 | bytes 22544384 | tf_op jit(solution)/shard_map/pd,cd->pc/dot_general | solution.py:803
  485.7 28.0 %fusion.99 = (f32[2048]{0:T(1024)S(1)}, f32[2048]{0:T(1024)S(1)}, f32[1024,2048]{1,0:T(8,128)}) fusion(f32[2048]{0:T(1024)S(1)} %get-tuple-element.126, f32[1024,2048]{1,0:T(8,128)} %copy-done.2, f32[2048]{0:T(1024)S(1)} %broadcast_multiply_fusion.2, bf16[4,256,2048]{2,1,0:T(8,128)(2,1)} %param.23, f32[2048]{0:T(1024)S(1)} %copy-done.74, ...), kind=kOutput, calls=%fused_computation.270 | convolution fusion | flops 9707712512 | bytes 68730880 | tf_op jit(solution)/shard_map/pd,cd->pc/dot_general | solution.py:803
  514.3 38.9 %gather_all.11 = f32[32,32,128]{2,1,0:T(8,128)} custom-call(f32[32,128]{1,0:T(8,128)} %pad_maximum_fusion.18.x_ref), custom_call_target="tpu_custom_call" | custom-call | tf_op jit(solution)/shard_map/gather_all/pallas_call | solution.py:53
  555.0 7.6 multiply_convert_fusion.1
  571.7 10.9 %gather_all.12 = f32[32,8,128]{2,1,0:T(8,128)} custom-call(f32[8,128]{1,0:T(8,128)} %pad_maximum_fusion.22.x_ref), custom_call_target="tpu_custom_call" | custom-call | tf_op jit(solution)/shard_map/gather_all/pallas_call | solution.py:53
  606.1 6.8 copy.85
  612.9 6.6 copy.81
  619.5 6.6 copy.83
  626.2 16.5 %multiply_reduce_fusion = (bf16[2048,256]{0,1:T(8,128)(2,1)S(1)}, bf16[2048,9]{0,1:T(8,128)(2,1)S(1)}) fusion(f32[2048,9]{0,1:T(8,128)S(1)} %copy-done.50, f32[2048,256]{0,1:T(8,128)} %copy.86, bf16[9,256,1024]{2,1,0:T(8,128)(2,1)} %bitcast.424, bf16[1024,2048]{1,0:T(8,128)(2,1)} %copy-done.3), kind=kOutput, calls=%fused_computation.1 | convolution fusion | flops 9682008064 | bytes 12169216 | tf_op jit(solution)/shard_map/pc,pd->cd/dot_general | solution.py:806
  642.8 13.8 %multiply_reduce_fusion.2 = (bf16[2048,256]{0,1:T(8,128)(2,1)S(1)}, bf16[2048,9]{0,1:T(8,128)(2,1)S(1)}) fusion(f32[2048,9]{0,1:T(8,128)S(1)} %copy-done.49, f32[2048,256]{0,1:T(8,128)S(1)} %copy-done.41, bf16[9,256,1024]{2,1,0:T(8,128)(2,1)S(1)} %bitcast.423, bf16[1024,2048]{1,0:T(8,128)(2,1)S(1)} %copy-done.5), kind=kOutput, calls=%fused_computation.3 | convolution fusion | flops 9682008064 | bytes 12169216 | tf_op jit(solution)/shard_map/pc,pd->cd/dot_general | solution.py:806
  656.7 13.6 %multiply_reduce_fusion.1 = (bf16[2048,256]{0,1:T(8,128)(2,1)S(1)}, bf16[2048,9]{0,1:T(8,128)(2,1)S(1)}) fusion(f32[2048,9]{0,1:T(8,128)S(1)} %copy-done.48, f32[2048,256]{0,1:T(8,128)S(1)} %copy-done.40, bf16[9,256,1024]{2,1,0:T(8,128)(2,1)S(1)} %bitcast.422, bf16[1024,2048]{1,0:T(8,128)(2,1)S(1)} %copy-done.5), kind=kOutput, calls=%fused_computation.2 | convolution fusion | flops 9682008064 | bytes 12169216 | tf_op jit(solution)/shard_map/pc,pd->cd/dot_general | solution.py:806
  682.2 42.2 %collective-permute-done.19 = bf16[4,264,512]{2,1,0:T(8,128)(2,1)S(1)} collective-permute-done((bf16[4,264,512]{2,1,0:T(8,128)(2,1)S(1)}, bf16[4,264,512]{2,1,0:T(8,128)(2,1)S(1)}, u32[]{:S(2)}, u32[]{:S(2)}) %collective-permute-start.19) | collective-permute-done | bytes 1081376 | tf_op jit(solution)/shard_map/ppermute | solution.py:81
  732.7 9.0 gather_all.13
  761.4 8.6 add_convert_fusion
  770.1 231.7 %all-reduce.14.cloned.1.call-done = (bf16[2048,512]{0,1:T(8,128)(2,1)}, bf16[3,9,2048]{2,1,0:T(8,128)(2,1)}, bf16[3,2048,256]{1,2,0:T(8,128)(2,1)}, bf16[9,512,5...) async-done(((bf16[2048,512]{0,1:T(8,128)(2,1)}, ...) | async-done | bytes 13938704 | tf_op jit(solution)/shard_map/psum | solution.py:867
  1001.8 7.4 convert_element_type.256
  1009.1 5.5 copy.92
  (453 shorter events, 244.4 us)
Async XLA Ops:
  7.2 142.3 %copy-start = (bf16[512,2048]{1,0:T(8,128)(2,1)S(1)}, bf16[512,2048]{1,0:T(8,128)(2,1)}, u32[]{:S(2)}) copy-start(bf16[512,2048]{1,0:T(8,128)(2,1)} %param.26) | copy-start | bytes 6291460
  30.6 118.3 %copy-start.56 = (f32[512]{0:T(512)}, f32[512]{0:T(512)S(1)}, u32[]{:S(2)}) copy-start(f32[512]{0:T(512)S(1)} %add_rsqrt_fusion.2) | copy-start | bytes 6148
  34.5 43.6 %collective-permute-start = (bf16[4,4,512]{2,1,0:T(4,128)(2,1)S(1)}, bf16[4,4,512]{2,1,0:T(4,128)(2,1)S(1)}, u32[]{:S(2)}, u32[]{:S(2)}) collective-permute-start(bf16[4,4,512]{2,1,0:T(4,128)(2,1)S(1)} %get-tuple-element.157), channel_id=1, source_target_pairs={{0,1},{2,3},{4,5},{6,7},{8,9},{10,11},{12,13},{14,15},{16,17},{18,... | collective-permute-start | bytes 49160 | tf_op jit(solution)/shard_map/ppermute | solution.py:70
  35.8 42.4 %collective-permute-start.1 = (bf16[4,4,512]{2,1,0:T(4,128)(2,1)S(1)}, bf16[4,4,512]{2,1,0:T(4,128)(2,1)S(1)}, u32[]{:S(2)}, u32[]{:S(2)}) collective-permute-start(bf16[4,4,512]{2,1,0:T(4,128)(2,1)S(1)} %get-tuple-element.158), channel_id=1, source_target_pairs={{1,0},{3,2},{5,4},{7,6},{9,8},{11,10},{13,12},{15,14},{17,16},{19,... | collective-permute-start | bytes 49160 | tf_op jit(solution)/shard_map/ppermute | solution.py:73
  79.4 30.9 %collective-permute-start.3 = (bf16[4,264,512]{2,1,0:T(8,128)(2,1)}, bf16[4,264,512]{2,1,0:T(8,128)(2,1)}, u32[]{:S(2)}, u32[]{:S(2)}) collective-permute-start(bf16[4,264,512]{2,1,0:T(8,128)(2,1)} %pad_maximum_fusion.1), channel_id=1, source_target_pairs={{2,0},{4,2},{6,4},{8,6},{10,8},{12,10},{14,12},{16,14},{18,16},{20... | collective-permute-start | bytes 3244040 | tf_op jit(solution)/shard_map/ppermute | solution.py:81
  101.5 31.2 %collective-permute-start.2 = (bf16[4,264,512]{2,1,0:T(8,128)(2,1)}, bf16[4,264,512]{2,1,0:T(8,128)(2,1)S(1)}, u32[]{:S(2)}, u32[]{:S(2)}) collective-permute-start(bf16[4,264,512]{2,1,0:T(8,128)(2,1)} %pad_maximum_fusion.1), channel_id=1, source_target_pairs={{0,2},{2,4},{4,6},{6,8},{8,10},{10,12},{12,14},{14,16},{16,18},{18... | collective-permute-start | bytes 3244040 | tf_op jit(solution)/shard_map/ppermute | solution.py:81
  112.9 22.3 %copy-start.36 = (bf16[4,256,512]{2,1,0:T(8,128)(2,1)}, bf16[4,256,512]{2,1,0:T(8,128)(2,1)S(1)}, u32[]{:S(2)}) copy-start(bf16[4,256,512]{2,1,0:T(8,128)(2,1)S(1)} %get-tuple-element.145) | copy-start | bytes 3145732
  153.7 23.3 %copy-start.58 = (f32[2048]{0:T(1024)S(1)}, f32[2048]{0:T(1024)}, u32[]{:S(2)}) copy-start(f32[2048]{0:T(1024)} %param.29) | copy-start | bytes 24580
  153.7 23.9 %copy-start.73 = (f32[2048]{0:T(1024)S(1)}, f32[2048]{0:T(1024)}, u32[]{:S(2)}) copy-start(f32[2048]{0:T(1024)} %param.30) | copy-start | bytes 24580
  186.7 148.8 %copy-start.43 = (f32[16,2048]{1,0:T(8,128)}, f32[16,2048]{1,0:T(8,128)S(1)}, u32[]{:S(2)}) copy-start(f32[16,2048]{1,0:T(8,128)S(1)} %fusion.69) | copy-start | bytes 393220
  188.3 569.1 %all-reduce.12.cloned.1.call-start = ((), (), s32[]{:S(2)}) async-start(), calls=%async_computation | async-start | bytes 262144 | tf_op jit(solution)/shard_map/psum | solution.py:782
  347.4 654.4 %all-reduce.14.cloned.1.call-start = ((), (), s32[]{:S(2)}) async-start(), calls=%async_computation.1 | async-start | bytes 28049408 | tf_op jit(solution)/shard_map/psum | solution.py:867
  348.1 49.6 %collective-permute-start.12 = (bf16[4,36,256]{2,1,0:T(8,128)(2,1)}, bf16[4,36,256]{2,1,0:T(8,128)(2,1)S(1)}, u32[]{:S(2)}, u32[]{:S(2)}) collective-permute-start(bf16[4,36,256]{2,1,0:T(8,128)(2,1)} %get-tuple-element.187), channel_id=1, source_target_pairs={{0,1},{2,3},{4,5},{6,7},{8,9},{10,11},{12,13},{14,15},{16,17},{18,... | collective-permute-start | bytes 221192 | tf_op jit(solution)/shard_map/ppermute | solution.py:70
  349.4 53.3 %collective-permute-start.13 = (bf16[4,36,256]{2,1,0:T(8,128)(2,1)}, bf16[4,36,256]{2,1,0:T(8,128)(2,1)S(1)}, u32[]{:S(2)}, u32[]{:S(2)}) collective-permute-start(bf16[4,36,256]{2,1,0:T(8,128)(2,1)} %get-tuple-element.188), channel_id=1, source_target_pairs={{1,0},{3,2},{5,4},{7,6},{9,8},{11,10},{13,12},{15,14},{17,16},{19,... | collective-permute-start | bytes 221192 | tf_op jit(solution)/shard_map/ppermute | solution.py:73
  353.0 38.5 %collective-permute-start.8 = (bf16[4,24,256]{2,1,0:T(8,128)(2,1)}, bf16[4,24,256]{2,1,0:T(8,128)(2,1)S(1)}, u32[]{:S(2)}, u32[]{:S(2)}) collective-permute-start(bf16[4,24,256]{2,1,0:T(8,128)(2,1)} %get-tuple-element.183), channel_id=1, source_target_pairs={{0,1},{2,3},{4,5},{6,7},{8,9},{10,11},{12,13},{14,15},{16,17},{18,... | collective-permute-start | bytes 147464 | tf_op jit(solution)/shard_map/ppermute | solution.py:70
  355.8 31.0 %collective-permute-start.4 = (bf16[4,12,256]{2,1,0:T(8,128)(2,1)}, bf16[4,12,256]{2,1,0:T(8,128)(2,1)S(1)}, u32[]{:S(2)}, u32[]{:S(2)}) collective-permute-start(bf16[4,12,256]{2,1,0:T(8,128)(2,1)} %get-tuple-element.179), channel_id=1, source_target_pairs={{0,1},{2,3},{4,5},{6,7},{8,9},{10,11},{12,13},{14,15},{16,17},{18,... | collective-permute-start | bytes 73736 | tf_op jit(solution)/shard_map/ppermute | solution.py:70
  357.1 31.9 %collective-permute-start.5 = (bf16[4,12,256]{2,1,0:T(8,128)(2,1)}, bf16[4,12,256]{2,1,0:T(8,128)(2,1)S(1)}, u32[]{:S(2)}, u32[]{:S(2)}) collective-permute-start(bf16[4,12,256]{2,1,0:T(8,128)(2,1)} %get-tuple-element.180), channel_id=1, source_target_pairs={{1,0},{3,2},{5,4},{7,6},{9,8},{11,10},{13,12},{15,14},{17,16},{19,... | collective-permute-start | bytes 73736 | tf_op jit(solution)/shard_map/ppermute | solution.py:73
  386.7 8.8 collective-permute-start.9
  389.2 19.0 %collective-permute-start.6 = (bf16[4,280,256]{2,1,0:T(8,128)(2,1)S(1)}, bf16[4,280,256]{2,1,0:T(8,128)(2,1)S(1)}, u32[]{:S(2)}, u32[]{:S(2)}) collective-permute-start(bf16[4,280,256]{2,1,0:T(8,128)(2,1)S(1)} %pad_maximum_fusion.9), channel_id=1, source_target_pairs={{6,0},{8,2},{10,4},{12,6},{14,8},{16,10},{18,12},{20,14},{22,16},{... | collective-permute-start | bytes 1720328 | tf_op jit(solution)/shard_map/ppermute | solution.py:81
  391.6 30.9 %collective-permute-start.7 = (bf16[4,280,256]{2,1,0:T(8,128)(2,1)S(1)}, bf16[4,280,256]{2,1,0:T(8,128)(2,1)S(1)}, u32[]{:S(2)}, u32[]{:S(2)}) collective-permute-start(bf16[4,280,256]{2,1,0:T(8,128)(2,1)S(1)} %pad_maximum_fusion.9), channel_id=1, source_target_pairs={{0,6},{2,8},{4,10},{6,12},{8,14},{10,16},{12,18},{14,20},{16,22},{... | collective-permute-start | bytes 1720328 | tf_op jit(solution)/shard_map/ppermute | solution.py:81
  395.6 29.3 %collective-permute-start.10 = (bf16[4,304,256]{2,1,0:T(8,128)(2,1)S(1)}, bf16[4,304,256]{2,1,0:T(8,128)(2,1)S(1)}, u32[]{:S(2)}, u32[]{:S(2)}) collective-permute-start(bf16[4,304,256]{2,1,0:T(8,128)(2,1)S(1)} %pad_maximum_fusion.8), channel_id=1, source_target_pairs={{12,0},{14,2},{16,4},{18,6},{20,8},{22,10},{24,12},{26,14},{28,16}... | collective-permute-start | bytes 1867784 | tf_op jit(solution)/shard_map/ppermute | solution.py:81
  397.7 32.9 %collective-permute-start.11 = (bf16[4,304,256]{2,1,0:T(8,128)(2,1)S(1)}, bf16[4,304,256]{2,1,0:T(8,128)(2,1)S(1)}, u32[]{:S(2)}, u32[]{:S(2)}) collective-permute-start(bf16[4,304,256]{2,1,0:T(8,128)(2,1)S(1)} %pad_maximum_fusion.8), channel_id=1, source_target_pairs={{0,12},{2,14},{4,16},{6,18},{8,20},{10,22},{12,24},{14,26},{16,28}... | collective-permute-start | bytes 1867784 | tf_op jit(solution)/shard_map/ppermute | solution.py:81
  402.9 52.0 %collective-permute-start.14 = (bf16[4,328,256]{2,1,0:T(8,128)(2,1)S(1)}, bf16[4,328,256]{2,1,0:T(8,128)(2,1)S(1)}, u32[]{:S(2)}, u32[]{:S(2)}) collective-permute-start(bf16[4,328,256]{2,1,0:T(8,128)(2,1)S(1)} %pad_maximum_fusion.7), channel_id=1, source_target_pairs={{18,0},{20,2},{22,4},{24,6},{26,8},{28,10},{30,12},{19,1},{21,3},{... | collective-permute-start | bytes 2015240 | tf_op jit(solution)/shard_map/ppermute | solution.py:81
  408.2 47.2 %collective-permute-start.15 = (bf16[4,328,256]{2,1,0:T(8,128)(2,1)S(1)}, bf16[4,328,256]{2,1,0:T(8,128)(2,1)S(1)}, u32[]{:S(2)}, u32[]{:S(2)}) collective-permute-start(bf16[4,328,256]{2,1,0:T(8,128)(2,1)S(1)} %pad_maximum_fusion.7), channel_id=1, source_target_pairs={{0,18},{2,20},{4,22},{6,24},{8,26},{10,28},{12,30},{1,19},{3,21},{... | collective-permute-start | bytes 2015240 | tf_op jit(solution)/shard_map/ppermute | solution.py:81
  430.7 27.4 %slice-start.9 = ((s8[9437184]{0:T(1024)(128)(4,1)}), s8[4194304]{0:T(1024)(128)(4,1)S(1)}, s32[]{:S(2)}) async-start(s8[9437184]{0:T(1024)(128)(4,1)} %bitcast.405), calls=%async_computation.11 | async-start | bytes 8388608
  431.6 23.6 %copy-start.14 = (bf16[4,1024,256]{2,1,0:T(8,128)(2,1)S(1)}, bf16[4,1024,256]{2,1,0:T(8,128)(2,1)}, u32[]{:S(2)}) copy-start(bf16[4,1024,256]{2,1,0:T(8,128)(2,1)} %get-tuple-element.27) | copy-start | bytes 6291460
  485.7 69.2 %copy-start.59 = (f32[2048]{0:T(1024)S(1)}, f32[2048]{0:T(1024)}, u32[]{:S(2)}) copy-start(f32[2048]{0:T(1024)} %get-tuple-element.125) | copy-start | bytes 24580
  590.6 82.4 %collective-permute-start.16 = (bf16[4,4,512]{2,1,0:T(4,128)(2,1)S(1)}, bf16[4,4,512]{2,1,0:T(4,128)(2,1)S(1)}, u32[]{:S(2)}, u32[]{:S(2)}) collective-permute-start(bf16[4,4,512]{2,1,0:T(4,128)(2,1)S(1)} %get-tuple-element.153), channel_id=1, source_target_pairs={{0,1},{2,3},{4,5},{6,7},{8,9},{10,11},{12,13},{14,15},{16,17},{18,... | collective-permute-start | bytes 49160 | tf_op jit(solution)/shard_map/ppermute | solution.py:70
  592.1 80.9 %collective-permute-start.17 = (bf16[4,4,512]{2,1,0:T(4,128)(2,1)S(1)}, bf16[4,4,512]{2,1,0:T(4,128)(2,1)S(1)}, u32[]{:S(2)}, u32[]{:S(2)}) collective-permute-start(bf16[4,4,512]{2,1,0:T(4,128)(2,1)S(1)} %get-tuple-element.154), channel_id=1, source_target_pairs={{1,0},{3,2},{5,4},{7,6},{9,8},{11,10},{13,12},{15,14},{17,16},{19,... | collective-permute-start | bytes 49160 | tf_op jit(solution)/shard_map/ppermute | solution.py:73
  626.2 30.4 %slice-start.12 = ((s8[4718592]{0:T(1024)(128)(4,1)}), s8[4194304]{0:T(1024)(128)(4,1)S(1)}, s32[]{:S(2)}) async-start(s8[4718592]{0:T(1024)(128)(4,1)} %bitcast.420), calls=%async_computation.14 | async-start | bytes 8388608
  673.3 51.1 %collective-permute-start.19 = (bf16[4,264,512]{2,1,0:T(8,128)(2,1)S(1)}, bf16[4,264,512]{2,1,0:T(8,128)(2,1)S(1)}, u32[]{:S(2)}, u32[]{:S(2)}) collective-permute-start(bf16[4,264,512]{2,1,0:T(8,128)(2,1)S(1)} %pad_maximum_fusion.2), channel_id=1, source_target_pairs={{0,2},{2,4},{4,6},{6,8},{8,10},{10,12},{12,14},{14,16},{16,18},{18... | collective-permute-start | bytes 3244040 | tf_op jit(solution)/shard_map/ppermute | solution.py:81
  678.2 47.9 %collective-permute-start.18 = (bf16[4,264,512]{2,1,0:T(8,128)(2,1)S(1)}, bf16[4,264,512]{2,1,0:T(8,128)(2,1)S(1)}, u32[]{:S(2)}, u32[]{:S(2)}) collective-permute-start(bf16[4,264,512]{2,1,0:T(8,128)(2,1)S(1)} %pad_maximum_fusion.2), channel_id=1, source_target_pairs={{2,0},{4,2},{6,4},{8,6},{10,8},{12,10},{14,12},{16,14},{18,16},{20... | collective-permute-start | bytes 3244040 | tf_op jit(solution)/shard_map/ppermute | solution.py:81
  (95 other events, 772.2 us)
Sparse Core Ops, SparseCore 0:
  347.5 171.0 all-reduce.11
  750.1 251.6 all-reduce.13

commit v3 on v2

--- a/solution.py
+++ b/solution.py
@@ -262,6 +262,7 @@
     head_bias,
     factors,
     info,
+    crop_sums,
     branch_low,
     proj_part,
     head_part,
@@ -269,6 +270,7 @@
     crop_pre,
     sums_five,
     sums_four,
+    crop_table,
     field,
     send_main,
     recv_main,
@@ -288,6 +290,7 @@
     five_slots,
     back_five,
     back_four,
+    crop_pieces,
     main_sems,
     side_sems,
     crop_sems,
@@ -295,6 +298,8 @@
     five_sems,
     back_five_sems,
     back_four_sems,
+    piece_sems,
+    table_sems,
 ):
     rows, cols, row, col, me = place()
     low, wide = jnp.bfloat16, jnp.float32
@@ -323,6 +328,21 @@
     pre[0] = jnp.dot(trunk[...], aspp_point[...], preferred_element_type=wide)
     await_all()
     share(crop_slots, crop_sems)
+    crop_pieces[me] = crop_sums[me]
+
+    def scatter(step, carry):
+        other = lax.rem(me + step, rows * cols)
+        pltpu.make_async_remote_copy(
+            crop_sums.at[other],
+            crop_pieces.at[me],
+            piece_sems.at[0],
+            piece_sems.at[1],
+            device_id=(other // cols, lax.rem(other, cols)),
+            device_id_type=MESH,
+        ).start()
+        return carry
+
+    lax.fori_loop(1, rows * cols, scatter, 0)
     side_from = pl.multiple_of((1 - col) * (PAD + width), 16)
     side_to = pl.multiple_of((1 - col) * (width - PAD), 16)
 
@@ -437,6 +457,9 @@
         lines(assemble)
         statistics(lambda span: pre[index + 1, span, :], four_slots, per * (index + 1), 4 * per)
     share(four_slots, four_sems)
+    shared(crop_pieces, piece_sems)
+    crop_table[me] = jnp.sum(crop_pieces[...], axis=0)
+    share(crop_table, table_sems)
     shared(crop_slots, crop_sems)
     crop_total = jnp.sum(crop_slots[...], axis=0)
     crop_value = jnp.concatenate([crop_total[:half], crop_total[half:]], axis=1) / crop_count[...]
@@ -583,6 +606,7 @@
             return carry
 
         lines(branch_back)
+    shared(crop_table, table_sems)
     for index in range(3):
         step = BASE_RATE * (index + 1) // height
         for way in range(3):
@@ -595,7 +619,7 @@
 
 
 def pyramid(height, trunk, depth, sep_point, aspp_point, crop_part, crop_count, members, proj_weight,
-            gains, shifts, head_weight, head_bias, factors, info):
+            gains, shifts, head_weight, head_bias, factors, info, crop_sums):
     devices = lax.axis_size("rows") * lax.axis_size("cols")
     pixels = trunk.shape[0]
     width = pixels // height
@@ -614,12 +638,13 @@
         shape((crops, aspp), wide),
         shape((8, LANES), wide),
         shape((8 * per, LANES), wide),
+        shape(crop_sums.shape, wide),
     )
     sems = pltpu.SemaphoreType.DMA
     return pl.pallas_call(
         functools.partial(pyramid_kernel, height),
         out_shape=outs,
-        in_specs=[whole] * 14,
+        in_specs=[whole] * 15,
         out_specs=(whole,) * len(outs),
         scratch_shapes=[
             pltpu.VMEM((height, width + 2 * PAD, aspp), wide),
@@ -641,8 +666,11 @@
             pltpu.VMEM((devices, 8, LANES), wide),
             pltpu.VMEM((devices, 8, LANES), wide),
             pltpu.VMEM((devices, 8 * per, LANES), wide),
+            pltpu.VMEM(crop_sums.shape, wide),
             sems((2, 3, 3)),
             sems((2, 3, 3)),
+            sems((2,)),
+            sems((2,)),
             sems((2,)),
             sems((2,)),
             sems((2,)),
@@ -652,9 +680,1089 @@
         compiler_params=pltpu.CompilerParams(
             collective_id=10, has_side_effects=True, vmem_limit_bytes=VMEM_BYTES
         ),
+        cost_estimate=pl.CostEstimate(
+            flops=100 * pixels * trunk.shape[1] * aspp, bytes_accessed=64 * pixels * trunk.shape[1], transcendentals=0
+        ),
         name="pyramid",
     )(trunk, depth, sep_point, aspp_point, crop_part, crop_count, members, proj_weight, gains, shifts,
-      head_weight, head_bias, factors, info)
+      head_weight, head_bias, factors, info, crop_sums)
+
+
+def pyramid_weights_kernel(
+    branch_low,
+    trunk,
+    depth,
+    sep_point,
+    crop_local,
+    proj_part,
+    head_part,
+    near,
+    early,
+    crop_total,
+    depth_part,
+    turned,
+    shifted,
+    moved,
+    gathered,
+    crop_slots,
+    main_sems,
+    edge_sems,
+    crop_sems,
+):
+    rows, cols, row, col, me = place()
+    low, wide = jnp.bfloat16, jnp.float32
+    height, width, aspp = branch_low.shape[1:]
+    pixels, channels = trunk.shape
+    half = crop_local.shape[0]
+    greet_all()
+
+    def exists(target):
+        return jnp.logical_and(target >= 0, target < rows)
+
+    def step_of(index):
+        return BASE_RATE * (index + 1) // height
+
+    edge_from = pl.multiple_of((1 - col) * (width - PAD), 16)
+    edge_to = pl.multiple_of(col * (width + PAD), 16)
+    blank = pl.multiple_of(col * (width + PAD), 16)
+
+    def main_copy(index, way):
+        return pltpu.make_async_remote_copy(
+            branch_low.at[index + 1],
+            near.at[index, way, :, pl.ds(PAD, width), :],
+            main_sems.at[0, index, way],
+            main_sems.at[1, index, way],
+            device_id=(row + (1 - way) * step_of(index), col),
+            device_id_type=MESH,
+        )
+
+    def edge_copy(index, way):
+        return pltpu.make_async_remote_copy(
+            branch_low.at[index + 1, :, pl.ds(edge_from, PAD), :],
+            near.at[index, way, :, pl.ds(edge_to, PAD), :],
+            edge_sems.at[0, index, way],
+            edge_sems.at[1, index, way],
+            device_id=(row + (1 - way) * step_of(index), 1 - col),
+            device_id_type=MESH,
+        )
+
+    for index in range(3):
+        for way in range(3):
+            near[index, way, :, pl.ds(blank, PAD), :] = jnp.zeros((height, PAD, aspp), low)
+            if way == 1:
+                near[index, way, :, PAD : PAD + width, :] = branch_low[index + 1]
+            else:
+
+                @pl.when(jnp.logical_not(exists(row - (1 - way) * step_of(index))))
+                def _():
+                    near[index, way] = jnp.zeros(near.shape[2:], low)
+
+    crop_slots[me, :half, :] = crop_local[:, :LANES]
+    crop_slots[me, half:, :] = crop_local[:, LANES:]
+    await_all()
+    for index in range(3):
+        edge_copy(index, 1).start()
+    for index in range(3):
+        for way in (0, 2):
+
+            @pl.when(exists(row + (1 - way) * step_of(index)))
+            def _():
+                main_copy(index, way).start()
+                edge_copy(index, way).start()
+
+    share(crop_slots, crop_sems)
+
+    def turn(block, carry):
+        span = pl.ds(pl.multiple_of(block * width, width), width)
+        for line in range(height):
+            turned[span, line * width : (line + 1) * width] = trunk[
+                line * width : (line + 1) * width, span
+            ].T
+        return carry
+
+    lax.fori_loop(0, channels // width, turn, 0)
+    part_rows = channels // 2
+
+    def point(part, carry):
+        span = pl.ds(pl.multiple_of(part * part_rows, part_rows), part_rows)
+        own = branch_low[0].reshape(pixels, aspp)
+        early[pl.ds(pl.multiple_of(channels + part * part_rows, part_rows), part_rows), aspp:] = jnp.dot(
+            turned[span, :], own, preferred_element_type=wide
+        ).astype(low)
+        return carry
+
+    lax.fori_loop(0, 2, point, 0)
+    lane = lax.broadcasted_iota(jnp.int32, (part_rows, LANES), 1)
+    depth_part[...] = jnp.zeros(depth_part.shape, wide)
+    gathered[...] = jnp.zeros(gathered.shape, wide)
+    for index, way in ((0, 1), (1, 1), (2, 1), (0, 0), (0, 2), (1, 0), (1, 2), (2, 0), (2, 2)):
+        rate = BASE_RATE * (index + 1)
+
+        @pl.when(exists(row - (1 - way) * step_of(index)))
+        def _():
+            if way != 1:
+                main_copy(index, way).wait_recv()
+            edge_copy(index, way).wait_recv()
+
+        shifted[...] = near[index, way].astype(wide)
+        for side in range(3):
+            tap = 3 * (2 - way) + side
+            at = PAD - (side - 1) * rate
+            for line in range(height):
+                moved[line * width : (line + 1) * width, :] = shifted[line, at : at + width, :].astype(
+                    low
+                )
+            order = 9 * index + tap
+
+            def collect(part, carry):
+                span = pl.ds(pl.multiple_of(part * part_rows, part_rows), part_rows)
+                made = jnp.dot(turned[span, :], moved[...], preferred_element_type=wide)
+                gathered[index, span, :] += made * depth[span, order : order + 1]
+                total = jnp.sum(made * sep_point[index, span, :].astype(wide), axis=1, keepdims=True)
+                depth_part[span, :] = jnp.where(lane == order, total, depth_part[span, :])
+                return carry
+
+            lax.fori_loop(0, 2, collect, 0)
+    early[:channels, :aspp] = gathered[0].astype(low)
+    early[:channels, aspp:] = gathered[1].astype(low)
+    early[channels : 2 * channels, :aspp] = gathered[2].astype(low)
+    at = 2 * channels
+    for table in (proj_part, depth_part, head_part):
+        extent = table.shape[1]
+        blocks = 2 * aspp // extent
+        size = table.shape[0] // blocks
+        for block in range(blocks):
+            early[at : at + size, block * extent : (block + 1) * extent] = table[
+                block * size : (block + 1) * size, :
+            ].astype(low)
+        at += size
+    if early.shape[0] > at:
+        early[at:, :] = jnp.zeros((early.shape[0] - at, 2 * aspp), low)
+    shared(crop_slots, crop_sems)
+    total = jnp.sum(crop_slots[...], axis=0)
+    crop_total[...] = jnp.concatenate([total[:half], total[half:]], axis=1)
+    for index in range(3):
+        for way in range(3):
+
+            @pl.when(exists(row + (1 - way) * step_of(index)))
+            def _():
+                if way != 1:
+                    main_copy(index, way).wait_send()
+                edge_copy(index, way).wait_send()
+
+
+def early_rows(channels, proj_part, head_part):
+    rows = 2 * channels
+    for size, extent in ((proj_part.shape[0], proj_part.shape[1]), (channels, LANES), head_part.shape):
+        rows += size * extent // (2 * proj_part.shape[1])
+    return rows
+
+
+def pyramid_weights(branch_low, trunk, depth, sep_point, crop_local, proj_part, head_part):
+    devices = lax.axis_size("rows") * lax.axis_size("cols")
+    height, width, aspp = branch_low.shape[1:]
+    pixels, channels = trunk.shape
+    crops = crop_local.shape[0]
+    low, wide = jnp.bfloat16, jnp.float32
+    shape = jax.ShapeDtypeStruct
+    whole = pl.BlockSpec(memory_space=pltpu.VMEM)
+    sems = pltpu.SemaphoreType.DMA
+    outs = (
+        shape((3, 3, height, width + 2 * PAD, aspp), low),
+        shape((sum_rows(early_rows(channels, proj_part, head_part)), 2 * aspp), low),
+        shape((crops, aspp), wide),
+    )
+    return pl.pallas_call(
+        pyramid_weights_kernel,
+        out_shape=outs,
+        in_specs=[whole] * 7,
+        out_specs=(whole,) * len(outs),
+        scratch_shapes=[
+            pltpu.VMEM((channels, LANES), wide),
+            pltpu.VMEM((channels, pixels), low),
+            pltpu.VMEM((height, width + 2 * PAD, aspp), wide),
+            pltpu.VMEM((pixels, aspp), low),
+            pltpu.VMEM((3, channels, aspp), wide),
+            pltpu.VMEM((devices, 2 * crops, LANES), wide),
+            sems((2, 3, 3)),
+            sems((2, 3, 3)),
+            sems((2,)),
+        ],
+        compiler_params=pltpu.CompilerParams(
+            collective_id=11, has_side_effects=True, vmem_limit_bytes=VMEM_BYTES
+        ),
+        cost_estimate=pl.CostEstimate(
+            flops=100 * pixels * channels * aspp, bytes_accessed=64 * pixels * channels, transcendentals=0
+        ),
+        name="pyramid_weights",
+    )(branch_low, trunk, depth, sep_point, crop_local, proj_part, head_part)
+
+
+def share_rows(slots, at, size, sems):
+    rows, cols, row, col, me = place()
+
+    def go(step, carry):
+        other = lax.rem(me + step, rows * cols)
+        mine = slots.at[me, pl.ds(at, size), :]
+        pltpu.make_async_remote_copy(
+            mine,
+            mine,
+            sems.at[0],
+            sems.at[1],
+            device_id=(other // cols, lax.rem(other, cols)),
+            device_id_type=MESH,
+        ).start()
+        return carry
+
+    lax.fori_loop(1, rows * cols, go, 0)
+
+
+def shared_rows(slots, at, size, sems):
+    rows, cols, row, col, me = place()
+    others = slots.at[pl.ds(0, rows * cols - 1), pl.ds(at, size), :]
+    pltpu.make_async_remote_copy(
+        others,
+        others,
+        sems.at[0],
+        sems.at[1],
+        device_id=(row, lax.rem(col + 1, cols)),
+        device_id_type=MESH,
+    ).wait()
+
+
+def trunk_back_kernel(
+    near,
+    own_low,
+    depth,
+    sep_point,
+    aspp_point,
+    members,
+    crop_high,
+    crop_rest,
+    expanded,
+    features,
+    three,
+    dilated,
+    two,
+    second_act,
+    expand_weight,
+    early,
+    pre_grad,
+    expand_part,
+    dilated_low,
+    sums_three,
+    sums_two,
+    early_out,
+    fetched,
+    chunk_in,
+    shifted,
+    moved,
+    maps,
+    grown,
+    expand_low,
+    slots_three,
+    slots_two,
+    sems_three,
+    sems_two,
+    fetch_sems,
+    chunk_sems,
+    early_own,
+    *early_refs,
+):
+    rows, cols, row, col, me = place()
+    low, wide = jnp.bfloat16, jnp.float32
+    height = near.shape[2]
+    early_sum = Sum(early, early_own, early_out, *early_refs)
+    aspp = sep_point.shape[2]
+    pixels, channels = expanded.shape
+    middle = dilated.shape[1]
+    width = pixels // height
+    count = float(pixels * rows * cols)
+    per = aspp // LANES
+    chunks = channels // aspp
+    greet_all()
+
+    def fetch(number):
+        return pltpu.make_async_copy(
+            near.at[number // 3, number % 3], fetched.at[number % 2], fetch_sems.at[number % 2]
+        )
+
+    fetch(0).start()
+    own_half = pltpu.make_async_copy(
+        early.at[early_sum.half_span(col)], early_own, early_refs[-1]
+    )
+    own_half.start()
+
+    def chunk_of(block):
+        return pl.ds(pl.multiple_of(block * aspp, aspp), aspp)
+
+    def own(block, carry):
+        span = chunk_of(block)
+        grown[:, span] = (
+            across(own_low[...], aspp_point[span, :])
+            + jnp.dot(members[...], crop_high[:, span], preferred_element_type=wide)
+            + jnp.dot(members[...], crop_rest[:, span], preferred_element_type=wide)
+        )
+        return carry
+
+    lax.fori_loop(0, chunks, own, 0)
+    await_all()
+    own_half.wait()
+    early_sum.start_halves()
+
+    def fetch_chunk(block):
+        slot = lax.rem(block, 2)
+        return pltpu.make_async_copy(
+            expanded.at[:, chunk_of(block)], chunk_in.at[slot], chunk_sems.at[slot]
+        )
+
+    def advance(block):
+        @pl.when(block + 1 < chunks)
+        def _():
+            fetch_chunk(block + 1).start()
+
+        fetch_chunk(block).wait()
+
+    def back(block, line, span):
+        rows_span = slice(line * width, (line + 1) * width)
+        value = chunk_in[lax.rem(block, 2), rows_span, :]
+        normed = (value - three[0:1, span]) * three[1:2, span]
+        return rows_span, normed
+
+    for index in range(3):
+        rate = BASE_RATE * (index + 1)
+        for way in range(3):
+            number = 3 * index + way
+            if number < 8:
+                fetch(number + 1).start()
+            fetch(number).wait()
+            shifted[...] = fetched[number % 2].astype(wide)
+            for side in range(3):
+                tap = 3 * (2 - way) + side
+                at = PAD - (side - 1) * rate
+                for line in range(height):
+                    moved[line * width : (line + 1) * width, tap * aspp : (tap + 1) * aspp] = shifted[
+                        line, at : at + width, :
+                    ].astype(low)
+
+        def one_chunk(block, carry):
+            span = chunk_of(block)
+            rows_of = sep_point[index, span, :].astype(wide)
+            for tap in range(9):
+                order = 9 * index + tap
+                maps[:, tap * aspp : (tap + 1) * aspp] = (
+                    rows_of * depth[span, order : order + 1]
+                ).astype(low)
+            total = grown[:, span] + across(moved[...], maps[...])
+            if index < 2:
+                grown[:, span] = total
+                return carry
+            advance(block)
+            shift_sum, gain_sum = jnp.zeros((1, aspp), wide), jnp.zeros((1, aspp), wide)
+            for line in range(height):
+                rows_span, normed = back(block, line, span)
+                gated = (
+                    normed * three[2:3, span]
+                    + three[3:4, span]
+                    + features[rows_span, span].astype(wide)
+                )
+                sigma = sigmoid(gated)
+                up = total[rows_span, :] * (sigma * (1.0 + gated * (1.0 - sigma)))
+                grown[rows_span, span] = up
+                pre_grad[rows_span, span] = up.astype(low)
+                shift_sum = shift_sum + jnp.sum(up, axis=0, keepdims=True)
+                gain_sum = gain_sum + jnp.sum(up * normed, axis=0, keepdims=True)
+            for part in range(per):
+                lanes = slice(part * LANES, (part + 1) * LANES)
+                slots_three[me, pl.ds(block * 2 * per + part, 1), :] = shift_sum[:, lanes]
+                slots_three[me, pl.ds(block * 2 * per + per + part, 1), :] = gain_sum[:, lanes]
+            pair = block // 2
+
+            @pl.when(lax.rem(block, 2) == 1)
+            def _():
+                share_rows(slots_three, pl.multiple_of(pair * 4 * per, 8), 4 * per, sems_three.at[pair])
+
+            return carry
+
+        if index == 0:
+            early_sum.start_quarters()
+        if index == 2:
+            fetch_chunk(0).start()
+        lax.fori_loop(0, chunks, one_chunk, 0)
+        if index == 1:
+            early_sum.start_parts()
+
+    def finish(block, carry):
+        span = chunk_of(block)
+        pair = block // 2
+        at = pl.multiple_of(pair * 4 * per, 8)
+
+        @pl.when(lax.rem(block, 2) == 0)
+        def _():
+            shared_rows(slots_three, at, 4 * per, sems_three.at[pair])
+            sums_three[pl.ds(at, 4 * per), :] = jnp.sum(slots_three[:, pl.ds(at, 4 * per), :], axis=0)
+
+        advance(block)
+
+        def row_at(start):
+            first = block * 2 * per + start
+            return jnp.concatenate([sums_three[pl.ds(first + part, 1), :] for part in range(per)], axis=1)
+
+        shift_mean = row_at(0) / count
+        gain_mean = row_at(per) / count
+        factor = three[2:3, span] * three[1:2, span]
+        for line in range(height):
+            rows_span, normed = back(block, line, span)
+            inner = grown[rows_span, span] - shift_mean - normed * gain_mean
+            expand_low[rows_span, span] = (inner * factor).astype(low)
+        return carry
+
+    early_sum.start_back_parts()
+    fetch_chunk(0).start()
+    lax.fori_loop(0, chunks, finish, 0)
+    early_sum.start_back_quarters()
+    grown_two = across(expand_low[...], expand_weight[...])
+    shift_sum, gain_sum = jnp.zeros((1, middle), wide), jnp.zeros((1, middle), wide)
+    for line in range(height):
+        rows_span = slice(line * width, (line + 1) * width)
+        normed = (dilated[rows_span, :] - two[0:1, :]) * two[1:2, :]
+        gated = normed * two[2:3, :] + two[3:4, :]
+        sigma = sigmoid(gated)
+        up = grown_two[rows_span, :] * (sigma * (1.0 + gated * (1.0 - sigma)))
+        grown[rows_span, :middle] = up
+        shift_sum = shift_sum + jnp.sum(up, axis=0, keepdims=True)
+        gain_sum = gain_sum + jnp.sum(up * normed, axis=0, keepdims=True)
+    per_two = middle // LANES
+    put_row(slots_two, me, 0, shift_sum)
+    put_row(slots_two, me, per_two, gain_sum)
+    share(slots_two, sems_two)
+    for block in range(channels // middle):
+        span = slice(block * middle, (block + 1) * middle)
+        expand_part[block * middle : (block + 1) * middle, :] = down(
+            second_act[...], expand_low[:, span]
+        ).astype(low)
+    shared(slots_two, sems_two)
+    total = jnp.sum(slots_two[...], axis=0)
+    sums_two[...] = total
+    shift_mean = take_row(total, 0, middle) / count
+    gain_mean = take_row(total, per_two, middle) / count
+    factor = two[2:3, :] * two[1:2, :]
+    for line in range(height):
+        rows_span = slice(line * width, (line + 1) * width)
+        normed = (dilated[rows_span, :] - two[0:1, :]) * two[1:2, :]
+        inner = grown[rows_span, :middle] - shift_mean - normed * gain_mean
+        dilated_low[rows_span, :] = (inner * factor).astype(low)
+    early_sum.start_back_half()
+    early_sum.finish()
+
+
+def trunk_back(near, own_low, depth, sep_point, aspp_point, members, crop_high, crop_rest, expanded,
+               features, three, dilated, two, second_act, expand_weight, early):
+    devices = lax.axis_size("rows") * lax.axis_size("cols")
+    height, extent, aspp = near.shape[2:]
+    pixels, channels = expanded.shape
+    middle = dilated.shape[1]
+    chunks = channels // aspp
+    low, wide = jnp.bfloat16, jnp.float32
+    shape = jax.ShapeDtypeStruct
+    whole = pl.BlockSpec(memory_space=pltpu.VMEM)
+    away = pl.BlockSpec(memory_space=pl.ANY)
+    sems = pltpu.SemaphoreType.DMA
+    per_two = middle // LANES
+    outs = (
+        shape((pixels, channels), low),
+        shape((channels, middle), low),
+        shape((pixels, middle), low),
+        shape((chunks * 2 * (aspp // LANES), LANES), wide),
+        shape((2 * per_two, LANES), wide),
+        shape(early.shape, low),
+    )
+    return pl.pallas_call(
+        trunk_back_kernel,
+        out_shape=outs,
+        in_specs=[away] + [whole] * 7 + [away] + [whole] * 6 + [away],
+        out_specs=(whole,) * 5 + (away,),
+        scratch_shapes=[
+            pltpu.VMEM((2, height, extent, aspp), low),
+            pltpu.VMEM((2, pixels, aspp), wide),
+            pltpu.VMEM((height, extent, aspp), wide),
+            pltpu.VMEM((pixels, 9 * aspp), low),
+            pltpu.VMEM((aspp, 9 * aspp), low),
+            pltpu.VMEM((pixels, channels), wide),
+            pltpu.VMEM((pixels, channels), low),
+            pltpu.VMEM((devices, chunks * 2 * (aspp // LANES), LANES), wide),
+            pltpu.VMEM((devices, 2 * per_two, LANES), wide),
+            sems((chunks // 2, 2)),
+            sems((2,)),
+            sems((2,)),
+            sems((2,)),
+            pltpu.VMEM((early.shape[0] // 2, early.shape[1]), low),
+            *sum_scratch(*early.shape),
+        ],
+        compiler_params=pltpu.CompilerParams(
+            collective_id=12, has_side_effects=True, vmem_limit_bytes=VMEM_BYTES + (3 << 20)
+        ),
+        cost_estimate=pl.CostEstimate(
+            flops=80 * pixels * channels * aspp, bytes_accessed=64 * pixels * channels, transcendentals=0
+        ),
+        name="trunk_back",
+    )(near, own_low, depth, sep_point, aspp_point, members, crop_high, crop_rest, expanded, features,
+      three, dilated, two, second_act, expand_weight, early)
+
+
+EDGE = 16
+
+
+class Halo:
+    def __init__(self, near, direct, relay, edge):
+        self.near, self.direct, self.relay, self.edge = near, direct, relay, edge
+        self.rows, self.cols, self.row, self.col, _ = place()
+        self.height, self.width = near.shape[1], near.shape[2] - 2 * EDGE
+        self.odd = lax.rem(self.row, 2)
+        self.pair = self.row + 1 - 2 * self.odd
+        self.onward = self.row + 2 - 4 * self.odd
+        self.far = self.row - 1 + 2 * self.odd
+        self.pair_way = 2 - 2 * self.odd
+        self.far_way = 2 * self.odd
+
+    def exists(self, target):
+        return jnp.logical_and(target >= 0, target < self.rows)
+
+    def line_ref(self, way, line):
+        return self.near.at[way, line, pl.ds(EDGE, self.width), :]
+
+    def direct_copy(self, line):
+        return pltpu.make_async_remote_copy(
+            self.line_ref(1, line),
+            self.line_ref(self.far_way, line),
+            self.direct.at[0, line],
+            self.direct.at[1, line],
+            device_id=(self.pair, self.col),
+            device_id_type=MESH,
+        )
+
+    def relay_copy(self, line):
+        return pltpu.make_async_remote_copy(
+            self.line_ref(self.pair_way, line),
+            self.line_ref(self.far_way, line),
+            self.relay.at[0, line],
+            self.relay.at[1, line],
+            device_id=(self.onward, self.col),
+            device_id_type=MESH,
+        )
+
+    def edge_copy(self, way):
+        start = pl.multiple_of(EDGE + (1 - self.col) * (self.width - EDGE), 16)
+        end = pl.multiple_of(self.col * (self.width + EDGE), 16)
+        return pltpu.make_async_remote_copy(
+            self.near.at[1, :, pl.ds(start, EDGE), :],
+            self.near.at[way, :, pl.ds(end, EDGE), :],
+            self.edge.at[0, way],
+            self.edge.at[1, way],
+            device_id=(self.row + 1 - way, 1 - self.col),
+            device_id_type=MESH,
+        )
+
+    def clear(self):
+        near = self.near
+        blank = pl.multiple_of(self.col * (self.width + EDGE), 16)
+        for way in range(3):
+            near[way, :, pl.ds(blank, EDGE), :] = jnp.zeros(
+                (self.height, EDGE, near.shape[3]), near.dtype
+            )
+
+        @pl.when(jnp.logical_not(self.exists(self.far)))
+        def _():
+            near[self.far_way] = jnp.zeros(near.shape[1:], near.dtype)
+
+    def start(self):
+        self.edge_copy(1).start()
+        for line in range(self.height):
+            self.direct_copy(line).start()
+        for way in (0, 2):
+
+            @pl.when(self.exists(self.row + 1 - way))
+            def _():
+                self.edge_copy(way).start()
+
+    def wait_own(self):
+        self.edge_copy(1).wait_recv()
+
+    def pass_on(self):
+        for line in range(self.height):
+            self.direct_copy(line).wait_recv()
+
+            @pl.when(self.exists(self.onward))
+            def _():
+                self.relay_copy(line).start()
+
+    def wait_rest(self):
+        for way in (0, 2):
+
+            @pl.when(self.exists(self.row - 1 + way))
+            def _():
+                self.edge_copy(way).wait_recv()
+
+        @pl.when(self.exists(self.far))
+        def _():
+            for line in range(self.height):
+                self.relay_copy(line).wait_recv()
+
+    def drain(self):
+        self.edge_copy(1).wait_send()
+        for line in range(self.height):
+            self.direct_copy(line).wait_send()
+        for way in (0, 2):
+
+            @pl.when(self.exists(self.row + 1 - way))
+            def _():
+                self.edge_copy(way).wait_send()
+
+        @pl.when(self.exists(self.onward))
+        def _():
+            for line in range(self.height):
+                self.relay_copy(line).wait_send()
+
+
+PLANE = 4
+
+
+class Sum:
+    def __init__(self, full, own, out, half_in, quarter_in, part_in, half_sem, quarter_sem, part_sem, copy_sem):
+        self.full, self.out = full, out
+        self.half_in, self.quarter_in, self.part_in = half_in, quarter_in, part_in
+        self.half_sem, self.quarter_sem, self.part_sem = half_sem, quarter_sem, part_sem
+        self.copy_sem = copy_sem
+        self.rows, self.cols, self.row, self.col, _ = place()
+        self.parts = self.rows // PLANE
+        self.quarter, self.part = lax.rem(self.row, PLANE), self.row // PLANE
+        total = full.shape[0]
+        self.half_rows, self.quarter_rows = total // 2, total // 8
+        self.part_rows = self.quarter_rows // self.parts
+        self.data = full.at[self.half_span(self.col)] if own is None else own
+
+    def span(self, start, size):
+        return pl.ds(pl.multiple_of(start, 16), size)
+
+    def half_span(self, col):
+        return self.span(col * self.half_rows, self.half_rows)
+
+    def quarter_span(self, quarter):
+        return self.span(quarter * self.quarter_rows, self.quarter_rows)
+
+    def part_span(self, part):
+        return self.span(
+            self.quarter * self.quarter_rows + part * self.part_rows, self.part_rows
+        )
+
+    def out_at(self, span):
+        return self.out.at[self.span(self.col * self.half_rows + span.start, span.size)]
+
+    def plane_mate(self, step):
+        mate = lax.rem(self.quarter + step, PLANE)
+        return mate, (self.part * PLANE + mate, self.col)
+
+    def part_mate(self, step):
+        mate = lax.rem(self.part + step, self.parts)
+        return mate, (mate * PLANE + self.quarter, self.col)
+
+    def remote(self, src, dst, sems, out_at, in_at, target):
+        return pltpu.make_async_remote_copy(
+            src, dst, sems.at[0, out_at], sems.at[1, in_at], device_id=target, device_id_type=MESH
+        )
+
+    def half_copy(self):
+        return self.remote(
+            self.full.at[self.half_span(1 - self.col)],
+            self.half_in,
+            self.half_sem,
+            0,
+            0,
+            (self.row, 1 - self.col),
+        )
+
+    def quarter_copy(self, step):
+        mate, target = self.plane_mate(step)
+        return self.remote(
+            self.data.at[self.quarter_span(mate)],
+            self.quarter_in.at[self.quarter],
+            self.quarter_sem,
+            mate,
+            self.quarter,
+            target,
+        )
+
+    def quarter_arrival(self, step):
+        mate, target = self.plane_mate(step)
+        return self.remote(
+            self.quarter_in.at[mate], self.quarter_in.at[mate], self.quarter_sem, mate, mate, target
+        )
+
+    def part_copy(self, step):
+        mate, target = self.part_mate(step)
+        return self.remote(
+            self.data.at[self.part_span(mate)],
+            self.part_in.at[self.part],
+            self.part_sem,
+            mate,
+            self.part,
+            target,
+        )
+
+    def part_arrival(self, step):
+        mate, target = self.part_mate(step)
+        return self.remote(
+            self.part_in.at[mate], self.part_in.at[mate], self.part_sem, mate, mate, target
+        )
+
+    def start_halves(self):
+        self.half_copy().start()
+
+    def add(self, span, sources):
+        block = 64
+        base = span.start
+
+        def some(at, carry):
+            rows = pl.ds(pl.multiple_of(base + at * block, 16), block)
+            total = self.data[rows, :].astype(jnp.float32)
+            for source in sources:
+                total = total + source(pl.ds(pl.multiple_of(at * block, 16), block)).astype(jnp.float32)
+            self.data[rows, :] = total.astype(self.data.dtype)
+            return carry
+
+        full = span.size // block
+        lax.fori_loop(0, full, some, 0)
+        rest = span.size - full * block
+        if rest:
+            rows = pl.ds(pl.multiple_of(base + full * block, 16), rest)
+            total = self.data[rows, :].astype(jnp.float32)
+            for source in sources:
+                total = total + source(pl.ds(full * block, rest)).astype(jnp.float32)
+            self.data[rows, :] = total.astype(self.data.dtype)
+
+    def start_quarters(self):
+        self.half_copy().wait()
+        self.add(self.span(0, self.half_rows), [lambda rows: self.half_in[rows, :]])
+        for step in range(1, PLANE):
+            self.quarter_copy(step).start()
+
+    def start_parts(self):
+        for step in range(1, PLANE):
+            self.quarter_copy(step).wait_send()
+            self.quarter_arrival(step).wait_recv()
+        mates = [self.plane_mate(step)[0] for step in range(1, PLANE)]
+        self.add(
+            self.quarter_span(self.quarter),
+            [lambda rows, mate=mate: self.quarter_in[mate, rows, :] for mate in mates],
+        )
+        for step in range(1, self.parts):
+            self.part_copy(step).start()
+
+    def back_part(self, step):
+        mate, target = self.part_mate(step)
+        mine = self.out_at(self.part_span(self.part))
+        apart = self.parts
+        return self.remote(
+            mine, mine, self.part_sem, apart + mate, apart + self.part, target
+        )
+
+    def back_part_arrival(self, step):
+        mate, target = self.part_mate(step)
+        theirs = self.out_at(self.part_span(mate))
+        apart = self.parts
+        return self.remote(theirs, theirs, self.part_sem, apart + mate, apart + mate, target)
+
+    def back_quarter(self, step):
+        mate, target = self.plane_mate(step)
+        mine = self.out_at(self.quarter_span(self.quarter))
+        return self.remote(
+            mine, mine, self.quarter_sem, PLANE + mate, PLANE + self.quarter, target
+        )
+
+    def back_quarter_arrival(self, step):
+        mate, target = self.plane_mate(step)
+        theirs = self.out_at(self.quarter_span(mate))
+        return self.remote(theirs, theirs, self.quarter_sem, PLANE + mate, PLANE + mate, target)
+
+    def back_half(self):
+        mine = self.out.at[self.half_span(self.col)]
+        return self.remote(mine, mine, self.half_sem, 1, 1, (self.row, 1 - self.col))
+
+    def back_half_arrival(self):
+        theirs = self.out.at[self.half_span(1 - self.col)]
+        return self.remote(theirs, theirs, self.half_sem, 1, 1, (self.row, 1 - self.col))
+
+    def start_back_parts(self):
+        for step in range(1, self.parts):
+            self.part_copy(step).wait_send()
+            self.part_arrival(step).wait_recv()
+        mates = [self.part_mate(step)[0] for step in range(1, self.parts)]
+        span = self.part_span(self.part)
+        self.add(span, [lambda rows, mate=mate: self.part_in[mate, rows, :] for mate in mates])
+        copy = pltpu.make_async_copy(self.data.at[span], self.out_at(span), self.copy_sem)
+        copy.start()
+        copy.wait()
+        for step in range(1, self.parts):
+            self.back_part(step).start()
+
+    def start_back_quarters(self):
+        for step in range(1, self.parts):
+            self.back_part(step).wait_send()
+            self.back_part_arrival(step).wait_recv()
+        for step in range(1, PLANE):
+            self.back_quarter(step).start()
+
+    def start_back_half(self):
+        for step in range(1, PLANE):
+            self.back_quarter(step).wait_send()
+            self.back_quarter_arrival(step).wait_recv()
+        self.back_half().start()
+
+    def finish(self):
+        self.back_half().wait_send()
+        self.back_half_arrival().wait_recv()
+
+
+def sum_scratch(total, lanes):
+    parts = lax.axis_size("rows") // PLANE
+    low, sems = jnp.bfloat16, pltpu.SemaphoreType.DMA
+    return [
+        pltpu.VMEM((total // 2, lanes), low),
+        pltpu.VMEM((PLANE, total // 8, lanes), low),
+        pltpu.VMEM((parts, total // 8 // parts, lanes), low),
+        sems((2, 2)),
+        sems((2, 2 * PLANE)),
+        sems((2, 2 * parts)),
+        sems,
+    ]
+
+
+def sum_rows(rows):
+    unit = 2 * lax.axis_size("rows") * 16
+    return -(-rows // unit) * unit
+
+
+def tail_kernel(
+    dilated_low,
+    first_act,
+    dilated_weight,
+    reduced,
+    one,
+    features,
+    reduce_weight,
+    pre_grad,
+    expand_part,
+    features_grad,
+    expand_out,
+    dilated_out,
+    reduce_out,
+    sums_one,
+    near,
+    shifted,
+    moved,
+    act_turned,
+    features_turned,
+    first_grad,
+    reduced_low,
+    expand_own,
+    dilated_data,
+    reduce_data,
+    slots,
+    direct,
+    relay,
+    edge,
+    sems_one,
+    *sum_refs,
+):
+    rows, cols, row, col, me = place()
+    low, wide = jnp.bfloat16, jnp.float32
+    height = near.shape[1]
+    pixels, middle = dilated_low.shape
+    channels = features.shape[1]
+    width = pixels // height
+    count = float(pixels * rows * cols)
+    half = len(sum_refs) // 3
+    sums = [
+        Sum(full, own, out, *refs)
+        for full, own, out, refs in (
+            (expand_part, expand_own, expand_out, sum_refs[:half]),
+            (dilated_data, None, dilated_out, sum_refs[half : 2 * half]),
+            (reduce_data, None, reduce_out, sum_refs[2 * half :]),
+        )
+    ]
+    expand_sum, dilated_sum, reduce_sum = sums
+    halo = Halo(near, direct, relay, edge)
+    greet_all()
+    own_half = pltpu.make_async_copy(
+        expand_part.at[expand_sum.half_span(col)], expand_own, sum_refs[half - 1]
+    )
+    own_half.start()
+    halo.clear()
+    for line in range(height):
+        near[1, line, EDGE : EDGE + width, :] = dilated_low[line * width : (line + 1) * width, :]
+    for data, used in ((dilated_data, 9 * middle), (reduce_data, channels)):
+        if data.shape[0] > used:
+            data[used:, :] = jnp.zeros((data.shape[0] - used, data.shape[1]), low)
+    own_half.wait()
+    await_all()
+    halo.start()
+    expand_sum.start_halves()
+
+    def turn_features(block, carry):
+        span = pl.ds(pl.multiple_of(block * width, width), width)
+        for line in range(height):
+            features_turned[span, line * width : (line + 1) * width] = features[
+                line * width : (line + 1) * width, span
+            ].T
+        return carry
+
+    def turn_act(block, carry):
+        span = pl.ds(pl.multiple_of(block * width, width), width)
+        for line in range(height):
+            act_turned[span, line * width : (line + 1) * width] = first_act[
+                line * width : (line + 1) * width, span
+            ].T
+        return carry
+
+    lax.fori_loop(0, middle // width, turn_act, 0)
+
+    def one_way(way):
+        shifted[...] = near[way].astype(wide)
+        for side in range(3):
+            tap = 3 * (2 - way) + side
+            at = EDGE - (side - 1) * MID_RATE
+            for line in range(height):
+                moved[line * width : (line + 1) * width, :] = shifted[line, at : at + width, :].astype(
+                    low
+                )
+            made = across(moved[...], dilated_weight[tap])
+            if way == 1 and side == 0:
+                first_grad[...] = made
+            else:
+                first_grad[...] += made
+            dilated_data[tap * middle : (tap + 1) * middle, :] = jnp.dot(
+                act_turned[...], moved[...], preferred_element_type=wide
+            ).astype(low)
+
+    halo.wait_own()
+    one_way(1)
+    halo.pass_on()
+    expand_sum.start_quarters()
+    lax.fori_loop(0, channels // width, turn_features, 0)
+    halo.wait_rest()
+    one_way(0)
+    one_way(2)
+    dilated_sum.start_halves()
+    expand_sum.start_parts()
+    shift_sum, gain_sum = jnp.zeros((1, middle), wide), jnp.zeros((1, middle), wide)
+    for line in range(height):
+        span = slice(line * width, (line + 1) * width)
+        normed = (reduced[span, :] - one[0:1, :]) * one[1:2, :]
+        gated = normed * one[2:3, :] + one[3:4, :]
+        sigma = sigmoid(gated)
+        up = first_grad[span, :] * (sigma * (1.0 + gated * (1.0 - sigma)))
+        first_grad[span, :] = up
+        shift_sum = shift_sum + jnp.sum(up, axis=0, keepdims=True)
+        gain_sum = gain_sum + jnp.sum(up * normed, axis=0, keepdims=True)
+    per = middle // LANES
+    put_row(slots, me, 0, shift_sum)
+    put_row(slots, me, per, gain_sum)
+    share(slots, sems_one)
+    expand_sum.start_back_parts()
+    dilated_sum.start_quarters()
+    shared(slots, sems_one)
+    total = jnp.sum(slots[...], axis=0)
+    sums_one[...] = total
+    shift_mean = take_row(total, 0, middle) / count
+    gain_mean = take_row(total, per, middle) / count
+    factor = one[2:3, :] * one[1:2, :]
+    for line in range(height):
+        span = slice(line * width, (line + 1) * width)
+        normed = (reduced[span, :] - one[0:1, :]) * one[1:2, :]
+        inner = first_grad[span, :] - shift_mean - normed * gain_mean
+        reduced_low[span, :] = (inner * factor).astype(low)
+    reduce_data[:channels, :] = jnp.dot(
+        features_turned[...], reduced_low[...], preferred_element_type=wide
+    ).astype(low)
+    reduce_sum.start_halves()
+    expand_sum.start_back_quarters()
+    chunk = 2 * LANES
+
+    def last(block, carry):
+        span = pl.ds(pl.multiple_of(block * chunk, chunk), chunk)
+        made = across(reduced_low[...], reduce_weight[span, :])
+        features_grad[:, span] = (made + pre_grad[:, span].astype(wide)).astype(low)
+        return carry
+
+    lax.fori_loop(0, channels // chunk, last, 0)
+    reduce_sum.start_quarters()
+    dilated_sum.start_parts()
+    expand_sum.start_back_half()
+    reduce_sum.start_parts()
+    dilated_sum.start_back_parts()
+    reduce_sum.start_back_parts()
+    dilated_sum.start_back_quarters()
+    reduce_sum.start_back_quarters()
+    dilated_sum.start_back_half()
+    reduce_sum.start_back_half()
+    for each in sums:
+        each.finish()
+    halo.drain()
+
+
+def tail(height, dilated_low, first_act, dilated_weight, reduced, one, features, reduce_weight, pre_grad,
+         expand_part):
+    devices = lax.axis_size("rows") * lax.axis_size("cols")
+    pixels, middle = dilated_low.shape
+    channels = features.shape[1]
+    width = pixels // height
+    low, wide = jnp.bfloat16, jnp.float32
+    shape = jax.ShapeDtypeStruct
+    whole = pl.BlockSpec(memory_space=pltpu.VMEM)
+    away = pl.BlockSpec(memory_space=pl.ANY)
+    sems = pltpu.SemaphoreType.DMA
+    per = middle // LANES
+    expand_part = jnp.pad(
+        expand_part, ((0, sum_rows(expand_part.shape[0]) - expand_part.shape[0]), (0, 0))
+    )
+    sizes = [sum_rows(expand_part.shape[0]), sum_rows(9 * middle), sum_rows(channels)]
+    outs = (
+        shape((pixels, channels), low),
+        *[shape((size, middle), low) for size in sizes],
+        shape((2 * per, LANES), wide),
+    )
+    scratch = [
+        pltpu.VMEM((3, height, width + 2 * EDGE, middle), low),
+        pltpu.VMEM((height, width + 2 * EDGE, middle), wide),
+        pltpu.VMEM((pixels, middle), low),
+        pltpu.VMEM((middle, pixels), low),
+        pltpu.VMEM((channels, pixels), low),
+        pltpu.VMEM((pixels, middle), wide),
+        pltpu.VMEM((pixels, middle), low),
+        pltpu.VMEM((sizes[0] // 2, middle), low),
+        *[pltpu.VMEM((size, middle), low) for size in sizes[1:]],
+        pltpu.VMEM((devices, 2 * per, LANES), wide),
+        sems((2, height)),
+        sems((2, height)),
+        sems((2, 3)),
+        sems((2,)),
+    ]
+    for size in sizes:
+        scratch += sum_scratch(size, middle)
+    return pl.pallas_call(
+        functools.partial(tail_kernel),
+        out_shape=outs,
+        in_specs=[whole] * 8 + [away],
+        out_specs=(whole, away, away, away, whole),
+        scratch_shapes=scratch,
+        compiler_params=pltpu.CompilerParams(
+            collective_id=13, has_side_effects=True, vmem_limit_bytes=VMEM_BYTES + (3 << 20)
+        ),
+        cost_estimate=pl.CostEstimate(
+            flops=400 * pixels * middle * middle, bytes_accessed=256 * pixels * channels, transcendentals=0
+        ),
+        name="tail",
+    )(dilated_low, first_act, dilated_weight, reduced, one, features, reduce_weight, pre_grad, expand_part)
 
 
 def on_device(
@@ -702,11 +1810,11 @@
     means, squares, crop_counts, keeps, valids = unpack(
         gathered, mean.shape, square.shape, (CROPS,), (1,), (1,)
     )
-    center, scale_one = merged_stats(means, squares, share, count)
+    center_one, scale_one = merged_stats(means, squares, share, count)
     crop_count, keep_count, valid_count = (
         jnp.sum(crop_counts, axis=0), jnp.sum(keeps), jnp.sum(valids)
     )
-    normed_one = normalize(reduced, center, scale_one)
+    normed_one = normalize(reduced, center_one, scale_one)
     gated_one = normed_one[0] * mid_gain[0] + mid_shift[0]
     first_act = sigmoid_linear(gated_one).astype(low)
     first_field = first_act.reshape(height, width, -1)
@@ -719,15 +1827,15 @@
     dilated = dilated[None]
     mean, square = local_stats(dilated)
     means, squares = unpack(gather_all(pack(mean, square), 1), mean.shape, square.shape)
-    center, scale_two = merged_stats(means, squares, share, count)
-    normed_two = normalize(dilated, center, scale_two)
+    center_two, scale_two = merged_stats(means, squares, share, count)
+    normed_two = normalize(dilated, center_two, scale_two)
     gated_two = normed_two[0] * mid_gain[1] + mid_shift[1]
     second_act = sigmoid_linear(gated_two).astype(low)
     expanded = matmul(second_act, expand_weight)[None]
     mean, square = local_stats(expanded)
     means, squares = unpack(gather_all(pack(mean, square), 2), mean.shape, square.shape)
-    center, scale_three = merged_stats(means, squares, share, count)
-    normed_three = normalize(expanded, center, scale_three)
+    center_three, scale_three = merged_stats(means, squares, share, count)
+    normed_three = normalize(expanded, center_three, scale_three)
     pre_trunk = normed_three[0] * out_gain + out_shift + flat.astype(jnp.float32)
     trunk = sigmoid_linear(pre_trunk).astype(low)
     local_sums = jnp.einsum("pk,pc->kc", members, trunk, preferred_element_type=jnp.float32)
@@ -745,7 +1853,14 @@
         [labels.reshape(pixels).astype(jnp.float32), keep, valid, *geometry_target.reshape(4, pixels)],
         axis=1,
     )
-    branch_low, proj_part, head_part, crop_local, crop_pre, sums_five, sums_four = pyramid(
+    devices = lax.axis_size("rows") * lax.axis_size("cols")
+    crop_rows = CROPS * channels // LANES
+    piece = -(-crop_rows // devices)
+    crop_sums = jnp.pad(local_sums.reshape(crop_rows, LANES), ((0, piece * devices - crop_rows), (0, 0)))
+    crop_sums = jnp.pad(
+        crop_sums.reshape(devices, piece, LANES), ((0, 0), (0, -piece % 8), (0, 0))
+    )
+    branch_low, proj_part, head_part, crop_local, crop_pre, sums_five, sums_four, crop_table = pyramid(
         height,
         trunk,
         jnp.pad(sep_depth.reshape(27, channels).astype(jnp.float32), ((0, 5), (0, 0))),
@@ -761,7 +1876,9 @@
         jnp.pad(jnp.broadcast_to(head_bias, (8, outs)), wide_row),
         jnp.broadcast_to(factors, (8, LANES)),
         jnp.pad(info, ((0, 0), (0, 1))),
-    )
+        crop_sums,
+    )
+    crop_table = crop_table[:, :piece].reshape(-1, LANES)[:crop_rows].reshape(CROPS, channels)
     per = aspp_width // LANES
     proj_shift_grad = sums_five[:per].reshape(1, aspp_width)
     proj_gain_grad = sums_five[per : 2 * per].reshape(1, aspp_width)
@@ -775,97 +1892,92 @@
     losses = loss_sums / counts
     objective = jnp.sum(scale_exp * losses - task_scales)
     grad_scales = scale_exp * losses - 1.0
-    (crop_total,) = shared_sums(3, crop_local)
-    taps = sep_depth.astype(jnp.float32)[:, :, :, None] * sep_point.astype(jnp.float32)[:, None, :, :]
-    taps = jnp.transpose(taps.astype(low), (0, 2, 1, 3)).reshape(3, channels, 9 * aspp_width)
+    near, early, crop_total = pyramid_weights(
+        branch_low.reshape(4, height, width, aspp_width),
+        trunk,
+        jnp.pad(sep_depth.reshape(27, channels).astype(jnp.float32).T, ((0, 0), (0, LANES - 27))),
+        sep_point,
+        crop_local,
+        proj_part,
+        head_part,
+    )
     crop_low = (crop_total * gate_slope(crop_pre)).astype(low)
-    pooled = (lax.psum(local_sums, ("rows", "cols")) / crop_count[:, None]).astype(low)
+    pooled = (crop_table / crop_count[:, None]).astype(low)
     grad_pool_weight = jnp.einsum("kc,kd->cd", pooled, crop_low, preferred_element_type=jnp.float32)
     pooled_grad = (
         jnp.einsum("kd,cd->kc", crop_low, pool_weight, preferred_element_type=jnp.float32)
         / crop_count[:, None]
     )
-    trunk_grad = jnp.einsum(
-        "pd,cd->pc", branch_low[0], aspp_point, preferred_element_type=jnp.float32
-    )
-    trunk_grad = trunk_grad + jnp.dot(members_wide, pooled_grad, precision=highest)
-    grad_aspp_point = jnp.einsum(
-        "pc,pd->cd", trunk, branch_low[0], preferred_element_type=jnp.float32
-    )
-    point_grads = []
-    depth_grads = []
-    for index in range(3):
-        rate = BASE_RATE * (index + 1)
-        near = fetch(branch_low[index + 1].reshape(height, width, aspp_width), rate)
-        moved = jnp.concatenate(
-            [offset_piece(near, 8 - tap, rate, width) for tap in range(9)], axis=1
-        )
-        trunk_grad = trunk_grad + jnp.einsum(
-            "pd,cd->pc", moved, taps[index], preferred_element_type=jnp.float32
-        )
-        whole = jnp.einsum("pc,pd->cd", trunk, moved, preferred_element_type=jnp.float32)
-        whole = whole.reshape(channels, 9, aspp_width)
-        point_grads.append(jnp.sum(whole * sep_depth[index].T.astype(jnp.float32)[:, :, None], axis=1))
-        depth_grads.append(
-            jnp.sum(whole * sep_point[index].astype(jnp.float32)[:, None, :], axis=2).T
-        )
-    pre_grad = trunk_grad * gate_slope(pre_trunk)
-    expand_grad, out_gain_grad, out_shift_grad = norm_backward(
-        pre_grad[None], normed_three, scale_three, out_gain[None], count, 7
-    )
-    expand_low = expand_grad[0].astype(low)
-    grad_expand_weight = jnp.einsum(
-        "pc,pd->cd", second_act, expand_low, preferred_element_type=jnp.float32
-    )
-    second_grad = jnp.einsum(
-        "pd,cd->pc", expand_low, expand_weight, preferred_element_type=jnp.float32
-    )
-    dilated_grad, two_gain_grad, two_shift_grad = norm_backward(
-        (second_grad * gate_slope(gated_two))[None], normed_two, scale_two, mid_gain[1:2], count, 8
-    )
-    dilated_low = dilated_grad[0].astype(low)
-    dilated_near = fetch(dilated_low.reshape(height, width, -1), MID_RATE)
-    first_grad = jnp.zeros((pixels, dilated_weight.shape[1]), jnp.float32)
-    dilated_grads = []
-    for tap in range(9):
-        dilated_grads.append(
-            jnp.einsum(
-                "pc,pd->cd",
-                offset_piece(first_near, tap, MID_RATE, width),
-                dilated_low,
-                preferred_element_type=jnp.float32,
-            )
-        )
-        first_grad = first_grad + jnp.einsum(
-            "pd,cd->pc",
-            offset_piece(dilated_near, 8 - tap, MID_RATE, width),
-            dilated_weight[tap],
-            preferred_element_type=jnp.float32,
-        )
-    reduced_grad, one_gain_grad, one_shift_grad = norm_backward(
-        (first_grad * gate_slope(gated_one))[None], normed_one, scale_one, mid_gain[0:1], count, 9
-    )
-    reduced_low = reduced_grad[0].astype(low)
-    grad_reduce_weight = jnp.einsum(
-        "pc,pd->cd", flat, reduced_low, preferred_element_type=jnp.float32
-    )
-    input_grad = (
-        jnp.einsum("pd,cd->pc", reduced_low, reduce_weight, preferred_element_type=jnp.float32)
-        + pre_grad
-    )
-    grad_features = input_grad.astype(low).reshape(height, width, channels)
-    parts = (
-        grad_reduce_weight,
-        jnp.stack(dilated_grads),
-        grad_expand_weight,
-        grad_aspp_point,
-        jnp.stack(depth_grads),
-        jnp.stack(point_grads),
-        proj_part,
-        head_part,
-    )
-    summed = lax.psum(tuple(part.astype(low) for part in parts), ("rows", "cols"))
-    summed = [part.astype(jnp.float32) for part in summed]
+    pooled_grad = jnp.pad(pooled_grad, ((0, LANES - CROPS), (0, 0)))
+    crop_high = pooled_grad.astype(low)
+    crop_rest = (pooled_grad - crop_high.astype(jnp.float32)).astype(low)
+    pre_low, expand_part, dilated_low, sums_three, sums_two, early_sum = trunk_back(
+        near,
+        branch_low[0],
+        jnp.pad(sep_depth.reshape(27, channels).astype(jnp.float32).T, ((0, 0), (0, LANES - 27))),
+        sep_point,
+        aspp_point,
+        jnp.pad(members, ((0, 0), (0, LANES - CROPS))),
+        crop_high,
+        crop_rest,
+        expanded[0],
+        flat,
+        jnp.pad(
+            jnp.concatenate([center_three, scale_three, out_gain[None], out_shift[None]]), ((0, 4), (0, 0))
+        ),
+        dilated[0],
+        jnp.pad(
+            jnp.concatenate([center_two, scale_two, mid_gain[1:2], mid_shift[1:2]]), ((0, 4), (0, 0))
+        ),
+        second_act,
+        expand_weight,
+        early,
+    )
+    folded = sums_three.reshape(-1, 2 * per, LANES)
+    out_shift_grad = folded[:, :per].reshape(1, channels)
+    out_gain_grad = folded[:, per:].reshape(1, channels)
+    middle = dilated_low.shape[1]
+    two_shift_grad, two_gain_grad = sums_two.reshape(2, 1, middle)
+    grad_features, expand_sum, dilated_sum, reduce_sum, sums_one = tail(
+        height,
+        dilated_low,
+        first_act,
+        dilated_weight,
+        reduced[0],
+        jnp.pad(
+            jnp.concatenate([center_one, scale_one, mid_gain[0:1], mid_shift[0:1]]), ((0, 4), (0, 0))
+        ),
+        flat,
+        reduce_weight,
+        pre_low,
+        expand_part,
+    )
+    one_shift_grad, one_gain_grad = sums_one.reshape(2, 1, middle)
+    grad_features = grad_features.reshape(height, width, channels)
+    expand_sum = expand_sum[:channels].reshape(-1, middle, middle)
+    grad_expand_weight = jnp.transpose(expand_sum, (1, 0, 2)).reshape(middle, channels)
+    first, second = early_sum[:channels], early_sum[channels : 2 * channels]
+    sep_sum = jnp.stack([first[:, :aspp_width], first[:, aspp_width:], second[:, :aspp_width]])
+    at = 2 * channels
+    tables = []
+    for size, extent in ((proj_weight.shape[0], aspp_width), (channels, LANES), (aspp_width, LANES)):
+        blocks = 2 * aspp_width // extent
+        table = early_sum[at : at + size // blocks].reshape(size // blocks, blocks, extent)
+        tables.append(jnp.transpose(table, (1, 0, 2)).reshape(size, extent))
+        at += size // blocks
+    summed = [
+        value.astype(jnp.float32)
+        for value in (
+            reduce_sum[:channels],
+            dilated_sum[: 9 * middle].reshape(9, middle, middle),
+            grad_expand_weight,
+            second[:, aspp_width:],
+            tables[1][:, :27].T.reshape(3, 9, channels),
+            sep_sum,
+            tables[0],
+            tables[2],
+        )
+    ]
     grad_mid_gain = jnp.concatenate([one_gain_grad, two_gain_grad], axis=0)
     grad_mid_shift = jnp.concatenate([one_shift_grad, two_shift_grad], axis=0)
     grad_aspp_gain = jnp.concatenate([branch_gain_grad, proj_gain_grad], axis=0)

time: 1050 us -> 790 us (0.75)
  Pallas kernels: 260 us -> 619 us
  waiting for transfers between devices: 334 us -> 40.3 us
  matrix products: 186 us -> 20.7 us
  local copies, waits for them, and re-layouts: 99.9 us -> 40.2 us
  starting transfers between devices: 53.8 us -> 10.1 us
  other arithmetic: 83 us -> 50.8 us
  between operations: 17.1 us -> 2.57 us
    pallas_call x0 -> x3, Pallas kernels: none -> 427 us  [the longest x1 180 us: tail(): pl.pallas_call(functools.partial(tail_kernel), out_shape=outs, in_specs=[...]
    psum x2 -> x0, waiting for transfers between devices: 232 us -> none  [the longest x1 232 us: on_device(): lax.psum(tuple((part.astype(low) for part in parts)), ('rows', 'cols'))]
    dot_general x31 -> x0, matrix products: 158 us -> none  [the longest x3 52.4 us: on_device(): jnp.einsum('pd,cd->pc', moved, taps[index], preferred_element_type=jnp.fl...]
    pallas_call x7 -> x3, Pallas kernels: 115 us -> 39.3 us  [gather_all(): pl.pallas_call(functools.partial(gather_kernel, rows, cols), out_shape=ja...]
    ppermute x10 -> x2, waiting for transfers between devices: 102 us -> 40.3 us  [from_behind(): lax.ppermute(value, axis, [(source, source + steps) for source in range(i...]
    ppermute x10 -> x2, starting transfers between devices: 32.7 us -> 6.53 us  [from_behind(): lax.ppermute(value, axis, [(source, source + steps) for source in range(i...]
    convert_element_type x10 -> x7, other arithmetic: 41.2 us -> 18.2 us  [the longest x5 16.7 us: on_device(): value.astype(jnp.float32)]
    dot_general x3 -> x0, local copies, waits for them, and re-layouts: 20.1 us -> none  [on_device(): jnp.einsum('pc,pd->cd', trunk, moved, preferred_element_type=jnp.float32)]
  transfers between devices with their start and end apart: 22 -> 4, of which waited for: 8 -> 2; matrix products, arithmetic and copies ran while one was open for 27% -> 3% of each run, Pallas kernels for 7% -> 0%
where the time goes in v3:
time: 790 us; the launch traced here: 784 us
  Pallas kernels  619 us (78%)
  other arithmetic  50.8 us (6%)
  waiting for transfers between devices  40.3 us (5%)
  local copies, waits for them, and re-layouts  40.2 us (5%)
  matrix products  20.7 us (3%)
  starting transfers between devices  10.1 us (1%)
    pallas_call x1, Pallas kernels, tail(): pl.pallas_call(functools.partial(tail_kernel), out_shape=outs, in_specs=[...  180 us
    pallas_call x1, Pallas kernels, pyramid(): pl.pallas_call(functools.partial(pyramid_kernel, height), out_shape=outs,...  152 us
    pallas_call x1, Pallas kernels, trunk_back(): pl.pallas_call(trunk_back_kernel, out_shape=outs, in_specs=[away] + [whol...  143 us
    pallas_call x1, Pallas kernels, pyramid_weights(): pl.pallas_call(pyramid_weights_kernel, out_shape=outs, in_specs=[whole] *...  104 us
    ppermute x2, waiting for transfers between devices, from_behind(): lax.ppermute(value, axis, [(source, source + steps) for source in range(i...  40.3 us
    pallas_call x3, Pallas kernels, gather_all(): pl.pallas_call(functools.partial(gather_kernel, rows, cols), out_shape=ja...  39.3 us
    convert_element_type x5, other arithmetic, on_device(): value.astype(jnp.float32)  16.7 us
    dot_general x11, matrix products, matmul(): return jnp.dot(left, right, preferred_element_type=jnp.float32)  16.5 us
  transfers between devices with their start and end apart: 4, of which 2 were waited for; matrix products, arithmetic and copies ran while one was open for 3% of the time, Pallas kernels for 0%

profile of v3, /device:TPU:11, one launch (start us, length us, event | category | flops | bytes accessed | tf_op | source)
XLA Modules:
  0.0 783.6 jit_solution(7985490329450578423)
XLA Ops:
  0.7 5.2 fusion.51
  9.9 12.8 %gather_all.3 = f32[32,16,128]{2,1,0:T(8,128)} custom-call(f32[16,128]{1,0:T(8,128)} %pad_bitcast_fusion.x_ref), custom_call_target="tpu_custom_call" | custom-call | tf_op jit(solution)/shard_map/gather_all/pallas_call | solution.py:53
  25.4 2.3 collective-permute-start.1
  33.2 1.8 compare_select_fusion.1
  38.3 1.7 pad.56.members
  42.5 1.9 pad.62.info
  45.7 2.1 collective-permute-start.3
  47.8 1.8 fusion.11
  49.6 4.5 collective-permute-start.2
  54.4 1.7 fusion.9
  56.9 16.0 %collective-permute-done.3 = bf16[4,264,512]{2,1,0:T(8,128)(2,1)S(1)} collective-permute-done((bf16[4,264,512]{2,1,0:T(8,128)(2,1)S(1)}, bf16[4,264,512]{2,1,0:T(8,128)(2,1)S(1)}, u32[]{:S(2)}, u32[]{:S(2)}) %collective-permute-start.3) | collective-permute-done | bytes 1081376 | tf_op jit(solution)/shard_map/ppermute | solution.py:81
  74.7 24.3 %collective-permute-done.2 = bf16[4,264,512]{2,1,0:T(8,128)(2,1)S(1)} collective-permute-done((bf16[4,264,512]{2,1,0:T(8,128)(2,1)S(1)}, bf16[4,264,512]{2,1,0:T(8,128)(2,1)S(1)}, u32[]{:S(2)}, u32[]{:S(2)}) %collective-permute-start.2) | collective-permute-done | bytes 1081376 | tf_op jit(solution)/shard_map/ppermute | solution.py:81
  103.8 8.9 %gather_all.4 = f32[32,8,128]{2,1,0:T(8,128)} custom-call(f32[8,128]{1,0:T(8,128)} %pad_maximum_fusion.6.x_ref), custom_call_target="tpu_custom_call" | custom-call | tf_op jit(solution)/shard_map/gather_all/pallas_call | solution.py:53
  114.5 2.3 fusion.53
  117.8 2.5 copy-done
  120.9 17.6 %gather_all.5 = f32[32,32,128]{2,1,0:T(8,128)} custom-call(f32[32,128]{1,0:T(8,128)} %pad_maximum_fusion.3.x_ref), custom_call_target="tpu_custom_call" | custom-call | tf_op jit(solution)/shard_map/gather_all/pallas_call | solution.py:53
  140.0 6.3 multiply_convert_fusion.trunk
  146.3 2.0 copy-done.2
  152.8 152.4 %pyramid.1 = (bf16[4,1024,256]{2,1,0:T(8,128)(2,1)}, bf16[1280,256]{1,0:T(8,128)(2,1)}, bf16[256,128]{1,0:T(8,128)(2,1)}, f32[16,256]{1,0:T(8,128)}, f32[16,256]...) custom-call(bf16[1024,2048]{1,0:T(8,128)(2,1)} %copy-done.2, f32[32,2048]{1,0:T(8,128)} %pad.55.depth, ...), custom_call_target="tpu_custom_call" | custom-call | flops 53687091200 | bytes 134217728 | tf_op jit(solution)/shard_map/pyramid/pallas_call | solution.py:644
  307.9 1.9 slice_bitcast_fusion.4.own_low
  309.8 103.8 %pyramid_weights.1 = (bf16[3,3,4,352,256]{4,3,2,1,0:T(8,128)(2,1)}, bf16[5632,512]{1,0:T(8,128)(2,1)}, f32[16,256]{1,0:T(8,128)}) custom-call(bf16[4,4,256,256]{3,2,1,0:T(8,128)(2,1)} %bitcast.221, bf16[1024,2048]{1,0:T(8,128)(2,1)} %copy-done.2, f32[2048,128]{1,0:T(8,128)} %pad.63.depth, bf16[3,2048,256]{2,1,0:T(8,128)(2,1)} %sep_point.5, ...), custom_call_target="tpu_custom_call" | custom-call | flops 53687091200 | bytes 134217728 | tf_op jit(solution)/shard_map/pyramid_weights/pallas_call | solution.py:875
  417.7 143.3 %trunk_back.1 = (bf16[1024,2048]{1,0:T(8,128)(2,1)}, bf16[2048,512]{1,0:T(8,128)(2,1)}, bf16[1024,512]{1,0:T(8,128)(2,1)}, f32[32,128]{1,0:T(8,128)}, f32[8,128]{1,0:T(8,128)}, /*index=5*/bf16[5632,512]{1,0:T(8,128)(2,1)}) custom-call(bf16[3,3,4,352,256]{4,3,2,1,0:T(8,128)(2,1)} %get-tuple-element.46.near, bf16[1024,256]{1,0:T(8,128)(2,1)} %slice_bitcast_fusion.4.own_low, ...), custom_call_target="tpu_custom_call" | custom-call | flops 42949672960 | bytes 134217728 | tf_op jit(solution)/shard_map/trunk_back/pallas_call | solution.py:1180
  561.0 4.6 slice_bitcast_fusion.2
  566.8 2.3 slice_convert_fusion.1
  570.5 3.8 broadcast_add_fusion
  574.9 180.1 %tail.1 = (bf16[1024,2048]{1,0:T(8,128)(2,1)}, bf16[2048,512]{1,0:T(8,128)(2,1)}, bf16[4608,512]{1,0:T(8,128)(2,1)}, bf16[2048,512]{1,0:T(8,128)(2,1)}, f32[8,128]{1,0:T(8,128)}) custom-call(bf16[1024,512]{1,0:T(8,128)(2,1)} %get-tuple-element.50.dilated_low, bf16[1024,512]{1,0:T(8,128)(2,1)} %copy-done.6, bf16[9,512,512]{2,1,0:T(8,128)(2,1)} %dilated_weight.1, ...), custom_call_target="tpu_custom_call" | custom-call | flops 107374182400 | bytes 536870912 | tf_op jit(solution)/shard_map/tail/pallas_call | solution.py:1752
  755.0 4.3 convert_element_type.188
  759.4 5.1 convert.14
  765.1 2.7 copy.78
  769.8 1.9 fusion.33
  775.6 4.9 maximum_convert_fusion
  781.1 2.0 copy.99
  (196 shorter events, 52.2 us)
Async XLA Ops:
  0.7 5.3 copy-start.28
  0.7 5.5 copy-start.21
  0.7 6.4 copy-start.22
  5.9 18.7 %copy-start.3 = (f32[1024,512]{1,0:T(8,128)}, f32[1024,512]{1,0:T(8,128)S(1)}, u32[]{:S(2)}) copy-start(f32[1024,512]{1,0:T(8,128)S(1)} %get-tuple-element.155.reduced) | copy-start | bytes 6291460
  5.9 17.9 %copy-start.29 = (f32[2,512]{1,0:T(2,128)S(1)}, f32[2,512]{1,0:T(2,128)}, u32[]{:S(2)}) copy-start(f32[2,512]{1,0:T(2,128)} %param.28) | copy-start | bytes 12292
  5.9 17.9 %copy-start.30 = (f32[2,512]{1,0:T(2,128)S(1)}, f32[2,512]{1,0:T(2,128)}, u32[]{:S(2)}) copy-start(f32[2,512]{1,0:T(2,128)} %param.27) | copy-start | bytes 12292
  24.6 23.2 %copy-start.6 = (bf16[1024,512]{1,0:T(8,128)(2,1)}, bf16[1024,512]{1,0:T(8,128)(2,1)S(1)}, u32[]{:S(2)}) copy-start(bf16[1024,512]{1,0:T(8,128)(2,1)S(1)} %get-tuple-element.111.first_act) | copy-start | bytes 3145732
  24.6 6.0 copy-start.36
  24.6 8.0 %copy-start.31 = (s32[4,256]{1,0:T(4,128)S(1)}, s32[4,256]{1,0:T(4,128)}, u32[]{:S(2)}) copy-start(s32[4,256]{1,0:T(4,128)} %param.42) | copy-start | bytes 12292
  24.6 8.0 %copy-start.18 = (f32[4,4,256]{2,1,0:T(4,128)S(1)}, f32[4,4,256]{2,1,0:T(4,128)}, u32[]{:S(2)}) copy-start(f32[4,4,256]{2,1,0:T(4,128)} %param.45) | copy-start | bytes 49156
  24.6 10.4 %copy-start.12 = (bf16[3,9,2048]{2,0,1:T(4,128)(2,1)S(1)}, bf16[3,9,2048]{2,0,1:T(4,128)(2,1)}, u32[]{:S(2)}) copy-start(bf16[3,9,2048]{2,0,1:T(4,128)(2,1)} %param.32) | copy-start | bytes 331780
  25.3 11.0 %copy-start.26 = (f32[5,256]{1,0:T(8,128)S(1)}, f32[5,256]{1,0:T(8,128)}, u32[]{:S(2)}) copy-start(f32[5,256]{1,0:T(8,128)} %param.36) | copy-start | bytes 15364
  25.3 12.9 %copy-start.23 = (bf16[256,17]{0,1:T(8,128)(2,1)S(1)}, bf16[256,17]{0,1:T(8,128)(2,1)}, u32[]{:S(2)}) copy-start(bf16[256,17]{0,1:T(8,128)(2,1)} %param.38) | copy-start | bytes 26116
  25.4 20.1 %collective-permute-start.1 = (bf16[4,4,512]{2,1,0:T(4,128)(2,1)S(1)}, bf16[4,4,512]{2,1,0:T(4,128)(2,1)S(1)}, u32[]{:S(2)}, u32[]{:S(2)}) collective-permute-start(bf16[4,4,512]{2,1,0:T(4,128)(2,1)S(1)} %get-tuple-element.126), channel_id=1, source_target_pairs={{1,0},{3,2},{5,4},{7,6},{9,8},{11,10},{13,12},{15,14},{17,16},{19,... | collective-permute-start | bytes 49160 | tf_op jit(solution)/shard_map/ppermute | solution.py:73
  27.7 17.8 %collective-permute-start = (bf16[4,4,512]{2,1,0:T(4,128)(2,1)S(1)}, bf16[4,4,512]{2,1,0:T(4,128)(2,1)S(1)}, u32[]{:S(2)}, u32[]{:S(2)}) collective-permute-start(bf16[4,4,512]{2,1,0:T(4,128)(2,1)S(1)} %get-tuple-element.125), channel_id=1, source_target_pairs={{0,1},{2,3},{4,5},{6,7},{8,9},{10,11},{12,13},{14,15},{16,17},{18,... | collective-permute-start | bytes 49160 | tf_op jit(solution)/shard_map/ppermute | solution.py:70
  29.7 384.6 %copy-start.24 = (f32[16]{0:T(128)}, f32[16]{0:T(128)S(1)}, u32[]{:S(2)}) copy-start(f32[16]{0:T(128)S(1)} %slice_reduce_fusion.8) | copy-start | bytes 196
  44.4 11.7 %slice-start = ((s8[4718592]{0:T(1024)(128)(4,1)}), s8[4194304]{0:T(1024)(128)(4,1)S(1)}, s32[]{:S(2)}) async-start(s8[4718592]{0:T(1024)(128)(4,1)} %bitcast.189), calls=%async_computation | async-start | bytes 8388608
  45.7 27.2 %collective-permute-start.3 = (bf16[4,264,512]{2,1,0:T(8,128)(2,1)S(1)}, bf16[4,264,512]{2,1,0:T(8,128)(2,1)S(1)}, u32[]{:S(2)}, u32[]{:S(2)}) collective-permute-start(bf16[4,264,512]{2,1,0:T(8,128)(2,1)S(1)} %pad_maximum_fusion), channel_id=1, source_target_pairs={{2,0},{4,2},{6,4},{8,6},{10,8},{12,10},{14,12},{16,14},{18,16},{20... | collective-permute-start | bytes 3244040 | tf_op jit(solution)/shard_map/ppermute | solution.py:81
  47.8 8.3 %slice-start.1 = ((s8[4718592]{0:T(1024)(128)(4,1)}), s8[524288]{0:T(1024)(128)(4,1)S(1)}, s32[]{:S(2)}) async-start(s8[4718592]{0:T(1024)(128)(4,1)} %bitcast.189), calls=%async_computation.1 | async-start | bytes 1048576
  49.6 49.3 %collective-permute-start.2 = (bf16[4,264,512]{2,1,0:T(8,128)(2,1)S(1)}, bf16[4,264,512]{2,1,0:T(8,128)(2,1)S(1)}, u32[]{:S(2)}, u32[]{:S(2)}) collective-permute-start(bf16[4,264,512]{2,1,0:T(8,128)(2,1)S(1)} %pad_maximum_fusion), channel_id=1, source_target_pairs={{0,2},{2,4},{4,6},{6,8},{8,10},{10,12},{12,14},{14,16},{16,18},{18... | collective-permute-start | bytes 3244040 | tf_op jit(solution)/shard_map/ppermute | solution.py:81
  102.6 11.9 %copy-start.1 = (f32[1024,512]{1,0:T(8,128)}, f32[1024,512]{1,0:T(8,128)S(1)}, u32[]{:S(2)}) copy-start(f32[1024,512]{1,0:T(8,128)S(1)} %get-tuple-element.157.dilated) | copy-start | bytes 6291460
  116.9 3.4 copy-start
  120.3 19.7 %copy-start.16 = (f32[2048]{0:T(1024)S(1)}, f32[2048]{0:T(1024)}, u32[]{:S(2)}) copy-start(f32[2048]{0:T(1024)} %param.30) | copy-start | bytes 24580
  120.3 19.7 %copy-start.17 = (f32[2048]{0:T(1024)S(1)}, f32[2048]{0:T(1024)}, u32[]{:S(2)}) copy-start(f32[2048]{0:T(1024)} %param.29) | copy-start | bytes 24580
  148.3 3.8 copy-start.35
  309.8 103.8 %copy-start.20 = (f32[16,256]{1,0:T(8,128)S(1)}, f32[16,256]{1,0:T(8,128)}, u32[]{:S(2)}) copy-start(f32[16,256]{1,0:T(8,128)} %get-tuple-element.48) | copy-start | bytes 49156
  565.6 3.5 copy-start.34
  565.6 4.8 copy-start.37
  755.0 4.4 copy-start.5
  759.4 5.1 copy-start.10
  772.5 3.1 copy-start.7
  775.6 5.5 copy-start.8
  (13 other events, 27.4 us)

commit v4 on v3

--- a/solution.py
+++ b/solution.py
@@ -17,144 +17,9 @@
 MESH = pl.DeviceIdType.MESH
 
 
-def gather_kernel(rows, cols, x_ref, out_ref, send, recv):
-    devices = rows * cols
-    me = lax.axis_index("rows") * cols + lax.axis_index("cols")
-    barrier = pltpu.get_barrier_semaphore()
-
-    def peer(step):
-        other = lax.rem(me + step, devices)
-        return (other // cols, lax.rem(other, cols))
-
-    def greet(step, carry):
-        pl.semaphore_signal(barrier, inc=1, device_id=peer(step), device_id_type=MESH)
-        return carry
-
-    lax.fori_loop(1, devices, greet, 0)
-    out_ref[me] = x_ref[...]
-    pl.semaphore_wait(barrier, devices - 1)
-
-    def go(step, carry):
-        pltpu.make_async_remote_copy(
-            x_ref, out_ref.at[me], send, recv, device_id=peer(step), device_id_type=MESH
-        ).start()
-        return carry
-
-    lax.fori_loop(1, devices, go, 0)
-    others = out_ref.at[pl.ds(0, devices - 1)]
-    pltpu.make_async_remote_copy(
-        others, others, send, recv, device_id=peer(1), device_id_type=MESH
-    ).wait()
-
-
-def gather_all(value, collective):
-    rows, cols = lax.axis_size("rows"), lax.axis_size("cols")
-    flat = value.reshape(-1, LANES)
-    gathered = pl.pallas_call(
-        functools.partial(gather_kernel, rows, cols),
-        out_shape=jax.ShapeDtypeStruct((rows * cols,) + flat.shape, flat.dtype),
-        in_specs=[pl.BlockSpec(memory_space=pltpu.VMEM)],
-        out_specs=pl.BlockSpec(memory_space=pltpu.VMEM),
-        scratch_shapes=[pltpu.SemaphoreType.DMA, pltpu.SemaphoreType.DMA],
-        compiler_params=pltpu.CompilerParams(collective_id=collective, has_side_effects=True),
-        name="gather_all",
-    )(flat)
-    return gathered.reshape((rows * cols,) + value.shape)
-
-
-def extended(block, sides, width):
-    for axis, dim in sides:
-        count = lax.axis_size(axis)
-        forward = [(i, i + 1) for i in range(count - 1)]
-        backward = [(target, source) for source, target in forward]
-        low = lax.ppermute(
-            lax.slice_in_dim(block, block.shape[dim] - width, None, axis=dim), axis, forward
-        )
-        high = lax.ppermute(lax.slice_in_dim(block, 0, width, axis=dim), axis, backward)
-        block = jnp.concatenate([low, block, high], axis=dim)
-    return block
-
-
-def from_behind(value, axis, steps):
-    count = lax.axis_size(axis)
-    initial, last = (max(0, -steps), min(count, count - steps))
-    return lax.ppermute(value, axis, [(source, source + steps) for source in range(initial, last)])
-
-
-def sigmoid_linear(value):
-    return value * jax.nn.sigmoid(value)
-
-
 def gate_slope(value):
     sigma = jax.nn.sigmoid(value)
     return sigma * (1.0 + value * (1.0 - sigma))
-
-
-def matmul(left, right):
-    return jnp.dot(left, right, preferred_element_type=jnp.float32)
-
-
-def fetch(block, rate):
-    step = rate // block.shape[0]
-    widened = extended(block, (("cols", 1),), rate)
-    moved = {}
-    for sign in (1, -1):
-        moved[sign] = from_behind(widened, "rows", sign * step)
-    return (moved[1], widened, moved[-1])
-
-
-def offset_piece(near, index, rate, width):
-    start = rate + (index % 3 - 1) * rate
-    rows_part = near[index // 3]
-    return rows_part[:, start : start + width, :].reshape(-1, rows_part.shape[2])
-
-
-def local_stats(value):
-    mean = jnp.mean(value, axis=1)
-    centered = value - mean[:, None, :]
-    return mean, jnp.sum(centered * centered, axis=1)
-
-
-def merged_stats(means, squares, share, count):
-    center = jnp.mean(means, axis=0)
-    apart = means - center
-    spread = (jnp.sum(squares, axis=0) + share * jnp.sum(apart * apart, axis=0)) / count
-    return center, lax.rsqrt(spread + EPS)
-
-
-def pack(*values):
-    flat = jnp.concatenate([value.reshape(-1) for value in values])
-    unit = 8 * LANES
-    short = -flat.shape[0] % unit
-    return jnp.pad(flat, (0, short)) if short else flat
-
-
-def unpack(flat, *shapes):
-    out, at = [], 0
-    for shape in shapes:
-        size = 1
-        for extent in shape:
-            size *= extent
-        out.append(flat[..., at : at + size].reshape(flat.shape[:-1] + tuple(shape)))
-        at += size
-    return out
-
-
-def shared_sums(collective, *values):
-    flat = jnp.sum(gather_all(pack(*values), collective), axis=0)
-    return unpack(flat, *[value.shape for value in values])
-
-
-def normalize(value, center, scale):
-    return (value - center[:, None, :]) * scale[:, None, :]
-
-
-def norm_backward(upstream, normed, scale, gain, count, collective, *extra):
-    shift_grad, gain_grad, *extra = shared_sums(
-        collective, jnp.sum(upstream, axis=1), jnp.sum(upstream * normed, axis=1), *extra
-    )
-    inner = upstream - shift_grad[:, None, :] / count - normed * (gain_grad / count)[:, None, :]
-    return (inner * (gain * scale)[:, None, :], gain_grad, shift_grad, *extra)
 
 
 PAD = 48
@@ -215,6 +80,91 @@
         device_id=(row, lax.rem(col + 1, cols)),
         device_id_type=MESH,
     ).wait()
+
+
+def share_column(slots, sems):
+    rows, cols, row, col, me = place()
+
+    def go(step, carry):
+        other = lax.rem(row + step, rows)
+        pltpu.make_async_remote_copy(
+            slots.at[row],
+            slots.at[row],
+            sems.at[0],
+            sems.at[1],
+            device_id=(other, col),
+            device_id_type=MESH,
+        ).start()
+        return carry
+
+    lax.fori_loop(1, rows, go, 0)
+
+
+def shared_column(slots, sems):
+    rows, cols, row, col, me = place()
+    others = slots.at[pl.ds(0, rows - 1)]
+    pltpu.make_async_remote_copy(
+        others,
+        others,
+        sems.at[0],
+        sems.at[1],
+        device_id=(lax.rem(row + 1, rows), col),
+        device_id_type=MESH,
+    ).wait()
+
+
+class PairSum:
+    def __init__(self, own, pair, slots, all_, sems):
+        self.own, self.pair, self.slots, self.all_, self.sems = own, pair, slots, all_, sems
+        self.rows, self.cols, self.row, self.col, _ = place()
+
+    def to_pair(self, src, dst, at):
+        return pltpu.make_async_remote_copy(
+            src,
+            dst,
+            self.sems.at[at, 0],
+            self.sems.at[at, 1],
+            device_id=(self.row, 1 - self.col),
+            device_id_type=MESH,
+        )
+
+    def out_copy(self):
+        return self.to_pair(self.own.at[1 - self.col], self.pair, 0)
+
+    def back_copy(self):
+        return self.to_pair(self.all_.at[self.col], self.all_.at[self.col], 2)
+
+    def put(self, value):
+        self.own[0] = value[:, :LANES]
+        self.own[1] = value[:, LANES:]
+
+    def start(self):
+        self.out_copy().start()
+
+    def start_column(self):
+        self.out_copy().wait()
+        self.slots[self.row] = self.own[self.col] + self.pair[...]
+        share_column(self.slots, self.sems.at[1])
+
+    def start_back(self):
+        shared_column(self.slots, self.sems.at[1])
+        self.all_[self.col] = jnp.sum(self.slots[...], axis=0)
+        self.back_copy().start()
+
+    def finish(self):
+        self.back_copy().wait()
+        return jnp.concatenate([self.all_[0], self.all_[1]], axis=1)
+
+
+def pair_sum_scratch(count):
+    wide = jnp.float32
+    return [
+        pltpu.VMEM((2, count, LANES), wide),
+        pltpu.VMEM((count, LANES), wide),
+        pltpu.VMEM((lax.axis_size("rows"), count, LANES), wide),
+        pltpu.VMEM((2, count, LANES), wide),
+        pltpu.SemaphoreType.DMA((3, 2)),
+    ]
 
 
 def put_row(slots, me, at, vector):
@@ -285,7 +235,6 @@
     upstream,
     proj_low,
     branch_up,
-    crop_slots,
     four_slots,
     five_slots,
     back_five,
@@ -293,13 +242,13 @@
     crop_pieces,
     main_sems,
     side_sems,
-    crop_sems,
     four_sems,
     five_sems,
     back_five_sems,
     back_four_sems,
     piece_sems,
     table_sems,
+    *crop_refs,
 ):
     rows, cols, row, col, me = place()
     low, wide = jnp.bfloat16, jnp.float32
@@ -313,6 +262,9 @@
     def exists(target):
         return jnp.logical_and(target >= 0, target < rows)
 
+    def step_of(index):
+        return (BASE_RATE // height) * (index + 1)
+
     for index in range(3):
         step = BASE_RATE * (index + 1) // height
         for way in (0, 2):
@@ -320,14 +272,13 @@
             @pl.when(jnp.logical_not(exists(row - (1 - way) * step)))
             def _():
                 recv_main[index, way] = jnp.zeros(recv_main.shape[2:], low)
-                recv_side[index, way] = jnp.zeros(recv_side.shape[2:], low)
 
     half = crop_part.shape[0]
-    crop_slots[me, :half, :] = crop_part[:, :LANES]
-    crop_slots[me, half:, :] = crop_part[:, LANES:]
+    crop_total = PairSum(*crop_refs)
+    crop_total.put(crop_part[...])
     pre[0] = jnp.dot(trunk[...], aspp_point[...], preferred_element_type=wide)
     await_all()
-    share(crop_slots, crop_sems)
+    crop_total.start()
     crop_pieces[me] = crop_sums[me]
 
     def scatter(step, carry):
@@ -346,29 +297,49 @@
     side_from = pl.multiple_of((1 - col) * (PAD + width), 16)
     side_to = pl.multiple_of((1 - col) * (width - PAD), 16)
 
-    def main_copy(index, way, step):
+    def main_copy(index, way):
         return pltpu.make_async_remote_copy(
             send_main.at[index, way],
             recv_main.at[index, way],
             main_sems.at[0, index, way],
             main_sems.at[1, index, way],
-            device_id=(row + (1 - way) * step, col),
+            device_id=(row + (1 - way) * step_of(index), col),
             device_id_type=MESH,
         )
 
-    def side_copy(index, way, step):
+    def side_copy(index, way):
         return pltpu.make_async_remote_copy(
             send_side.at[index, way],
             recv_side.at[index, way],
             side_sems.at[0, index, way],
             side_sems.at[1, index, way],
-            device_id=(row + (1 - way) * step, 1 - col),
+            device_id=(row, 1 - col),
             device_id_type=MESH,
         )
 
+    def flush(number):
+        index, way = 2 - number // 3, lax.rem(2 * lax.rem(number, 3), 3)
+        side_copy(index, way).wait_recv()
+
+        @pl.when(way == 1)
+        def _():
+            for line in range(height):
+                edge = pl.ds(pl.multiple_of(line * width + side_to, 16), PAD)
+                pre[index + 1, edge, :] += recv_side[index, way, line].astype(wide)
+
+        @pl.when(way != 1)
+        def _():
+            edge = pl.ds(side_to, PAD)
+            send_main[index, way, :, edge, :] = (
+                send_main[index, way, :, edge, :].astype(wide) + recv_side[index, way].astype(wide)
+            ).astype(low)
+
+            @pl.when(exists(row + (1 - way) * step_of(index)))
+            def _():
+                main_copy(index, way).start()
+
     for index in (2, 1, 0):
         rate = BASE_RATE * (index + 1)
-        step = rate // height
 
         def one_way(turn, carry):
             way = lax.rem(2 * turn, 3)
@@ -397,17 +368,18 @@
             def _():
                 send_main[index, way] = field[:, PAD : PAD + width, :].astype(low)
 
-                @pl.when(exists(row + (1 - way) * step))
-                def _():
-                    main_copy(index, way, step).start()
-
-            @pl.when(exists(row + (1 - way) * step))
+            side_copy(index, way).start()
+            number = 3 * (2 - index) + turn
+
+            @pl.when(number > 0)
             def _():
-                side_copy(index, way, step).start()
+                flush(number - 1)
 
             return carry
 
         lax.fori_loop(0, 3, one_way, 0)
+    flush(8)
+    crop_total.start_column()
 
     def lines(body, carry=0):
         def run(line, carry):
@@ -433,36 +405,26 @@
     per = aspp // LANES
     statistics(lambda span: pre[0, span, :], four_slots, 0, 4 * per)
     for index in (2, 1, 0):
-        step = BASE_RATE * (index + 1) // height
-        for way in (0, 2, 1):
-
-            @pl.when(exists(row - (1 - way) * step))
+        for way in (0, 2):
+
+            @pl.when(exists(row - (1 - way) * step_of(index)))
             def _():
-                if way != 1:
-                    main_copy(index, way, step).wait_recv()
-                side_copy(index, way, step).wait_recv()
+                main_copy(index, way).wait_recv()
 
         def assemble(line, span, carry):
             pre[index + 1, span, :] += recv_main[index, 0, line].astype(wide) + recv_main[
                 index, 2, line
             ].astype(wide)
-            edge = pl.ds(pl.multiple_of(line * width + side_to, 16), PAD)
-            pre[index + 1, edge, :] += (
-                recv_side[index, 0, line].astype(wide)
-                + recv_side[index, 1, line].astype(wide)
-                + recv_side[index, 2, line].astype(wide)
-            )
             return carry
 
         lines(assemble)
         statistics(lambda span: pre[index + 1, span, :], four_slots, per * (index + 1), 4 * per)
     share(four_slots, four_sems)
+    crop_total.start_back()
     shared(crop_pieces, piece_sems)
     crop_table[me] = jnp.sum(crop_pieces[...], axis=0)
     share(crop_table, table_sems)
-    shared(crop_slots, crop_sems)
-    crop_total = jnp.sum(crop_slots[...], axis=0)
-    crop_value = jnp.concatenate([crop_total[:half], crop_total[half:]], axis=1) / crop_count[...]
+    crop_value = crop_total.finish() / crop_count[...]
     crop_pre[...] = crop_value
     crop_act[...] = jnp.zeros(crop_act.shape, low)
     crop_act[:half, :] = (crop_value * sigmoid(crop_value)).astype(low)
@@ -608,14 +570,13 @@
         lines(branch_back)
     shared(crop_table, table_sems)
     for index in range(3):
-        step = BASE_RATE * (index + 1) // height
         for way in range(3):
-
-            @pl.when(exists(row + (1 - way) * step))
+            side_copy(index, way).wait_send()
+        for way in (0, 2):
+
+            @pl.when(exists(row + (1 - way) * step_of(index)))
             def _():
-                if way != 1:
-                    main_copy(index, way, step).wait_send()
-                side_copy(index, way, step).wait_send()
+                main_copy(index, way).wait_send()
 
 
 def pyramid(height, trunk, depth, sep_point, aspp_point, crop_part, crop_count, members, proj_weight,
@@ -661,7 +622,6 @@
             pltpu.VMEM((pixels, aspp), wide),
             pltpu.VMEM((pixels, aspp), low),
             pltpu.VMEM((4, pixels, aspp), wide),
-            pltpu.VMEM((devices, 2 * crops, LANES), wide),
             pltpu.VMEM((devices, 8 * per, LANES), wide),
             pltpu.VMEM((devices, 8, LANES), wide),
             pltpu.VMEM((devices, 8, LANES), wide),
@@ -675,7 +635,7 @@
             sems((2,)),
             sems((2,)),
             sems((2,)),
-            sems((2,)),
+            *pair_sum_scratch(crops),
         ],
         compiler_params=pltpu.CompilerParams(
             collective_id=10, has_side_effects=True, vmem_limit_bytes=VMEM_BYTES
@@ -704,16 +664,16 @@
     shifted,
     moved,
     gathered,
-    crop_slots,
     main_sems,
     edge_sems,
-    crop_sems,
+    *crop_refs,
 ):
     rows, cols, row, col, me = place()
     low, wide = jnp.bfloat16, jnp.float32
     height, width, aspp = branch_low.shape[1:]
     pixels, channels = trunk.shape
-    half = crop_local.shape[0]
+    crop_sum = PairSum(*crop_refs)
+    crop_sum.put(crop_local[...])
     greet_all()
 
     def exists(target):
@@ -722,7 +682,7 @@
     def step_of(index):
         return BASE_RATE * (index + 1) // height
 
-    edge_from = pl.multiple_of((1 - col) * (width - PAD), 16)
+    edge_from = pl.multiple_of(PAD + (1 - col) * (width - PAD), 16)
     edge_to = pl.multiple_of(col * (width + PAD), 16)
     blank = pl.multiple_of(col * (width + PAD), 16)
 
@@ -738,11 +698,11 @@
 
     def edge_copy(index, way):
         return pltpu.make_async_remote_copy(
-            branch_low.at[index + 1, :, pl.ds(edge_from, PAD), :],
+            near.at[index, way, :, pl.ds(edge_from, PAD), :],
             near.at[index, way, :, pl.ds(edge_to, PAD), :],
             edge_sems.at[0, index, way],
             edge_sems.at[1, index, way],
-            device_id=(row + (1 - way) * step_of(index), 1 - col),
+            device_id=(row, 1 - col),
             device_id_type=MESH,
         )
 
@@ -757,20 +717,19 @@
                 def _():
                     near[index, way] = jnp.zeros(near.shape[2:], low)
 
-    crop_slots[me, :half, :] = crop_local[:, :LANES]
-    crop_slots[me, half:, :] = crop_local[:, LANES:]
     await_all()
     for index in range(3):
         edge_copy(index, 1).start()
-    for index in range(3):
+
+    def send(index):
         for way in (0, 2):
 
             @pl.when(exists(row + (1 - way) * step_of(index)))
             def _():
                 main_copy(index, way).start()
-                edge_copy(index, way).start()
-
-    share(crop_slots, crop_sems)
+
+    send(0)
+    crop_sum.start()
 
     def turn(block, carry):
         span = pl.ds(pl.multiple_of(block * width, width), width)
@@ -798,20 +757,29 @@
     for index, way in ((0, 1), (1, 1), (2, 1), (0, 0), (0, 2), (1, 0), (1, 2), (2, 0), (2, 2)):
         rate = BASE_RATE * (index + 1)
 
-        @pl.when(exists(row - (1 - way) * step_of(index)))
-        def _():
-            if way != 1:
+        if way != 1:
+
+            @pl.when(exists(row - (1 - way) * step_of(index)))
+            def _():
                 main_copy(index, way).wait_recv()
-            edge_copy(index, way).wait_recv()
-
-        shifted[...] = near[index, way].astype(wide)
-        for side in range(3):
+                edge_copy(index, way).start()
+
+        for side in (1, 0, 2):
+            if side == 0:
+
+                @pl.when(exists(row - (1 - way) * step_of(index)))
+                def _():
+                    edge_copy(index, way).wait_recv()
+
+                shifted[...] = near[index, way].astype(wide)
             tap = 3 * (2 - way) + side
             at = PAD - (side - 1) * rate
             for line in range(height):
-                moved[line * width : (line + 1) * width, :] = shifted[line, at : at + width, :].astype(
-                    low
-                )
+                if side == 1:
+                    piece = near[index, way, line, PAD : PAD + width, :]
+                else:
+                    piece = shifted[line, at : at + width, :].astype(low)
+                moved[line * width : (line + 1) * width, :] = piece
             order = 9 * index + tap
 
             def collect(part, carry):
@@ -823,6 +791,12 @@
                 return carry
 
             lax.fori_loop(0, 2, collect, 0)
+        if way == 1 and index > 0:
+            send(index)
+        if way == 1 and index == 0:
+            crop_sum.start_column()
+        if way == 0 and index == 0:
+            crop_sum.start_back()
     early[:channels, :aspp] = gathered[0].astype(low)
     early[:channels, aspp:] = gathered[1].astype(low)
     early[channels : 2 * channels, :aspp] = gathered[2].astype(low)
@@ -838,17 +812,19 @@
         at += size
     if early.shape[0] > at:
         early[at:, :] = jnp.zeros((early.shape[0] - at, 2 * aspp), low)
-    shared(crop_slots, crop_sems)
-    total = jnp.sum(crop_slots[...], axis=0)
-    crop_total[...] = jnp.concatenate([total[:half], total[half:]], axis=1)
+    crop_total[...] = crop_sum.finish()
     for index in range(3):
         for way in range(3):
 
-            @pl.when(exists(row + (1 - way) * step_of(index)))
+            @pl.when(exists(row - (1 - way) * step_of(index)))
             def _():
-                if way != 1:
+                edge_copy(index, way).wait_send()
+
+            if way != 1:
+
+                @pl.when(exists(row + (1 - way) * step_of(index)))
+                def _():
                     main_copy(index, way).wait_send()
-                edge_copy(index, way).wait_send()
 
 
 def early_rows(channels, proj_part, head_part):
@@ -859,7 +835,6 @@
 
 
 def pyramid_weights(branch_low, trunk, depth, sep_point, crop_local, proj_part, head_part):
-    devices = lax.axis_size("rows") * lax.axis_size("cols")
     height, width, aspp = branch_low.shape[1:]
     pixels, channels = trunk.shape
     crops = crop_local.shape[0]
@@ -883,10 +858,9 @@
             pltpu.VMEM((height, width + 2 * PAD, aspp), wide),
             pltpu.VMEM((pixels, aspp), low),
             pltpu.VMEM((3, channels, aspp), wide),
-            pltpu.VMEM((devices, 2 * crops, LANES), wide),
             sems((2, 3, 3)),
             sems((2, 3, 3)),
-            sems((2,)),
+            *pair_sum_scratch(crops),
         ],
         compiler_params=pltpu.CompilerParams(
             collective_id=11, has_side_effects=True, vmem_limit_bytes=VMEM_BYTES
@@ -966,13 +940,12 @@
     sems_two,
     fetch_sems,
     chunk_sems,
-    early_own,
     *early_refs,
 ):
     rows, cols, row, col, me = place()
     low, wide = jnp.bfloat16, jnp.float32
     height = near.shape[2]
-    early_sum = Sum(early, early_own, early_out, *early_refs)
+    early_sum = Sums(early, True, early_out, early_refs)
     aspp = sep_point.shape[2]
     pixels, channels = expanded.shape
     middle = dilated.shape[1]
@@ -988,10 +961,7 @@
         )
 
     fetch(0).start()
-    own_half = pltpu.make_async_copy(
-        early.at[early_sum.half_span(col)], early_own, early_refs[-1]
-    )
-    own_half.start()
+    early_sum.fetch()
 
     def chunk_of(block):
         return pl.ds(pl.multiple_of(block * aspp, aspp), aspp)
@@ -1007,8 +977,8 @@
 
     lax.fori_loop(0, chunks, own, 0)
     await_all()
-    own_half.wait()
-    early_sum.start_halves()
+    early_sum.fetched()
+    early_sum.start_half()
 
     def fetch_chunk(block):
         slot = lax.rem(block, 2)
@@ -1085,12 +1055,12 @@
             return carry
 
         if index == 0:
-            early_sum.start_quarters()
+            early_sum.start_level(0)
         if index == 2:
             fetch_chunk(0).start()
         lax.fori_loop(0, chunks, one_chunk, 0)
         if index == 1:
-            early_sum.start_parts()
+            early_sum.start_level(1)
 
     def finish(block, carry):
         span = chunk_of(block)
@@ -1117,10 +1087,10 @@
             expand_low[rows_span, span] = (inner * factor).astype(low)
         return carry
 
-    early_sum.start_back_parts()
+    early_sum.start_back(1)
     fetch_chunk(0).start()
     lax.fori_loop(0, chunks, finish, 0)
-    early_sum.start_back_quarters()
+    early_sum.start_back(0)
     grown_two = across(expand_low[...], expand_weight[...])
     shift_sum, gain_sum = jnp.zeros((1, middle), wide), jnp.zeros((1, middle), wide)
     for line in range(height):
@@ -1196,8 +1166,7 @@
             sems((2,)),
             sems((2,)),
             sems((2,)),
-            pltpu.VMEM((early.shape[0] // 2, early.shape[1]), low),
-            *sum_scratch(*early.shape),
+            *sums_scratch(*early.shape, True),
         ],
         compiler_params=pltpu.CompilerParams(
             collective_id=12, has_side_effects=True, vmem_limit_bytes=VMEM_BYTES + (3 << 20)
@@ -1297,12 +1266,17 @@
                 self.relay_copy(line).start()
 
     def wait_rest(self):
+        self.wait_edges()
+        self.wait_relay()
+
+    def wait_edges(self):
         for way in (0, 2):
 
             @pl.when(self.exists(self.row - 1 + way))
             def _():
                 self.edge_copy(way).wait_recv()
 
+    def wait_relay(self):
         @pl.when(self.exists(self.far))
         def _():
             for line in range(self.height):
@@ -1324,21 +1298,311 @@
                 self.relay_copy(line).wait_send()
 
 
+def front_kernel(
+    features,
+    reduce_weight,
+    dilated_weight,
+    expand_weight,
+    pool_weight,
+    one_in,
+    two_in,
+    three_in,
+    counts,
+    members,
+    reduced,
+    first_act,
+    dilated,
+    second_act,
+    expanded,
+    trunk,
+    one,
+    two,
+    three,
+    count_sums,
+    crop_sums,
+    crop_part,
+    near,
+    shifted,
+    moved,
+    one_slots,
+    two_slots,
+    three_own,
+    three_pair,
+    three_slots,
+    three_all,
+    direct,
+    relay,
+    edge,
+    one_sems,
+    two_sems,
+    pair_sems,
+    three_sems,
+    all_sems,
+):
+    rows, cols, row, col, me = place()
+    low, wide = jnp.bfloat16, jnp.float32
+    height = near.shape[1]
+    pixels, middle = reduced.shape
+    channels = features.shape[1]
+    width = pixels // height
+    share_size = float(pixels)
+    count = float(pixels * rows * cols)
+    per = middle // LANES
+    halo = Halo(near, direct, relay, edge)
+    greet_all()
+    halo.clear()
+    reduced[...] = jnp.dot(features[...], reduce_weight[...], preferred_element_type=wide)
+
+    def lines(body, carry=0):
+        def run(line, carry):
+            return body(line, pl.ds(pl.multiple_of(line * width, width), width), carry)
+
+        return lax.fori_loop(0, height, run, carry)
+
+    def keep_low(line, span, carry):
+        near[1, line, EDGE : EDGE + width, :] = reduced[span, :].astype(low)
+        return carry
+
+    lines(keep_low)
+    await_all()
+    halo.start()
+
+    def statistics(value_of, extent):
+        zero = jnp.zeros((1, extent), wide)
+        total = lines(lambda line, span, acc: acc + jnp.sum(value_of(span), axis=0, keepdims=True), zero)
+        mean = total / share_size
+
+        def squares(line, span, acc):
+            apart = value_of(span) - mean
+            return acc + jnp.sum(apart * apart, axis=0, keepdims=True)
+
+        return mean, lines(squares, zero)
+
+    def settle(table, given, center, scale):
+        table[...] = jnp.zeros(table.shape, wide)
+        table[0:1, :] = center
+        table[1:2, :] = scale
+        table[2:4, :] = given[0:2, :]
+
+    def activated(value, table):
+        gated = (value - table[0:1, :]) * table[1:2, :] * table[2:3, :] + table[3:4, :]
+        return gated * sigmoid(gated)
+
+    mean, square = statistics(lambda span: reduced[span, :], middle)
+    one_slots[me] = jnp.zeros(one_slots.shape[1:], wide)
+    put_row(one_slots, me, 0, mean)
+    put_row(one_slots, me, per, square)
+    put_row(one_slots, me, 2 * per, counts[0:1, :])
+    share(one_slots, one_sems)
+    shared(one_slots, one_sems)
+    center, scale = merged(one_slots, per, share_size, count)
+    settle(one, one_in, take_row(center, 0, middle), take_row(scale, 0, middle))
+    count_sums[...] = jnp.sum(one_slots[:, 2 * per : 2 * per + 8, :], axis=0)
+
+    def first(line, span, carry):
+        first_act[span, :] = activated(reduced[span, :], one).astype(low)
+        return carry
+
+    lines(first)
+
+    def one_way(way, own):
+        alive = jnp.where(halo.exists(row - 1 + way), 1.0, 0.0)
+
+        def open_line(line, span, carry):
+            shifted[line] = activated(near[way, line].astype(wide), one) * alive
+            if own:
+                shifted[line, EDGE : EDGE + width, :] = first_act[span, :].astype(wide)
+            blank = pl.multiple_of(col * (width + EDGE), 16)
+            shifted[line, pl.ds(blank, EDGE), :] = jnp.zeros((EDGE, middle), wide)
+            for side in range(3):
+                at = EDGE + (side - 1) * MID_RATE
+                moved[span, side * middle : (side + 1) * middle] = shifted[
+                    line, at : at + width, :
+                ].astype(low)
+            return carry
+
+        lines(open_line)
+        made = jnp.dot(moved[...], dilated_weight[way], preferred_element_type=wide)
+        if own:
+            dilated[...] = made
+        else:
+            dilated[...] += made
+
+    halo.wait_own()
+    one_way(1, True)
+    halo.pass_on()
+    halo.wait_edges()
+    one_way(halo.pair_way, False)
+    halo.wait_relay()
+    one_way(halo.far_way, False)
+    mean, square = statistics(lambda span: dilated[span, :], middle)
+    put_row(two_slots, me, 0, mean)
+    put_row(two_slots, me, per, square)
+    share(two_slots, two_sems)
+    shared(two_slots, two_sems)
+    center, scale = merged(two_slots, per, share_size, count)
+    settle(two, two_in, take_row(center, 0, middle), take_row(scale, 0, middle))
+
+    def second(line, span, carry):
+        second_act[span, :] = activated(dilated[span, :], two).astype(low)
+        return carry
+
+    lines(second)
+    chunk = 2 * LANES
+    half_rows = channels // 2 // LANES
+    half_chunks = channels // 2 // chunk
+
+    def expand(block, carry):
+        span = pl.ds(pl.multiple_of(block * chunk, chunk), chunk)
+        expanded[:, span] = jnp.dot(second_act[...], expand_weight[:, span], preferred_element_type=wide)
+        mean, square = statistics(lambda rows_span: expanded[rows_span, span], chunk)
+        at = block // half_chunks * 2 * half_rows + lax.rem(block, half_chunks) * 2
+        for part in range(2):
+            lanes = slice(part * LANES, (part + 1) * LANES)
+            three_own[pl.ds(at + part, 1), :] = mean[:, lanes]
+            three_own[pl.ds(at + half_rows + part, 1), :] = square[:, lanes]
+        return carry
+
+    lax.fori_loop(0, channels // chunk, expand, 0)
+
+    def to_pair(src, dst, sems):
+        return pltpu.make_async_remote_copy(
+            src, dst, sems.at[0], sems.at[1], device_id=(row, 1 - col), device_id_type=MESH
+        )
+
+    theirs = pl.ds(pl.multiple_of((1 - col) * 2 * half_rows, 8), 2 * half_rows)
+    mine = pl.ds(pl.multiple_of(col * 2 * half_rows, 8), 2 * half_rows)
+    copy = to_pair(three_own.at[theirs], three_pair, pair_sems)
+    copy.start()
+    copy.wait()
+    own = three_own[mine, :]
+    other = three_pair[...]
+    apart = own[:half_rows] - other[:half_rows]
+    three_slots[row, :half_rows, :] = 0.5 * (own[:half_rows] + other[:half_rows])
+    three_slots[row, half_rows:, :] = (
+        own[half_rows:] + other[half_rows:] + (0.5 * share_size) * (apart * apart)
+    )
+    share_column(three_slots, three_sems)
+    shared_column(three_slots, three_sems)
+    center, scale = merged(three_slots, half_rows, 2.0 * share_size, count)
+    three_all[col, :half_rows, :] = center
+    three_all[col, half_rows:, :] = scale
+    copy = to_pair(three_all.at[col], three_all.at[col], all_sems)
+    copy.start()
+    copy.wait()
+    for half in range(2):
+        span = slice(half * channels // 2, (half + 1) * channels // 2)
+        three[0:1, span] = take_row(three_all[half], 0, channels // 2)
+        three[1:2, span] = take_row(three_all[half], half_rows, channels // 2)
+    three[2:4, :] = three_in[0:2, :]
+    three[4:8, :] = jnp.zeros((4, channels), wide)
+    crops = crop_sums.shape[0]
+
+    def last(block, carry):
+        span = pl.ds(pl.multiple_of(block * chunk, chunk), chunk)
+
+        def act_line(line, rows_span, carry):
+            normed = (expanded[rows_span, span] - three[0:1, span]) * three[1:2, span]
+            gated = (
+                normed * three[2:3, span] + three[3:4, span] + features[rows_span, span].astype(wide)
+            )
+            trunk[rows_span, span] = (gated * sigmoid(gated)).astype(low)
+            return carry
+
+        lines(act_line)
+        sums = jnp.dot(members[...], trunk[:, span], preferred_element_type=wide)[:crops, :]
+        crop_sums[:, span] = sums
+        high = sums.astype(low)
+        rest = (sums - high.astype(wide)).astype(low)
+        return (
+            carry
+            + jnp.dot(high, pool_weight[span, :], preferred_element_type=wide)
+            + jnp.dot(rest, pool_weight[span, :], preferred_element_type=wide)
+        )
+
+    crop_part[...] = lax.fori_loop(
+        0, channels // chunk, last, jnp.zeros((crops, pool_weight.shape[1]), wide)
+    )
+    halo.drain()
+
+
+def front(height, features, reduce_weight, dilated_weight, expand_weight, pool_weight, one_in, two_in,
+          three_in, counts, members):
+    rows = lax.axis_size("rows")
+    devices = rows * lax.axis_size("cols")
+    pixels, channels = features.shape
+    middle = reduce_weight.shape[1]
+    width = pixels // height
+    low, wide = jnp.bfloat16, jnp.float32
+    shape = jax.ShapeDtypeStruct
+    whole = pl.BlockSpec(memory_space=pltpu.VMEM)
+    sems = pltpu.SemaphoreType.DMA
+    per = middle // LANES
+    half_rows = channels // 2 // LANES
+    outs = (
+        shape((pixels, middle), wide),
+        shape((pixels, middle), low),
+        shape((pixels, middle), wide),
+        shape((pixels, middle), low),
+        shape((pixels, channels), wide),
+        shape((pixels, channels), low),
+        shape((8, middle), wide),
+        shape((8, middle), wide),
+        shape((8, channels), wide),
+        shape((8, LANES), wide),
+        shape((CROPS, channels), wide),
+        shape((CROPS, pool_weight.shape[1]), wide),
+    )
+    return pl.pallas_call(
+        front_kernel,
+        out_shape=outs,
+        in_specs=[whole] * 10,
+        out_specs=(whole,) * len(outs),
+        scratch_shapes=[
+            pltpu.VMEM((3, height, width + 2 * EDGE, middle), low),
+            pltpu.VMEM((height, width + 2 * EDGE, middle), wide),
+            pltpu.VMEM((pixels, 3 * middle), low),
+            pltpu.VMEM((devices, 2 * per + 8, LANES), wide),
+            pltpu.VMEM((devices, 2 * per, LANES), wide),
+            pltpu.VMEM((4 * half_rows, LANES), wide),
+            pltpu.VMEM((2 * half_rows, LANES), wide),
+            pltpu.VMEM((rows, 2 * half_rows, LANES), wide),
+            pltpu.VMEM((2, 2 * half_rows, LANES), wide),
+            sems((2, height)),
+            sems((2, height)),
+            sems((2, 3)),
+            sems((2,)),
+            sems((2,)),
+            sems((2,)),
+            sems((2,)),
+            sems((2,)),
+        ],
+        compiler_params=pltpu.CompilerParams(
+            collective_id=14, has_side_effects=True, vmem_limit_bytes=VMEM_BYTES
+        ),
+        name="front",
+    )(features, reduce_weight, dilated_weight, expand_weight, pool_weight, one_in, two_in, three_in,
+      counts, members)
+
+
 PLANE = 4
 
 
 class Sum:
-    def __init__(self, full, own, out, half_in, quarter_in, part_in, half_sem, quarter_sem, part_sem, copy_sem):
-        self.full, self.out = full, out
-        self.half_in, self.quarter_in, self.part_in = half_in, quarter_in, part_in
-        self.half_sem, self.quarter_sem, self.part_sem = half_sem, quarter_sem, part_sem
-        self.copy_sem = copy_sem
+    def __init__(self, full, own, out, plane_first, half_in, near_in, far_in, half_sem, near_sem, far_sem, copy_sem):
+        self.full, self.out, self.half_in = full, out, half_in
+        self.half_sem, self.copy_sem = half_sem, copy_sem
         self.rows, self.cols, self.row, self.col, _ = place()
-        self.parts = self.rows // PLANE
-        self.quarter, self.part = lax.rem(self.row, PLANE), self.row // PLANE
-        total = full.shape[0]
-        self.half_rows, self.quarter_rows = total // 2, total // 8
-        self.part_rows = self.quarter_rows // self.parts
+        parts = self.rows // PLANE
+        quarter, part = lax.rem(self.row, PLANE), self.row // PLANE
+        plane = (PLANE, quarter, lambda mate: part * PLANE + mate)
+        rest = (parts, part, lambda mate: mate * PLANE + quarter)
+        self.levels = (plane, rest) if plane_first else (rest, plane)
+        self.arrivals, self.sems = (near_in, far_in), (near_sem, far_sem)
+        self.half_rows = full.shape[0] // 2
+        self.sizes = [self.half_rows // self.levels[0][0]]
+        self.sizes.append(self.sizes[0] // self.levels[1][0])
+        self.own = own
         self.data = full.at[self.half_span(self.col)] if own is None else own
 
     def span(self, start, size):
@@ -1347,76 +1611,59 @@
     def half_span(self, col):
         return self.span(col * self.half_rows, self.half_rows)
 
-    def quarter_span(self, quarter):
-        return self.span(quarter * self.quarter_rows, self.quarter_rows)
-
-    def part_span(self, part):
-        return self.span(
-            self.quarter * self.quarter_rows + part * self.part_rows, self.part_rows
-        )
+    def level_span(self, level, at):
+        base = 0 if level == 0 else self.levels[0][1] * self.sizes[0]
+        return self.span(base + at * self.sizes[level], self.sizes[level])
 
     def out_at(self, span):
         return self.out.at[self.span(self.col * self.half_rows + span.start, span.size)]
 
-    def plane_mate(self, step):
-        mate = lax.rem(self.quarter + step, PLANE)
-        return mate, (self.part * PLANE + mate, self.col)
-
-    def part_mate(self, step):
-        mate = lax.rem(self.part + step, self.parts)
-        return mate, (mate * PLANE + self.quarter, self.col)
+    def mates(self, level):
+        count, at, row_of = self.levels[level]
+        for step in range(1, count):
+            mate = lax.rem(at + step, count)
+            yield mate, (row_of(mate), self.col)
 
     def remote(self, src, dst, sems, out_at, in_at, target):
         return pltpu.make_async_remote_copy(
             src, dst, sems.at[0, out_at], sems.at[1, in_at], device_id=target, device_id_type=MESH
         )
 
+    def fetch(self):
+        return pltpu.make_async_copy(self.full.at[self.half_span(self.col)], self.own, self.copy_sem)
+
     def half_copy(self):
+        other = self.full.at[self.half_span(1 - self.col)]
+        return self.remote(other, self.half_in, self.half_sem, 0, 0, (self.row, 1 - self.col))
+
+    def level_copy(self, level, mate, target):
+        at = self.levels[level][1]
         return self.remote(
-            self.full.at[self.half_span(1 - self.col)],
-            self.half_in,
-            self.half_sem,
-            0,
-            0,
-            (self.row, 1 - self.col),
-        )
-
-    def quarter_copy(self, step):
-        mate, target = self.plane_mate(step)
-        return self.remote(
-            self.data.at[self.quarter_span(mate)],
-            self.quarter_in.at[self.quarter],
-            self.quarter_sem,
+            self.data.at[self.level_span(level, mate)],
+            self.arrivals[level].at[at],
+            self.sems[level],
             mate,
-            self.quarter,
+            at,
             target,
         )
 
-    def quarter_arrival(self, step):
-        mate, target = self.plane_mate(step)
-        return self.remote(
-            self.quarter_in.at[mate], self.quarter_in.at[mate], self.quarter_sem, mate, mate, target
-        )
-
-    def part_copy(self, step):
-        mate, target = self.part_mate(step)
-        return self.remote(
-            self.data.at[self.part_span(mate)],
-            self.part_in.at[self.part],
-            self.part_sem,
-            mate,
-            self.part,
-            target,
-        )
-
-    def part_arrival(self, step):
-        mate, target = self.part_mate(step)
-        return self.remote(
-            self.part_in.at[mate], self.part_in.at[mate], self.part_sem, mate, mate, target
-        )
-
-    def start_halves(self):
-        self.half_copy().start()
+    def level_arrival(self, level, mate, target):
+        slot = self.arrivals[level].at[mate]
+        return self.remote(slot, slot, self.sems[level], mate, mate, target)
+
+    def back_copy(self, level, mate, target):
+        count, at, _ = self.levels[level]
+        mine = self.out_at(self.level_span(level, at))
+        return self.remote(mine, mine, self.sems[level], count + mate, count + at, target)
+
+    def back_arrival(self, level, mate, target):
+        count = self.levels[level][0]
+        theirs = self.out_at(self.level_span(level, mate))
+        return self.remote(theirs, theirs, self.sems[level], count + mate, count + mate, target)
+
+    def back_half(self, col):
+        part = self.out.at[self.half_span(col)]
+        return self.remote(part, part, self.half_sem, 1, 1, (self.row, 1 - self.col))
 
     def add(self, span, sources):
         block = 64
@@ -1440,105 +1687,131 @@
                 total = total + source(pl.ds(full * block, rest)).astype(jnp.float32)
             self.data[rows, :] = total.astype(self.data.dtype)
 
-    def start_quarters(self):
-        self.half_copy().wait()
-        self.add(self.span(0, self.half_rows), [lambda rows: self.half_in[rows, :]])
-        for step in range(1, PLANE):
-            self.quarter_copy(step).start()
-
-    def start_parts(self):
-        for step in range(1, PLANE):
-            self.quarter_copy(step).wait_send()
-            self.quarter_arrival(step).wait_recv()
-        mates = [self.plane_mate(step)[0] for step in range(1, PLANE)]
+    def start_half(self):
+        self.half_copy().start()
+
+    def start_level(self, level):
+        if level == 0:
+            self.half_copy().wait()
+            self.add(self.span(0, self.half_rows), [lambda rows: self.half_in[rows, :]])
+        else:
+            self.gather(0)
+        for mate, target in self.mates(level):
+            self.level_copy(level, mate, target).start()
+
+    def gather(self, level):
+        for mate, target in self.mates(level):
+            self.level_copy(level, mate, target).wait_send()
+            self.level_arrival(level, mate, target).wait_recv()
         self.add(
-            self.quarter_span(self.quarter),
-            [lambda rows, mate=mate: self.quarter_in[mate, rows, :] for mate in mates],
+            self.level_span(level, self.levels[level][1]),
+            [lambda rows, mate=mate: self.arrivals[level][mate, rows, :] for mate, _ in self.mates(level)],
         )
-        for step in range(1, self.parts):
-            self.part_copy(step).start()
-
-    def back_part(self, step):
-        mate, target = self.part_mate(step)
-        mine = self.out_at(self.part_span(self.part))
-        apart = self.parts
-        return self.remote(
-            mine, mine, self.part_sem, apart + mate, apart + self.part, target
-        )
-
-    def back_part_arrival(self, step):
-        mate, target = self.part_mate(step)
-        theirs = self.out_at(self.part_span(mate))
-        apart = self.parts
-        return self.remote(theirs, theirs, self.part_sem, apart + mate, apart + mate, target)
-
-    def back_quarter(self, step):
-        mate, target = self.plane_mate(step)
-        mine = self.out_at(self.quarter_span(self.quarter))
-        return self.remote(
-            mine, mine, self.quarter_sem, PLANE + mate, PLANE + self.quarter, target
-        )
-
-    def back_quarter_arrival(self, step):
-        mate, target = self.plane_mate(step)
-        theirs = self.out_at(self.quarter_span(mate))
-        return self.remote(theirs, theirs, self.quarter_sem, PLANE + mate, PLANE + mate, target)
-
-    def back_half(self):
-        mine = self.out.at[self.half_span(self.col)]
-        return self.remote(mine, mine, self.half_sem, 1, 1, (self.row, 1 - self.col))
-
-    def back_half_arrival(self):
-        theirs = self.out.at[self.half_span(1 - self.col)]
-        return self.remote(theirs, theirs, self.half_sem, 1, 1, (self.row, 1 - self.col))
-
-    def start_back_parts(self):
-        for step in range(1, self.parts):
-            self.part_copy(step).wait_send()
-            self.part_arrival(step).wait_recv()
-        mates = [self.part_mate(step)[0] for step in range(1, self.parts)]
-        span = self.part_span(self.part)
-        self.add(span, [lambda rows, mate=mate: self.part_in[mate, rows, :] for mate in mates])
-        copy = pltpu.make_async_copy(self.data.at[span], self.out_at(span), self.copy_sem)
-        copy.start()
-        copy.wait()
-        for step in range(1, self.parts):
-            self.back_part(step).start()
-
-    def start_back_quarters(self):
-        for step in range(1, self.parts):
-            self.back_part(step).wait_send()
-            self.back_part_arrival(step).wait_recv()
-        for step in range(1, PLANE):
-            self.back_quarter(step).start()
+
+    def start_back(self, level):
+        if level == 1:
+            self.gather(1)
+            span = self.level_span(1, self.levels[1][1])
+            copy = pltpu.make_async_copy(self.data.at[span], self.out_at(span), self.copy_sem)
+            copy.start()
+            copy.wait()
+        else:
+            for mate, target in self.mates(1):
+                self.back_copy(1, mate, target).wait_send()
+                self.back_arrival(1, mate, target).wait_recv()
+        for mate, target in self.mates(level):
+            self.back_copy(level, mate, target).start()
 
     def start_back_half(self):
-        for step in range(1, PLANE):
-            self.back_quarter(step).wait_send()
-            self.back_quarter_arrival(step).wait_recv()
-        self.back_half().start()
+        for mate, target in self.mates(0):
+            self.back_copy(0, mate, target).wait_send()
+            self.back_arrival(0, mate, target).wait_recv()
+        self.back_half(self.col).start()
 
     def finish(self):
-        self.back_half().wait_send()
-        self.back_half_arrival().wait_recv()
-
-
-def sum_scratch(total, lanes):
+        self.back_half(self.col).wait_send()
+        self.back_half(1 - self.col).wait_recv()
+
+
+class Sums:
+    def __init__(self, full, own, out, refs):
+        self.each = []
+        start = 0
+        for size, plane_first in sum_pieces(full.shape[0]):
+            span = pl.ds(start, size)
+            count = 7 if own is None else 8
+            mine, refs = list(refs[:count]), refs[count:]
+            part = None if own is None else mine.pop(0)
+            self.each.append(Sum(full.at[span], part, out.at[span], plane_first, *mine))
+            start += size
+        self.rest = refs
+
+    def fetch(self):
+        for each in self.each:
+            each.fetch().start()
+
+    def fetched(self):
+        for each in self.each:
+            each.fetch().wait()
+
+    def start_half(self):
+        for each in self.each:
+            each.start_half()
+
+    def start_level(self, level):
+        for each in self.each:
+            each.start_level(level)
+
+    def start_back(self, level):
+        for each in self.each:
+            each.start_back(level)
+
+    def start_back_half(self):
+        for each in self.each:
+            each.start_back_half()
+
+    def finish(self):
+        for each in self.each:
+            each.finish()
+
+
+def sum_unit():
+    return 2 * lax.axis_size("rows") * 16
+
+
+def sum_pieces(total):
+    unit = sum_unit()
+    units = total // unit
+    second = units // 3
+    pieces = [((units - second) * unit, True)]
+    if second:
+        pieces.append((second * unit, False))
+    return pieces
+
+
+def sums_scratch(total, lanes, away):
     parts = lax.axis_size("rows") // PLANE
     low, sems = jnp.bfloat16, pltpu.SemaphoreType.DMA
-    return [
-        pltpu.VMEM((total // 2, lanes), low),
-        pltpu.VMEM((PLANE, total // 8, lanes), low),
-        pltpu.VMEM((parts, total // 8 // parts, lanes), low),
-        sems((2, 2)),
-        sems((2, 2 * PLANE)),
-        sems((2, 2 * parts)),
-        sems,
-    ]
+    scratch = []
+    for size, plane_first in sum_pieces(total):
+        counts = (PLANE, parts) if plane_first else (parts, PLANE)
+        half = size // 2
+        if away:
+            scratch.append(pltpu.VMEM((half, lanes), low))
+        scratch += [
+            pltpu.VMEM((half, lanes), low),
+            pltpu.VMEM((counts[0], half // counts[0], lanes), low),
+            pltpu.VMEM((counts[1], half // counts[0] // counts[1], lanes), low),
+            sems((2, 2)),
+            sems((2, 2 * counts[0])),
+            sems((2, 2 * counts[1])),
+            sems,
+        ]
+    return scratch
 
 
 def sum_rows(rows):
-    unit = 2 * lax.axis_size("rows") * 16
+    unit = sum_unit()
     return -(-rows // unit) * unit
 
 
@@ -1564,7 +1837,6 @@
     features_turned,
     first_grad,
     reduced_low,
-    expand_own,
     dilated_data,
     reduce_data,
     slots,
@@ -1581,32 +1853,23 @@
     channels = features.shape[1]
     width = pixels // height
     count = float(pixels * rows * cols)
-    half = len(sum_refs) // 3
-    sums = [
-        Sum(full, own, out, *refs)
-        for full, own, out, refs in (
-            (expand_part, expand_own, expand_out, sum_refs[:half]),
-            (dilated_data, None, dilated_out, sum_refs[half : 2 * half]),
-            (reduce_data, None, reduce_out, sum_refs[2 * half :]),
-        )
-    ]
-    expand_sum, dilated_sum, reduce_sum = sums
+    expand_sum = Sums(expand_part, True, expand_out, sum_refs)
+    dilated_sum = Sums(dilated_data, None, dilated_out, expand_sum.rest)
+    reduce_sum = Sums(reduce_data, None, reduce_out, dilated_sum.rest)
+    sums = (expand_sum, dilated_sum, reduce_sum)
     halo = Halo(near, direct, relay, edge)
     greet_all()
-    own_half = pltpu.make_async_copy(
-        expand_part.at[expand_sum.half_span(col)], expand_own, sum_refs[half - 1]
-    )
-    own_half.start()
+    expand_sum.fetch()
     halo.clear()
     for line in range(height):
         near[1, line, EDGE : EDGE + width, :] = dilated_low[line * width : (line + 1) * width, :]
     for data, used in ((dilated_data, 9 * middle), (reduce_data, channels)):
         if data.shape[0] > used:
             data[used:, :] = jnp.zeros((data.shape[0] - used, data.shape[1]), low)
-    own_half.wait()
+    expand_sum.fetched()
     await_all()
     halo.start()
-    expand_sum.start_halves()
+    expand_sum.start_half()
 
     def turn_features(block, carry):
         span = pl.ds(pl.multiple_of(block * width, width), width)
@@ -1647,13 +1910,13 @@
     halo.wait_own()
     one_way(1)
     halo.pass_on()
-    expand_sum.start_quarters()
+    expand_sum.start_level(0)
     lax.fori_loop(0, channels // width, turn_features, 0)
     halo.wait_rest()
     one_way(0)
     one_way(2)
-    dilated_sum.start_halves()
-    expand_sum.start_parts()
+    dilated_sum.start_half()
+    expand_sum.start_level(1)
     shift_sum, gain_sum = jnp.zeros((1, middle), wide), jnp.zeros((1, middle), wide)
     for line in range(height):
         span = slice(line * width, (line + 1) * width)
@@ -1668,8 +1931,7 @@
     put_row(slots, me, 0, shift_sum)
     put_row(slots, me, per, gain_sum)
     share(slots, sems_one)
-    expand_sum.start_back_parts()
-    dilated_sum.start_quarters()
+    dilated_sum.start_level(0)
     shared(slots, sems_one)
     total = jnp.sum(slots[...], axis=0)
     sums_one[...] = total
@@ -1684,8 +1946,8 @@
     reduce_data[:channels, :] = jnp.dot(
         features_turned[...], reduced_low[...], preferred_element_type=wide
     ).astype(low)
-    reduce_sum.start_halves()
-    expand_sum.start_back_quarters()
+    reduce_sum.start_half()
+    expand_sum.start_back(1)
     chunk = 2 * LANES
 
     def last(block, carry):
@@ -1695,14 +1957,15 @@
         return carry
 
     lax.fori_loop(0, channels // chunk, last, 0)
-    reduce_sum.start_quarters()
-    dilated_sum.start_parts()
+    reduce_sum.start_level(0)
+    expand_sum.start_back(0)
+    dilated_sum.start_level(1)
+    reduce_sum.start_level(1)
     expand_sum.start_back_half()
-    reduce_sum.start_parts()
-    dilated_sum.start_back_parts()
-    reduce_sum.start_back_parts()
-    dilated_sum.start_back_quarters()
-    reduce_sum.start_back_quarters()
+    dilated_sum.start_back(1)
+    reduce_sum.start_back(1)
+    dilated_sum.start_back(0)
+    reduce_sum.start_back(0)
     dilated_sum.start_back_half()
     reduce_sum.start_back_half()
     for each in sums:
@@ -1739,7 +2002,6 @@
         pltpu.VMEM((channels, pixels), low),
         pltpu.VMEM((pixels, middle), wide),
         pltpu.VMEM((pixels, middle), low),
-        pltpu.VMEM((sizes[0] // 2, middle), low),
         *[pltpu.VMEM((size, middle), low) for size in sizes[1:]],
         pltpu.VMEM((devices, 2 * per, LANES), wide),
         sems((2, height)),
@@ -1747,8 +2009,8 @@
         sems((2, 3)),
         sems((2,)),
     ]
-    for size in sizes:
-        scratch += sum_scratch(size, middle)
+    for size, apart in zip(sizes, (True, False, False)):
+        scratch += sums_scratch(size, middle, apart)
     return pl.pallas_call(
         functools.partial(tail_kernel),
         out_shape=outs,
@@ -1792,54 +2054,41 @@
 ):
     height, width, channels = features.shape
     pixels = height * width
-    share = float(pixels)
-    count = float(pixels * lax.axis_size("rows") * lax.axis_size("cols"))
-    highest = lax.Precision.HIGHEST
     low = jnp.bfloat16
     aspp_width = proj_weight.shape[1]
     crop_flat = crop_ids.reshape(pixels)
-    members = (crop_flat[:, None] == jnp.arange(CROPS)[None, :]).astype(low)
-    members_wide = members.astype(jnp.float32)
+    members = (crop_flat[:, None] == jnp.arange(LANES)[None, :]).astype(low)
+    members_wide = members[:, :CROPS].astype(jnp.float32)
     keep = (1 - boundary_mask.reshape(pixels)).astype(jnp.float32)
     valid = valid_mask.reshape(pixels).astype(jnp.float32)
     flat = features.reshape(pixels, channels)
-    reduced = matmul(flat, reduce_weight)[None]
-    mean, square = local_stats(reduced)
-    own_counts = (jnp.sum(members_wide, axis=0), jnp.sum(keep)[None], jnp.sum(valid)[None])
-    gathered = gather_all(pack(mean, square, *own_counts), 0)
-    means, squares, crop_counts, keeps, valids = unpack(
-        gathered, mean.shape, square.shape, (CROPS,), (1,), (1,)
+    middle = reduce_weight.shape[1]
+
+    def pair_of(gain, shift):
+        return jnp.pad(jnp.stack([gain, shift]), ((0, 6), (0, 0)))
+
+    lanes = jnp.arange(LANES)
+    count_row = jnp.zeros((LANES,), jnp.float32)
+    count_row = count_row.at[:CROPS].set(jnp.sum(members_wide, axis=0))
+    count_row = count_row.at[CROPS].set(jnp.sum(keep)).at[CROPS + 1].set(jnp.sum(valid))
+    (
+        reduced, first_act, dilated, second_act, expanded, trunk, one, two, three, count_sums,
+        local_sums, crop_part,
+    ) = front(
+        height,
+        flat,
+        reduce_weight,
+        dilated_weight.reshape(3, 3 * middle, middle),
+        expand_weight,
+        pool_weight,
+        pair_of(mid_gain[0], mid_shift[0]),
+        pair_of(mid_gain[1], mid_shift[1]),
+        pair_of(out_gain, out_shift),
+        jnp.broadcast_to(count_row, (8, LANES)),
+        (lanes[:, None] == crop_flat[None, :]).astype(low),
     )
-    center_one, scale_one = merged_stats(means, squares, share, count)
-    crop_count, keep_count, valid_count = (
-        jnp.sum(crop_counts, axis=0), jnp.sum(keeps), jnp.sum(valids)
-    )
-    normed_one = normalize(reduced, center_one, scale_one)
-    gated_one = normed_one[0] * mid_gain[0] + mid_shift[0]
-    first_act = sigmoid_linear(gated_one).astype(low)
-    first_field = first_act.reshape(height, width, -1)
-    first_near = fetch(first_field, MID_RATE)
-    dilated = jnp.zeros((pixels, dilated_weight.shape[2]), jnp.float32)
-    for index in range(9):
-        dilated = dilated + matmul(
-            offset_piece(first_near, index, MID_RATE, width), dilated_weight[index]
-        )
-    dilated = dilated[None]
-    mean, square = local_stats(dilated)
-    means, squares = unpack(gather_all(pack(mean, square), 1), mean.shape, square.shape)
-    center_two, scale_two = merged_stats(means, squares, share, count)
-    normed_two = normalize(dilated, center_two, scale_two)
-    gated_two = normed_two[0] * mid_gain[1] + mid_shift[1]
-    second_act = sigmoid_linear(gated_two).astype(low)
-    expanded = matmul(second_act, expand_weight)[None]
-    mean, square = local_stats(expanded)
-    means, squares = unpack(gather_all(pack(mean, square), 2), mean.shape, square.shape)
-    center_three, scale_three = merged_stats(means, squares, share, count)
-    normed_three = normalize(expanded, center_three, scale_three)
-    pre_trunk = normed_three[0] * out_gain + out_shift + flat.astype(jnp.float32)
-    trunk = sigmoid_linear(pre_trunk).astype(low)
-    local_sums = jnp.einsum("pk,pc->kc", members, trunk, preferred_element_type=jnp.float32)
-    crop_part = jnp.dot(local_sums, pool_weight.astype(jnp.float32), precision=highest)
+    crop_count = count_sums[0, :CROPS]
+    keep_count, valid_count = count_sums[0, CROPS], count_sums[0, CROPS + 1]
     scale_exp = jnp.exp(task_scales)
     counts = jnp.stack([keep_count, valid_count, valid_count])
     factor = scale_exp / counts
@@ -1868,7 +2117,7 @@
         aspp_point,
         crop_part,
         jnp.broadcast_to(crop_count[:, None], (CROPS, aspp_width)),
-        jnp.pad(members, ((0, 0), (0, LANES - CROPS))),
+        members,
         proj_weight,
         jnp.pad(aspp_gain, ((0, 3), (0, 0))),
         jnp.pad(aspp_shift, ((0, 3), (0, 0))),
@@ -1917,18 +2166,14 @@
         jnp.pad(sep_depth.reshape(27, channels).astype(jnp.float32).T, ((0, 0), (0, LANES - 27))),
         sep_point,
         aspp_point,
-        jnp.pad(members, ((0, 0), (0, LANES - CROPS))),
+        members,
         crop_high,
         crop_rest,
-        expanded[0],
+        expanded,
         flat,
-        jnp.pad(
-            jnp.concatenate([center_three, scale_three, out_gain[None], out_shift[None]]), ((0, 4), (0, 0))
-        ),
-        dilated[0],
-        jnp.pad(
-            jnp.concatenate([center_two, scale_two, mid_gain[1:2], mid_shift[1:2]]), ((0, 4), (0, 0))
-        ),
+        three,
+        dilated,
+        two,
         second_act,
         expand_weight,
         early,
@@ -1936,17 +2181,14 @@
     folded = sums_three.reshape(-1, 2 * per, LANES)
     out_shift_grad = folded[:, :per].reshape(1, channels)
     out_gain_grad = folded[:, per:].reshape(1, channels)
-    middle = dilated_low.shape[1]
     two_shift_grad, two_gain_grad = sums_two.reshape(2, 1, middle)
     grad_features, expand_sum, dilated_sum, reduce_sum, sums_one = tail(
         height,
         dilated_low,
         first_act,
         dilated_weight,
-        reduced[0],
-        jnp.pad(
-            jnp.concatenate([center_one, scale_one, mid_gain[0:1], mid_shift[0:1]]), ((0, 4), (0, 0))
-        ),
+        reduced,
+        one,
         flat,
         reduce_weight,
         pre_low,

time: 790 us -> 691 us (0.87)
  waiting for transfers between devices: 40.3 us -> 0 us
  matrix products: 20.7 us -> 2.25 us
  Pallas kernels: 619 us -> 604 us
  other arithmetic: 50.8 us -> 36.5 us
  starting transfers between devices: 10.1 us -> 0 us
    pallas_call x3 -> x1, Pallas kernels: 39.3 us -> 106 us  [front(): pl.pallas_call(front_kernel, out_shape=outs, in_specs=[whole] * 10, out_s...]
    ppermute x4 -> x0, waiting for transfers between devices: 40.3 us -> none  [the longest x2 40.3 us: from_behind(): lax.ppermute(value, axis, [(source, source + steps) for source in range(i...]
    pallas_call x1, Pallas kernels: 180 us -> 152 us  [tail(): pl.pallas_call(functools.partial(tail_kernel), out_shape=outs, in_specs=[...]
    pallas_call x1, Pallas kernels: 104 us -> 76.9 us  [pyramid_weights(): pl.pallas_call(pyramid_weights_kernel, out_shape=outs, in_specs=[whole] *...]
    pallas_call x1, Pallas kernels: 152 us -> 129 us  [pyramid(): pl.pallas_call(functools.partial(pyramid_kernel, height), out_shape=outs,...]
    dot_general x13 -> x0, matrix products: 18.4 us -> none  [the longest x11 16.5 us: matmul(): return jnp.dot(left, right, preferred_element_type=jnp.float32)]
    ppermute x4 -> x0, starting transfers between devices: 10.1 us -> none  [the longest x2 6.53 us: from_behind(): lax.ppermute(value, axis, [(source, source + steps) for source in range(i...]
    convert_element_type x5 -> x2, other arithmetic: 9.19 us -> 0.96 us  [the longest x1 0.76 us: on_device(): (lanes[:, None] == crop_flat[None, :]).astype(low)]
  transfers between devices with their start and end apart: 4 -> 0, of which waited for: 2 -> 0; matrix products, arithmetic and copies ran while one was open for 3% -> 0% of each run, Pallas kernels for 0% -> 0%
where the time goes in v4:
time: 691 us; the launch traced here: 680 us
  Pallas kernels  604 us (87%)
  other arithmetic  36.5 us (5%)
  local copies, waits for them, and re-layouts  34.3 us (5%)
    pallas_call x1, Pallas kernels, tail(): pl.pallas_call(functools.partial(tail_kernel), out_shape=outs, in_specs=[...  152 us
    pallas_call x1, Pallas kernels, trunk_back(): pl.pallas_call(trunk_back_kernel, out_shape=outs, in_specs=[away] + [whol...  141 us
    pallas_call x1, Pallas kernels, pyramid(): pl.pallas_call(functools.partial(pyramid_kernel, height), out_shape=outs,...  129 us
    pallas_call x1, Pallas kernels, front(): pl.pallas_call(front_kernel, out_shape=outs, in_specs=[whole] * 10, out_s...  106 us
    pallas_call x1, Pallas kernels, pyramid_weights(): pl.pallas_call(pyramid_weights_kernel, out_shape=outs, in_specs=[whole] *...  76.9 us
    convert_element_type x5, other arithmetic, on_device(): value.astype(jnp.float32)  14.6 us

profile of v4, /device:TPU:11, one launch (start us, length us, event | category | flops | bytes accessed | tf_op | source)
XLA Modules:
  0.0 679.6 jit_solution(15211109343592618215)
XLA Ops:
  0.7 0.8 fusion.14
  3.9 1.3 convert_reduce_fusion.2
  5.8 1.3 convert_reduce_fusion.1
  9.1 1.4 select_maximum_fusion.three_in
  10.6 105.5 %front.1 = (f32[1024,512]{1,0:T(8,128)}, bf16[1024,512]{1,0:T(8,128)(2,1)}, f32[1024,512]{1,0:T(8,128)}, bf16[1024,512]{1,0:T(8,128)(2,1)}, f32[1024,2048]{1,0:T...) custom-call(bf16[1024,2048]{1,0:T(8,128)(2,1)} %bitcast.108, ...), custom_call_target="tpu_custom_call" | custom-call | tf_op jit(solution)/shard_map/front/pallas_call | solution.py:1556
  116.2 1.3 fusion.13
  117.5 1.4 exponential_divide_fusion
  120.1 1.3 compare_select_fusion.1
  123.4 1.6 reshape.244.crop_sums
  125.4 0.8 pad.61.info
  129.7 128.7 %pyramid.1 = (bf16[4,1024,256]{2,1,0:T(8,128)(2,1)}, bf16[1280,256]{1,0:T(8,128)(2,1)}, bf16[256,128]{1,0:T(8,128)(2,1)}, f32[16,256]{1,0:T(8,128)}, f32[16,256]...) custom-call(bf16[1024,2048]{1,0:T(8,128)(2,1)} %get-tuple-element.89.trunk, ...), custom_call_target="tpu_custom_call" | custom-call | flops 53687091200 | bytes 134217728 | tf_op jit(solution)/shard_map/pyramid/pallas_call | solution.py:605
  258.7 1.0 pad.62.depth
  259.8 76.9 %pyramid_weights.1 = (bf16[3,3,4,352,256]{4,3,2,1,0:T(8,128)(2,1)}, bf16[5632,512]{1,0:T(8,128)(2,1)}, f32[16,256]{1,0:T(8,128)}) custom-call(bf16[4,4,256,256]{3,2,1,0:T(8,128)(2,1)} %bitcast.115, bf16[1024,2048]{1,0:T(8,128)(2,1)} %get-tuple-element.89.trunk, f32[2048,128]{1,0:T(8,128)} %pad.62.depth, bf16[3,2048,256]{2,1,0:T(8,128)(2,1)} %sep_point.5, ...), custom_call_target="tpu_custom_call" | custom-call | flops 53687091200 | bytes 134217728 | tf_op jit(solution)/shard_map/pyramid_weights/pallas_call | solution.py:850
  337.8 0.9 fusion.crop_rest
  338.7 0.8 pad_convert_fusion.crop_high
  339.5 1.9 slice_bitcast_fusion.4.own_low
  341.4 141.0 %trunk_back.1 = (bf16[1024,2048]{1,0:T(8,128)(2,1)}, bf16[2048,512]{1,0:T(8,128)(2,1)}, bf16[1024,512]{1,0:T(8,128)(2,1)}, f32[32,128]{1,0:T(8,128)}, f32[8,128]{1,0:T(8,128)}, /*index=5*/bf16[5632,512]{1,0:T(8,128)(2,1)}) custom-call(bf16[3,3,4,352,256]{4,3,2,1,0:T(8,128)(2,1)} %get-tuple-element.98.near, bf16[1024,256]{1,0:T(8,128)(2,1)} %slice_bitcast_fusion.4.own_low, ...), custom_call_target="tpu_custom_call" | custom-call | flops 42949672960 | bytes 134217728 | tf_op jit(solution)/shard_map/trunk_back/pallas_call | solution.py:1150
  482.5 3.8 slice_bitcast_fusion.2
  486.3 3.2 maximum_convert_fusion
  489.5 152.2 %tail.1 = (bf16[1024,2048]{1,0:T(8,128)(2,1)}, bf16[2048,512]{1,0:T(8,128)(2,1)}, bf16[4608,512]{1,0:T(8,128)(2,1)}, bf16[2048,512]{1,0:T(8,128)(2,1)}, f32[8,128]{1,0:T(8,128)}) custom-call(bf16[1024,512]{1,0:T(8,128)(2,1)} %get-tuple-element.107.dilated_low, bf16[1024,512]{1,0:T(8,128)(2,1)} %get-tuple-element.108.first_act, ...), custom_call_target="tpu_custom_call" | custom-call | flops 107374182400 | bytes 536870912 | tf_op jit(solution)/shard_map/tail/pallas_call | solution.py:2014
  643.7 1.9 fusion.3
  645.6 7.5 %convert.14 = f32[9,512,512]{2,1,0:T(8,128)} convert(bf16[9,512,512]{2,1,0:T(8,128)(2,1)} %bitcast.103) | non-fusion elementwise | flops 2359296 | bytes 14155776 | tf_op jit(solution)/shard_map/convert_element_type | solution.py:2211
  653.7 2.7 copy.78
  656.4 2.6 convert_element_type.167
  659.0 1.2 slice_convert_fusion.1
  660.3 0.8 reshape.260
  661.2 1.2 copy.72
  662.3 1.1 copy_bitcast_fusion
  663.9 0.9 copy.74
  664.8 0.9 copy_bitcast_fusion.1
  669.5 3.8 broadcast_add_fusion
  674.4 4.8 copy.92
  (111 shorter events, 21.0 us)
Async XLA Ops:
  3.7 112.4 %copy-start.3 = (bf16[1024,128]{1,0:T(8,128)(2,1)}, bf16[1024,128]{1,0:T(8,128)(2,1)S(1)}, u32[]{:S(2)}) copy-start(bf16[1024,128]{1,0:T(8,128)(2,1)S(1)} %fusion.1.members) | copy-start | bytes 786436
  10.5 107.0 %copy-start.22 = (f32[3]{0:T(128)S(1)}, f32[3]{0:T(128)}, u32[]{:S(2)}) copy-start(f32[3]{0:T(128)} %param.46) | copy-start | bytes 40
  10.5 114.4 %copy-start.8 = (f32[4,4,256]{2,1,0:T(4,128)S(1)}, f32[4,4,256]{2,1,0:T(4,128)}, u32[]{:S(2)}) copy-start(f32[4,4,256]{2,1,0:T(4,128)} %param.51) | copy-start | bytes 49156
  10.5 114.5 %copy-start.19 = (s32[4,256]{1,0:T(4,128)S(1)}, s32[4,256]{1,0:T(4,128)}, u32[]{:S(2)}) copy-start(s32[4,256]{1,0:T(4,128)} %param.48) | copy-start | bytes 12292
  10.5 114.5 %copy-start.11 = (s32[4,256]{1,0:T(4,128)S(1)}, s32[4,256]{1,0:T(4,128)}, u32[]{:S(2)}) copy-start(s32[4,256]{1,0:T(4,128)} %param.49) | copy-start | bytes 12292
  10.5 114.6 %copy-start.12 = (s32[4,256]{1,0:T(4,128)S(1)}, s32[4,256]{1,0:T(4,128)}, u32[]{:S(2)}) copy-start(s32[4,256]{1,0:T(4,128)} %param.50) | copy-start | bytes 12292
  10.5 115.7 %copy-start.4 = (bf16[3,9,2048]{2,0,1:T(4,128)(2,1)S(1)}, bf16[3,9,2048]{2,0,1:T(4,128)(2,1)}, u32[]{:S(2)}) copy-start(bf16[3,9,2048]{2,0,1:T(4,128)(2,1)} %param.38) | copy-start | bytes 331780
  10.5 116.6 %copy-start.13 = (bf16[256,17]{0,1:T(8,128)(2,1)S(1)}, bf16[256,17]{0,1:T(8,128)(2,1)}, u32[]{:S(2)}) copy-start(bf16[256,17]{0,1:T(8,128)(2,1)} %param.44) | copy-start | bytes 26116
  10.6 117.3 %copy-start.14 = (f32[5,256]{1,0:T(8,128)S(1)}, f32[5,256]{1,0:T(8,128)}, u32[]{:S(2)}) copy-start(f32[5,256]{1,0:T(8,128)} %param.42) | copy-start | bytes 15364
  10.6 117.9 %copy-start.15 = (f32[5,256]{1,0:T(8,128)S(1)}, f32[5,256]{1,0:T(8,128)}, u32[]{:S(2)}) copy-start(f32[5,256]{1,0:T(8,128)} %param.43) | copy-start | bytes 15364
  10.6 118.5 %copy-start.24 = (f32[17]{0:T(128)S(1)}, f32[17]{0:T(128)}, u32[]{:S(2)}) copy-start(f32[17]{0:T(128)} %param.45) | copy-start | bytes 208
  122.7 214.7 %copy-start.17 = (f32[16]{0:T(128)}, f32[16]{0:T(128)S(1)}, u32[]{:S(2)}) copy-start(f32[16]{0:T(128)S(1)} %slice_bitcast_fusion.11) | copy-start | bytes 196
  259.8 76.9 %copy-start.10 = (f32[16,256]{1,0:T(8,128)S(1)}, f32[16,256]{1,0:T(8,128)}, u32[]{:S(2)}) copy-start(f32[16,256]{1,0:T(8,128)} %get-tuple-element.100) | copy-start | bytes 49156
  259.8 77.7 %copy-start = (bf16[2048,256]{1,0:T(8,128)(2,1)S(1)}, bf16[2048,256]{1,0:T(8,128)(2,1)}, u32[]{:S(2)}) copy-start(bf16[2048,256]{1,0:T(8,128)(2,1)} %pool_weight.1) | copy-start | bytes 3145732
  337.4 2.1 copy-start.6
  489.5 153.0 %copy-start.20 = (f32[8,128]{1,0:T(8,128)S(1)}, f32[8,128]{1,0:T(8,128)}, u32[]{:S(2)}) copy-start(f32[8,128]{1,0:T(8,128)} %get-tuple-element.118) | copy-start | bytes 12292
  489.5 154.2 %copy-start.5 = (f32[32,8,128]{2,1,0:T(8,128)S(1)}, f32[32,8,128]{2,1,0:T(8,128)}, u32[]{:S(2)}) copy-start(f32[32,8,128]{2,1,0:T(8,128)} %get-tuple-element.121) | copy-start | bytes 393220
  489.5 154.2 %copy-start.7 = (bf16[16,256]{1,0:T(8,128)(2,1)S(1)}, bf16[16,256]{1,0:T(8,128)(2,1)}, u32[]{:S(2)}) copy-start(bf16[16,256]{1,0:T(8,128)(2,1)} %copy-done.6) | copy-start | bytes 24580
  489.5 154.2 %copy-start.18 = (f32[16]{0:T(128)S(1)}, f32[16]{0:T(128)}, u32[]{:S(2)}) copy-start(f32[16]{0:T(128)} %copy-done.17) | copy-start | bytes 196
  645.6 7.5 %copy-start.2 = (bf16[2048,512]{1,0:T(8,128)(2,1)S(1)}, bf16[2048,512]{1,0:T(8,128)(2,1)}, u32[]{:S(2)}) copy-start(bf16[2048,512]{1,0:T(8,128)(2,1)} %get-tuple-element.116) | copy-start | bytes 6291460
  653.7 2.7 copy-start.1
  661.1 5.2 copy-start.9
  661.1 5.8 copy-start.16
  661.1 5.8 copy-start.21
  661.1 8.4 %copy-start.23 = (f32[3]{0:T(128)S(1)}, f32[3]{0:T(128)}, u32[]{:S(2)}) copy-start(f32[3]{0:T(128)} %param.46) | copy-start | bytes 40

commit v5 on v4

--- a/solution.py
+++ b/solution.py
@@ -203,15 +203,18 @@
     sep_point,
     aspp_point,
     crop_part,
-    crop_count,
+    count_sums,
     members,
     proj_weight,
     gains,
     shifts,
-    head_weight,
-    head_bias,
-    factors,
-    info,
+    head_raw,
+    bias_raw,
+    weights,
+    labels,
+    boundary,
+    valid_mask,
+    geometry,
     crop_sums,
     branch_low,
     proj_part,
@@ -221,6 +224,10 @@
     sums_five,
     sums_four,
     crop_table,
+    own_low,
+    closing,
+    head_weight,
+    head_bias,
     field,
     send_main,
     recv_main,
@@ -424,7 +431,12 @@
     shared(crop_pieces, piece_sems)
     crop_table[me] = jnp.sum(crop_pieces[...], axis=0)
     share(crop_table, table_sems)
-    crop_value = crop_total.finish() / crop_count[...]
+    crop_row = lax.broadcasted_iota(jnp.int32, (half, LANES), 0)
+    crop_lane = lax.broadcasted_iota(jnp.int32, (half, LANES), 1)
+    crop_count = jnp.sum(
+        jnp.where(crop_row == crop_lane, count_sums[0:1, :], 0.0), axis=1, keepdims=True
+    )
+    crop_value = crop_total.finish() / crop_count
     crop_pre[...] = crop_value
     crop_act[...] = jnp.zeros(crop_act.shape, low)
     crop_act[:half, :] = (crop_value * sigmoid(crop_value)).astype(low)
@@ -458,6 +470,16 @@
     center_five, scale_five = take_row(center_five, 0, aspp), take_row(scale_five, 0, aspp)
     gain_five, shift_five = gains[4:5, :], shifts[4:5, :]
     lane = lax.broadcasted_iota(jnp.int32, (width, LANES), 1)
+    outs = head_raw.shape[1]
+    head_weight[...] = jnp.zeros(head_weight.shape, low)
+    head_weight[:, :outs] = head_raw[...]
+    head_bias[...] = jnp.zeros(head_bias.shape, wide)
+    head_bias[0:1, :outs] = bias_raw[...]
+    one_lane = lax.broadcasted_iota(jnp.int32, (1, LANES), 1)
+    pixel_count = jnp.where(
+        one_lane < CLASSES, count_sums[0:1, CROPS : CROPS + 1], count_sums[0:1, CROPS + 1 : CROPS + 2]
+    )
+    factors = weights[0:1, :] / pixel_count
 
     def heads_of(line, span, carry):
         losses, bias_sum, shift_sum, gain_sum = carry
@@ -467,7 +489,17 @@
         act = (gated * sigma).astype(low)
         united[span, :] = act
         heads = jnp.dot(act, head_weight[...], preferred_element_type=wide) + head_bias[0:1, :]
-        facts = info[span, :]
+        row_of = pl.ds(line, 1)
+        facts = jnp.concatenate(
+            [
+                labels[row_of, :].astype(wide),
+                1.0 - boundary[row_of, :].astype(wide),
+                valid_mask[row_of, :].astype(wide),
+                *[geometry[part, row_of, :] for part in range(4)],
+                jnp.zeros((1, width), wide),
+            ],
+            axis=0,
+        ).T
         label, keep, valid = facts[:, 0:1], facts[:, 1:2], facts[:, 2:3]
         is_class = lane < CLASSES
         hot = jnp.where(lane.astype(wide) == label, 1.0, 0.0)
@@ -488,7 +520,7 @@
         grad = jnp.where(is_class, keep * (exps / totals - hot), 0.0)
         grad = jnp.where(is_depth, valid * error / root, grad)
         grad = jnp.where(is_normal, valid * error, grad)
-        grad = grad * factors[0:1, :]
+        grad = grad * factors
         grad_low = grad.astype(low)
         head_low[span, :] = grad_low
         up = across(grad_low, head_weight[...]) * (sigma * (1.0 + gated * (1.0 - sigma)))
@@ -514,6 +546,21 @@
     shared(back_five, back_five_sems)
     total_five = jnp.sum(back_five[...], axis=0)
     sums_five[...] = total_five
+    weighted = weights[1:2, :] * total_five[2 * per : 2 * per + 1, :] / pixel_count
+
+    def lanes_sum(row_value, first, last):
+        picked = jnp.where(jnp.logical_and(one_lane >= first, one_lane < last), row_value, 0.0)
+        return jnp.sum(picked, axis=1, keepdims=True)
+
+    tasks = (
+        lanes_sum(weighted, 0, 1),
+        lanes_sum(weighted, CLASSES, CLASSES + 1),
+        lanes_sum(weighted, CLASSES + 1, CLASSES + 4),
+    )
+    closing[...] = jnp.zeros(closing.shape, wide)
+    for part in range(3):
+        closing[0:1, part : part + 1] = tasks[part] - 1.0
+    closing[1:2, 0:1] = tasks[0] + tasks[1] + tasks[2] - lanes_sum(weights[2:3, :], 0, 3)
     shift_mean = take_row(total_five, 0, aspp) / count
     gain_mean = take_row(total_five, per, aspp) / count
 
@@ -564,7 +611,10 @@
         def branch_back(line, span, carry):
             normed = (pre[part, span, :] - centers[part]) * scales[part]
             inner = branch_up[part, span, :] - shift_mean - normed * gain_mean
-            branch_low[part, span, :] = (inner * factor).astype(low)
+            value = (inner * factor).astype(low)
+            branch_low[part, span, :] = value
+            if part == 0:
+                own_low[span, :] = value
             return carry
 
         lines(branch_back)
@@ -579,8 +629,8 @@
                 main_copy(index, way).wait_send()
 
 
-def pyramid(height, trunk, depth, sep_point, aspp_point, crop_part, crop_count, members, proj_weight,
-            gains, shifts, head_weight, head_bias, factors, info, crop_sums):
+def pyramid(height, trunk, depth, sep_point, aspp_point, crop_part, count_sums, members, proj_weight,
+            gains, shifts, head_weight, head_bias, weights, labels, boundary, valid, geometry, crop_sums):
     devices = lax.axis_size("rows") * lax.axis_size("cols")
     pixels = trunk.shape[0]
     width = pixels // height
@@ -600,14 +650,18 @@
         shape((8, LANES), wide),
         shape((8 * per, LANES), wide),
         shape(crop_sums.shape, wide),
+        shape((pixels, aspp), low),
+        shape((8, LANES), wide),
     )
     sems = pltpu.SemaphoreType.DMA
     return pl.pallas_call(
         functools.partial(pyramid_kernel, height),
         out_shape=outs,
-        in_specs=[whole] * 15,
+        in_specs=[whole] * 18,
         out_specs=(whole,) * len(outs),
         scratch_shapes=[
+            pltpu.VMEM((aspp, LANES), low),
+            pltpu.VMEM((8, LANES), wide),
             pltpu.VMEM((height, width + 2 * PAD, aspp), wide),
             pltpu.VMEM((3, 3, height, width, aspp), low),
             pltpu.VMEM((3, 3, height, width, aspp), low),
@@ -644,8 +698,8 @@
             flops=100 * pixels * trunk.shape[1] * aspp, bytes_accessed=64 * pixels * trunk.shape[1], transcendentals=0
         ),
         name="pyramid",
-    )(trunk, depth, sep_point, aspp_point, crop_part, crop_count, members, proj_weight, gains, shifts,
-      head_weight, head_bias, factors, info, crop_sums)
+    )(trunk, depth, sep_point, aspp_point, crop_part, count_sums, members, proj_weight, gains, shifts,
+      head_weight, head_bias, weights, labels, boundary, valid, geometry, crop_sums)
 
 
 def pyramid_weights_kernel(
@@ -1059,8 +1113,10 @@
         if index == 2:
             fetch_chunk(0).start()
         lax.fori_loop(0, chunks, one_chunk, 0)
+        if index == 0:
+            early_sum.start_level(1)
         if index == 1:
-            early_sum.start_level(1)
+            early_sum.start_back(1)
 
     def finish(block, carry):
         span = chunk_of(block)
@@ -1087,10 +1143,9 @@
             expand_low[rows_span, span] = (inner * factor).astype(low)
         return carry
 
-    early_sum.start_back(1)
+    early_sum.start_back(0)
     fetch_chunk(0).start()
     lax.fori_loop(0, chunks, finish, 0)
-    early_sum.start_back(0)
     grown_two = across(expand_low[...], expand_weight[...])
     shift_sum, gain_sum = jnp.zeros((1, middle), wide), jnp.zeros((1, middle), wide)
     for line in range(height):
@@ -1246,7 +1301,7 @@
 
     def start(self):
         self.edge_copy(1).start()
-        for line in range(self.height):
+        for line in range(self.height // 2):
             self.direct_copy(line).start()
         for way in (0, 2):
 
@@ -1257,13 +1312,22 @@
     def wait_own(self):
         self.edge_copy(1).wait_recv()
 
-    def pass_on(self):
-        for line in range(self.height):
-            self.direct_copy(line).wait_recv()
-
-            @pl.when(self.exists(self.onward))
-            def _():
-                self.relay_copy(line).start()
+    def pass_line(self, line):
+        self.direct_copy(line).wait_recv()
+
+        @pl.when(self.exists(self.onward))
+        def _():
+            self.relay_copy(line).start()
+
+    def pass_first(self):
+        for line in range(self.height // 2):
+            self.pass_line(line)
+        for line in range(self.height // 2, self.height):
+            self.direct_copy(line).start()
+
+    def pass_rest(self):
+        for line in range(self.height // 2, self.height):
+            self.pass_line(line)
 
     def wait_rest(self):
         self.wait_edges()
@@ -1304,11 +1368,13 @@
     dilated_weight,
     expand_weight,
     pool_weight,
-    one_in,
-    two_in,
-    three_in,
-    counts,
-    members,
+    mid_gain,
+    mid_shift,
+    out_gain,
+    out_shift,
+    crop_ids,
+    boundary,
+    valid,
     reduced,
     first_act,
     dilated,
@@ -1321,9 +1387,11 @@
     count_sums,
     crop_sums,
     crop_part,
+    pixel_crops,
     near,
     shifted,
     moved,
+    members,
     one_slots,
     two_slots,
     three_own,
@@ -1378,11 +1446,12 @@
 
         return mean, lines(squares, zero)
 
-    def settle(table, given, center, scale):
+    def settle(table, at, center, scale):
         table[...] = jnp.zeros(table.shape, wide)
         table[0:1, :] = center
         table[1:2, :] = scale
-        table[2:4, :] = given[0:2, :]
+        table[2:3, :] = mid_gain[at : at + 1, :]
+        table[3:4, :] = mid_shift[at : at + 1, :]
 
     def activated(value, table):
         gated = (value - table[0:1, :]) * table[1:2, :] * table[2:3, :] + table[3:4, :]
@@ -1392,11 +1461,25 @@
     one_slots[me] = jnp.zeros(one_slots.shape[1:], wide)
     put_row(one_slots, me, 0, mean)
     put_row(one_slots, me, per, square)
+    crop_of = lax.broadcasted_iota(jnp.int32, (LANES, width), 0)
+    for line in range(height):
+        hot = jnp.where(crop_of == crop_ids[line : line + 1, :], 1.0, 0.0)
+        members[:, line * width : (line + 1) * width] = hot.astype(low)
+        pixel_crops[line * width : (line + 1) * width, :] = hot.T.astype(low)
+    lane = lax.broadcasted_iota(jnp.int32, (8, LANES), 1)
+
+    def whole_sum(table):
+        part = jnp.sum(table[...].astype(wide), axis=0, keepdims=True)
+        return jnp.sum(part, axis=1, keepdims=True)
+
+    counts = across(jnp.ones((8, pixels), low), members[...])
+    counts = jnp.where(lane == CROPS, share_size - whole_sum(boundary), counts)
+    counts = jnp.where(lane == CROPS + 1, whole_sum(valid), counts)
     put_row(one_slots, me, 2 * per, counts[0:1, :])
     share(one_slots, one_sems)
     shared(one_slots, one_sems)
     center, scale = merged(one_slots, per, share_size, count)
-    settle(one, one_in, take_row(center, 0, middle), take_row(scale, 0, middle))
+    settle(one, 0, take_row(center, 0, middle), take_row(scale, 0, middle))
     count_sums[...] = jnp.sum(one_slots[:, 2 * per : 2 * per + 8, :], axis=0)
 
     def first(line, span, carry):
@@ -1428,9 +1511,10 @@
         else:
             dilated[...] += made
 
+    halo.pass_first()
     halo.wait_own()
     one_way(1, True)
-    halo.pass_on()
+    halo.pass_rest()
     halo.wait_edges()
     one_way(halo.pair_way, False)
     halo.wait_relay()
@@ -1441,7 +1525,7 @@
     share(two_slots, two_sems)
     shared(two_slots, two_sems)
     center, scale = merged(two_slots, per, share_size, count)
-    settle(two, two_in, take_row(center, 0, middle), take_row(scale, 0, middle))
+    settle(two, 1, take_row(center, 0, middle), take_row(scale, 0, middle))
 
     def second(line, span, carry):
         second_act[span, :] = activated(dilated[span, :], two).astype(low)
@@ -1494,9 +1578,10 @@
         span = slice(half * channels // 2, (half + 1) * channels // 2)
         three[0:1, span] = take_row(three_all[half], 0, channels // 2)
         three[1:2, span] = take_row(three_all[half], half_rows, channels // 2)
-    three[2:4, :] = three_in[0:2, :]
+    three[2:3, :] = out_gain[...]
+    three[3:4, :] = out_shift[...]
     three[4:8, :] = jnp.zeros((4, channels), wide)
-    crops = crop_sums.shape[0]
+    crops = CROPS
 
     def last(block, carry):
         span = pl.ds(pl.multiple_of(block * chunk, chunk), chunk)
@@ -1511,7 +1596,9 @@
 
         lines(act_line)
         sums = jnp.dot(members[...], trunk[:, span], preferred_element_type=wide)[:crops, :]
-        crop_sums[:, span] = sums
+        for part in range(2):
+            at = pl.multiple_of((2 * block + part) * crops, 8)
+            crop_sums[pl.ds(at, crops), :] = sums[:, part * LANES : (part + 1) * LANES]
         high = sums.astype(low)
         rest = (sums - high.astype(wide)).astype(low)
         return (
@@ -1526,8 +1613,8 @@
     halo.drain()
 
 
-def front(height, features, reduce_weight, dilated_weight, expand_weight, pool_weight, one_in, two_in,
-          three_in, counts, members):
+def front(height, features, reduce_weight, dilated_weight, expand_weight, pool_weight, mid_gain,
+          mid_shift, out_gain, out_shift, crop_ids, boundary, valid):
     rows = lax.axis_size("rows")
     devices = rows * lax.axis_size("cols")
     pixels, channels = features.shape
@@ -1550,18 +1637,20 @@
         shape((8, middle), wide),
         shape((8, channels), wide),
         shape((8, LANES), wide),
-        shape((CROPS, channels), wide),
+        shape((CROPS * channels // LANES, LANES), wide),
         shape((CROPS, pool_weight.shape[1]), wide),
+        shape((pixels, LANES), low),
     )
     return pl.pallas_call(
         front_kernel,
         out_shape=outs,
-        in_specs=[whole] * 10,
+        in_specs=[whole] * 12,
         out_specs=(whole,) * len(outs),
         scratch_shapes=[
             pltpu.VMEM((3, height, width + 2 * EDGE, middle), low),
             pltpu.VMEM((height, width + 2 * EDGE, middle), wide),
             pltpu.VMEM((pixels, 3 * middle), low),
+            pltpu.VMEM((LANES, pixels), low),
             pltpu.VMEM((devices, 2 * per + 8, LANES), wide),
             pltpu.VMEM((devices, 2 * per, LANES), wide),
             pltpu.VMEM((4 * half_rows, LANES), wide),
@@ -1581,8 +1670,8 @@
             collective_id=14, has_side_effects=True, vmem_limit_bytes=VMEM_BYTES
         ),
         name="front",
-    )(features, reduce_weight, dilated_weight, expand_weight, pool_weight, one_in, two_in, three_in,
-      counts, members)
+    )(features, reduce_weight, dilated_weight, expand_weight, pool_weight, mid_gain, mid_shift,
+      out_gain, out_shift, crop_ids, boundary, valid)
 
 
 PLANE = 4
@@ -1893,30 +1982,36 @@
         shifted[...] = near[way].astype(wide)
         for side in range(3):
             tap = 3 * (2 - way) + side
+            rows_of = pl.ds(pl.multiple_of(tap * middle, middle), middle)
             at = EDGE - (side - 1) * MID_RATE
             for line in range(height):
                 moved[line * width : (line + 1) * width, :] = shifted[line, at : at + width, :].astype(
                     low
                 )
             made = across(moved[...], dilated_weight[tap])
-            if way == 1 and side == 0:
+            if isinstance(way, int) and side == 0:
                 first_grad[...] = made
             else:
                 first_grad[...] += made
-            dilated_data[tap * middle : (tap + 1) * middle, :] = jnp.dot(
+            dilated_data[rows_of, :] = jnp.dot(
                 act_turned[...], moved[...], preferred_element_type=wide
             ).astype(low)
 
+    expand_sum.start_level(0)
     halo.wait_own()
     one_way(1)
-    halo.pass_on()
-    expand_sum.start_level(0)
+    halo.pass_first()
+    expand_sum.start_level(1)
     lax.fori_loop(0, channels // width, turn_features, 0)
-    halo.wait_rest()
-    one_way(0)
-    one_way(2)
+    halo.pass_rest()
+    expand_sum.start_back(1)
+    halo.wait_edges()
+    one_way(halo.pair_way)
+    expand_sum.start_back(0)
+    halo.wait_relay()
+    one_way(halo.far_way)
     dilated_sum.start_half()
-    expand_sum.start_level(1)
+    expand_sum.start_back_half()
     shift_sum, gain_sum = jnp.zeros((1, middle), wide), jnp.zeros((1, middle), wide)
     for line in range(height):
         span = slice(line * width, (line + 1) * width)
@@ -1947,7 +2042,6 @@
         features_turned[...], reduced_low[...], preferred_element_type=wide
     ).astype(low)
     reduce_sum.start_half()
-    expand_sum.start_back(1)
     chunk = 2 * LANES
 
     def last(block, carry):
@@ -1958,10 +2052,8 @@
 
     lax.fori_loop(0, channels // chunk, last, 0)
     reduce_sum.start_level(0)
-    expand_sum.start_back(0)
     dilated_sum.start_level(1)
     reduce_sum.start_level(1)
-    expand_sum.start_back_half()
     dilated_sum.start_back(1)
     reduce_sum.start_back(1)
     dilated_sum.start_back(0)
@@ -2027,6 +2119,57 @@
     )(dilated_low, first_act, dilated_weight, reduced, one, features, reduce_weight, pre_grad, expand_part)
 
 
+def widen_kernel(first, second, expand, dilated, reduce, sep_out, point_out, expand_out, dilated_out, reduce_out):
+    wide = jnp.float32
+    aspp, middle = point_out.shape[1], expand.shape[2]
+    sep_out[0] = first[:, :aspp].astype(wide)
+    sep_out[1] = first[:, aspp:].astype(wide)
+    sep_out[2] = second[:, :aspp].astype(wide)
+    point_out[...] = second[:, aspp:].astype(wide)
+    for block in range(expand.shape[0]):
+        expand_out[:, block * middle : (block + 1) * middle] = expand[block].astype(wide)
+    dilated_out[...] = dilated[...].astype(wide)
+    reduce_out[...] = reduce[...].astype(wide)
+
+
+def widen(early, expand, dilated, reduce, channels, aspp):
+    middle = reduce.shape[1]
+    wide = jnp.float32
+    steps = 8
+    rows = channels // steps
+    taps = 9 * middle // steps
+    lines = middle // steps
+    blocks = channels // middle
+    shape = jax.ShapeDtypeStruct
+    return pl.pallas_call(
+        widen_kernel,
+        grid=(steps,),
+        out_shape=(
+            shape((3, channels, aspp), wide),
+            shape((channels, aspp), wide),
+            shape((middle, channels), wide),
+            shape((9 * middle, middle), wide),
+            shape((channels, middle), wide),
+        ),
+        in_specs=[
+            pl.BlockSpec((rows, 2 * aspp), lambda step: (step, 0)),
+            pl.BlockSpec((rows, 2 * aspp), lambda step: (steps + step, 0)),
+            pl.BlockSpec((blocks, lines, middle), lambda step: (0, step, 0)),
+            pl.BlockSpec((taps, middle), lambda step: (step, 0)),
+            pl.BlockSpec((rows, middle), lambda step: (step, 0)),
+        ],
+        out_specs=(
+            pl.BlockSpec((3, rows, aspp), lambda step: (0, step, 0)),
+            pl.BlockSpec((rows, aspp), lambda step: (step, 0)),
+            pl.BlockSpec((lines, channels), lambda step: (step, 0)),
+            pl.BlockSpec((taps, middle), lambda step: (step, 0)),
+            pl.BlockSpec((rows, middle), lambda step: (step, 0)),
+        ),
+        compiler_params=pltpu.CompilerParams(vmem_limit_bytes=VMEM_BYTES),
+        name="widen",
+    )(early, early, expand[:channels].reshape(blocks, middle, middle), dilated, reduce)
+
+
 def on_device(
     features,
     reduce_weight,
@@ -2056,24 +2199,12 @@
     pixels = height * width
     low = jnp.bfloat16
     aspp_width = proj_weight.shape[1]
-    crop_flat = crop_ids.reshape(pixels)
-    members = (crop_flat[:, None] == jnp.arange(LANES)[None, :]).astype(low)
-    members_wide = members[:, :CROPS].astype(jnp.float32)
-    keep = (1 - boundary_mask.reshape(pixels)).astype(jnp.float32)
-    valid = valid_mask.reshape(pixels).astype(jnp.float32)
     flat = features.reshape(pixels, channels)
     middle = reduce_weight.shape[1]
 
-    def pair_of(gain, shift):
-        return jnp.pad(jnp.stack([gain, shift]), ((0, 6), (0, 0)))
-
-    lanes = jnp.arange(LANES)
-    count_row = jnp.zeros((LANES,), jnp.float32)
-    count_row = count_row.at[:CROPS].set(jnp.sum(members_wide, axis=0))
-    count_row = count_row.at[CROPS].set(jnp.sum(keep)).at[CROPS + 1].set(jnp.sum(valid))
     (
         reduced, first_act, dilated, second_act, expanded, trunk, one, two, three, count_sums,
-        local_sums, crop_part,
+        local_sums, crop_part, members,
     ) = front(
         height,
         flat,
@@ -2081,66 +2212,59 @@
         dilated_weight.reshape(3, 3 * middle, middle),
         expand_weight,
         pool_weight,
-        pair_of(mid_gain[0], mid_shift[0]),
-        pair_of(mid_gain[1], mid_shift[1]),
-        pair_of(out_gain, out_shift),
-        jnp.broadcast_to(count_row, (8, LANES)),
-        (lanes[:, None] == crop_flat[None, :]).astype(low),
+        mid_gain,
+        mid_shift,
+        out_gain.reshape(1, channels),
+        out_shift.reshape(1, channels),
+        crop_ids,
+        boundary_mask,
+        valid_mask,
     )
     crop_count = count_sums[0, :CROPS]
-    keep_count, valid_count = count_sums[0, CROPS], count_sums[0, CROPS + 1]
+    lane = jnp.arange(LANES)
     scale_exp = jnp.exp(task_scales)
-    counts = jnp.stack([keep_count, valid_count, valid_count])
-    factor = scale_exp / counts
-    lane = jnp.arange(LANES)
-    factors = jnp.where(
-        lane < CLASSES, factor[0], jnp.where(lane == CLASSES, factor[1], 2.0 * factor[2])
+    task_of = jnp.where(lane < CLASSES, scale_exp[0], jnp.where(lane == CLASSES, scale_exp[1], scale_exp[2]))
+    weights = jnp.stack(
+        [jnp.where(lane > CLASSES, 2.0, 1.0) * task_of, task_of, jnp.pad(task_scales, (0, LANES - 3))]
     )
     outs = head_weight.shape[1]
-    wide_row = ((0, 0), (0, LANES - outs))
-    info = jnp.stack(
-        [labels.reshape(pixels).astype(jnp.float32), keep, valid, *geometry_target.reshape(4, pixels)],
-        axis=1,
-    )
     devices = lax.axis_size("rows") * lax.axis_size("cols")
     crop_rows = CROPS * channels // LANES
     piece = -(-crop_rows // devices)
-    crop_sums = jnp.pad(local_sums.reshape(crop_rows, LANES), ((0, piece * devices - crop_rows), (0, 0)))
+    crop_sums = jnp.pad(local_sums, ((0, piece * devices - crop_rows), (0, 0)))
     crop_sums = jnp.pad(
         crop_sums.reshape(devices, piece, LANES), ((0, 0), (0, -piece % 8), (0, 0))
     )
-    branch_low, proj_part, head_part, crop_local, crop_pre, sums_five, sums_four, crop_table = pyramid(
+    branch_low, proj_part, head_part, crop_local, crop_pre, sums_five, sums_four, crop_table, own_low, closing = pyramid(
         height,
         trunk,
         jnp.pad(sep_depth.reshape(27, channels).astype(jnp.float32), ((0, 5), (0, 0))),
         sep_point,
         aspp_point,
         crop_part,
-        jnp.broadcast_to(crop_count[:, None], (CROPS, aspp_width)),
+        count_sums,
         members,
         proj_weight,
-        jnp.pad(aspp_gain, ((0, 3), (0, 0))),
-        jnp.pad(aspp_shift, ((0, 3), (0, 0))),
-        jnp.pad(head_weight, wide_row),
-        jnp.pad(jnp.broadcast_to(head_bias, (8, outs)), wide_row),
-        jnp.broadcast_to(factors, (8, LANES)),
-        jnp.pad(info, ((0, 0), (0, 1))),
+        aspp_gain,
+        aspp_shift,
+        head_weight,
+        head_bias.reshape(1, outs),
+        jnp.pad(weights, ((0, 5), (0, 0))),
+        labels,
+        boundary_mask,
+        valid_mask,
+        geometry_target,
         crop_sums,
     )
-    crop_table = crop_table[:, :piece].reshape(-1, LANES)[:crop_rows].reshape(CROPS, channels)
+    crop_table = crop_table[:, :piece].reshape(-1, LANES)[:crop_rows].reshape(-1, CROPS, LANES)
+    crop_table = jnp.transpose(crop_table, (1, 0, 2)).reshape(CROPS, channels)
     per = aspp_width // LANES
     proj_shift_grad = sums_five[:per].reshape(1, aspp_width)
     proj_gain_grad = sums_five[per : 2 * per].reshape(1, aspp_width)
-    loss_row = sums_five[2 * per]
     grad_head_bias = sums_five[2 * per + 1, :outs]
     branch_shift_grad = sums_four[: 4 * per].reshape(4, aspp_width)
     branch_gain_grad = sums_four[4 * per :].reshape(4, aspp_width)
-    loss_sums = jnp.stack(
-        [loss_row[0], loss_row[CLASSES], jnp.sum(loss_row[CLASSES + 1 : CLASSES + 4])]
-    )
-    losses = loss_sums / counts
-    objective = jnp.sum(scale_exp * losses - task_scales)
-    grad_scales = scale_exp * losses - 1.0
+    objective, grad_scales = closing[1, 0], closing[0, :3]
     near, early, crop_total = pyramid_weights(
         branch_low.reshape(4, height, width, aspp_width),
         trunk,
@@ -2162,7 +2286,7 @@
     crop_rest = (pooled_grad - crop_high.astype(jnp.float32)).astype(low)
     pre_low, expand_part, dilated_low, sums_three, sums_two, early_sum = trunk_back(
         near,
-        branch_low[0],
+        own_low,
         jnp.pad(sep_depth.reshape(27, channels).astype(jnp.float32).T, ((0, 0), (0, LANES - 27))),
         sep_point,
         aspp_point,
@@ -2196,29 +2320,26 @@
     )
     one_shift_grad, one_gain_grad = sums_one.reshape(2, 1, middle)
     grad_features = grad_features.reshape(height, width, channels)
-    expand_sum = expand_sum[:channels].reshape(-1, middle, middle)
-    grad_expand_weight = jnp.transpose(expand_sum, (1, 0, 2)).reshape(middle, channels)
-    first, second = early_sum[:channels], early_sum[channels : 2 * channels]
-    sep_sum = jnp.stack([first[:, :aspp_width], first[:, aspp_width:], second[:, :aspp_width]])
+    sep_sum, point_sum, grad_expand_weight, dilated_wide, reduce_wide = widen(
+        early_sum, expand_sum, dilated_sum, reduce_sum, channels, aspp_width
+    )
     at = 2 * channels
     tables = []
     for size, extent in ((proj_weight.shape[0], aspp_width), (channels, LANES), (aspp_width, LANES)):
         blocks = 2 * aspp_width // extent
         table = early_sum[at : at + size // blocks].reshape(size // blocks, blocks, extent)
+        table = table.astype(jnp.float32)
         tables.append(jnp.transpose(table, (1, 0, 2)).reshape(size, extent))
         at += size // blocks
     summed = [
-        value.astype(jnp.float32)
-        for value in (
-            reduce_sum[:channels],
-            dilated_sum[: 9 * middle].reshape(9, middle, middle),
-            grad_expand_weight,
-            second[:, aspp_width:],
-            tables[1][:, :27].T.reshape(3, 9, channels),
-            sep_sum,
-            tables[0],
-            tables[2],
-        )
+        reduce_wide,
+        dilated_wide.reshape(9, middle, middle),
+        grad_expand_weight,
+        point_sum,
+        tables[1][:, :27].T.reshape(3, 9, channels),
+        sep_sum,
+        tables[0],
+        tables[2],
     ]
     grad_mid_gain = jnp.concatenate([one_gain_grad, two_gain_grad], axis=0)
     grad_mid_shift = jnp.concatenate([one_shift_grad, two_shift_grad], axis=0)

time: 691 us -> 653 us (0.945)
  other arithmetic: 36.5 us -> 6.68 us
  local copies, waits for them, and re-layouts: 34.3 us -> 20.2 us
  Pallas kernels: 604 us -> 614 us
    convert_element_type x7 -> x0, other arithmetic: 15.6 us -> none  [the longest x5 14.6 us: on_device(): value.astype(jnp.float32)]
    pallas_call x1, Pallas kernels: 152 us -> 161 us  [tail(): pl.pallas_call(functools.partial(tail_kernel), out_shape=outs, in_specs=[...]
    pallas_call x1 -> x2, Pallas kernels: 106 us -> 107 us  [the longest x1 91.9 us: front(): pl.pallas_call(front_kernel, out_shape=outs, in_specs=[whole] * 12, out_s...]
where the time goes in v5:
time: 653 us; the launch traced here: 645 us
  Pallas kernels  614 us (94%)
  local copies, waits for them, and re-layouts  20.2 us (3%)
  other arithmetic  6.68 us (1%)
    pallas_call x1, Pallas kernels, tail(): pl.pallas_call(functools.partial(tail_kernel), out_shape=outs, in_specs=[...  161 us
    pallas_call x1, Pallas kernels, trunk_back(): pl.pallas_call(trunk_back_kernel, out_shape=outs, in_specs=[away] + [whol...  140 us
    pallas_call x1, Pallas kernels, pyramid(): pl.pallas_call(functools.partial(pyramid_kernel, height), out_shape=outs,...  130 us
    pallas_call x1, Pallas kernels, front(): pl.pallas_call(front_kernel, out_shape=outs, in_specs=[whole] * 12, out_s...  91.9 us
    pallas_call x1, Pallas kernels, pyramid_weights(): pl.pallas_call(pyramid_weights_kernel, out_shape=outs, in_specs=[whole] *...  76.9 us
    pallas_call x1, Pallas kernels, widen(): pl.pallas_call(widen_kernel, grid=(steps,), out_shape=(shape((3, channels...  14.6 us

profile of v5, /device:TPU:11, one launch (start us, length us, event | category | flops | bytes accessed | tf_op | source)
XLA Modules:
  0.0 644.7 jit_solution(11924432746763468117)
XLA Ops:
  0.7 91.9 %front.1 = (f32[1024,512]{1,0:T(8,128)}, bf16[1024,512]{1,0:T(8,128)(2,1)}, f32[1024,512]{1,0:T(8,128)}, bf16[1024,512]{1,0:T(8,128)(2,1)}, f32[1024,2048]{1,0:T...) custom-call(bf16[1024,2048]{1,0:T(8,128)(2,1)} %bitcast.67, ...), custom_call_target="tpu_custom_call" | custom-call | tf_op jit(solution)/shard_map/front/pallas_call | solution.py:1644
  92.7 0.6 fusion.11
  93.3 1.9 fusion.5
  95.2 0.6 select_maximum_fusion.weights
  96.0 0.7 pad.21.depth
  96.7 0.7 copy.49.head_raw
  97.4 129.5 %pyramid.1 = (bf16[4,1024,256]{2,1,0:T(8,128)(2,1)}, bf16[1280,256]{1,0:T(8,128)(2,1)}, bf16[256,128]{1,0:T(8,128)(2,1)}, f32[16,256]{1,0:T(8,128)}, f32[16,256]...) custom-call(bf16[1024,2048]{1,0:T(8,128)(2,1)} %get-tuple-element.61, ...), custom_call_target="tpu_custom_call" | custom-call | flops 53687091200 | bytes 134217728 | tf_op jit(solution)/shard_map/pyramid/pallas_call | solution.py:657
  227.3 1.0 pad.24.depth
  228.4 76.9 %pyramid_weights.1 = (bf16[3,3,4,352,256]{4,3,2,1,0:T(8,128)(2,1)}, bf16[5632,512]{1,0:T(8,128)(2,1)}, f32[16,256]{1,0:T(8,128)}) custom-call(bf16[4,4,256,256]{3,2,1,0:T(8,128)(2,1)} %bitcast.90, bf16[1024,2048]{1,0:T(8,128)(2,1)} %get-tuple-element.61.trunk, f32[2048,128]{1,0:T(8,128)} %pad.24.depth, bf16[3,2048,256]{2,1,0:T(8,128)(2,1)} %sep_point.5, ...), custom_call_target="tpu_custom_call" | custom-call | flops 53687091200 | bytes 134217728 | tf_op jit(solution)/shard_map/pyramid_weights/pallas_call | solution.py:904
  305.3 0.7 multiply_convert_fusion
  306.0 0.7 slice_bitcast_fusion.4
  307.1 0.9 fusion.crop_rest
  307.9 0.8 pad_convert_fusion.crop_high
  308.8 140.2 %trunk_back.1 = (bf16[1024,2048]{1,0:T(8,128)(2,1)}, bf16[2048,512]{1,0:T(8,128)(2,1)}, bf16[1024,512]{1,0:T(8,128)(2,1)}, f32[32,128]{1,0:T(8,128)}, f32[8,128]{1,0:T(8,128)}, /*index=5*/bf16[5632,512]{1,0:T(8,128)(2,1)}) custom-call(bf16[3,3,4,352,256]{4,3,2,1,0:T(8,128)(2,1)} %get-tuple-element.71.near, bf16[1024,256]{1,0:T(8,128)(2,1)} %get-tuple-element.72.own_low, ...), custom_call_target="tpu_custom_call" | custom-call | flops 42949672960 | bytes 134217728 | tf_op jit(solution)/shard_map/trunk_back/pallas_call | solution.py:1205
  449.0 161.0 %tail.1 = (bf16[1024,2048]{1,0:T(8,128)(2,1)}, bf16[2048,512]{1,0:T(8,128)(2,1)}, bf16[4608,512]{1,0:T(8,128)(2,1)}, bf16[2048,512]{1,0:T(8,128)(2,1)}, f32[8,128]{1,0:T(8,128)}) custom-call(bf16[1024,512]{1,0:T(8,128)(2,1)} %get-tuple-element.81.dilated_low, bf16[1024,512]{1,0:T(8,128)(2,1)} %get-tuple-element.82.first_act, ...), custom_call_target="tpu_custom_call" | custom-call | flops 107374182400 | bytes 536870912 | tf_op jit(solution)/shard_map/tail/pallas_call | solution.py:2106
  610.0 0.8 fusion.9
  610.8 0.6 pad_maximum_fusion.2
  611.4 14.6 %widen.1 = (f32[3,2048,256]{2,1,0:T(8,128)}, f32[2048,256]{1,0:T(8,128)}, f32[512,2048]{1,0:T(8,128)}, f32[4608,512]{1,0:T(8,128)}, f32[2048,512]{1,0:T(8,128)}) custom-call(bf16[5632,512]{1,0:T(8,128)(2,1)} %get-tuple-element.88.first.second, bf16[5632,512]{1,0:T(8,128)(2,1)} %get-tuple-element.88.first.second, bf16[4,512,512]{2,1,0:T(8,128)(2,1)} %bitcast.70, ...), custom_call_target="tpu_custom_call" | custom-call | tf_op jit(solution)/shard_map/widen/pallas_call | solution.py:2144
  626.1 0.6 pad_maximum_fusion
  626.8 1.9 fusion.2
  628.7 1.2 slice_convert_fusion
  629.9 0.8 reshape.193
  630.8 1.2 copy.54
  632.0 1.1 copy_bitcast_fusion
  633.5 0.9 copy.56
  634.4 0.9 copy_bitcast_fusion.1
  635.3 0.7 copy.57
  636.0 0.6 fusion.6
  636.6 1.2 slice.65
  637.8 1.2 slice_bitcast_fusion.2
  639.0 0.5 slice_bitcast_fusion.3
  639.5 4.8 copy.66
  (44 shorter events, 1.5 us)
Async XLA Ops:
  0.7 92.0 %copy-start.13 = (f32[3]{0:T(128)S(1)}, f32[3]{0:T(128)}, u32[]{:S(2)}) copy-start(f32[3]{0:T(128)} %param.40) | copy-start | bytes 40
  0.7 95.2 %copy-start.1 = (bf16[3,9,2048]{2,0,1:T(4,128)(2,1)S(1)}, bf16[3,9,2048]{2,0,1:T(4,128)(2,1)}, u32[]{:S(2)}) copy-start(bf16[3,9,2048]{2,0,1:T(4,128)(2,1)} %param.32) | copy-start | bytes 331780
  0.7 96.0 %copy-start.7 = (bf16[256,17]{0,1:T(8,128)(2,1)S(1)}, bf16[256,17]{0,1:T(8,128)(2,1)}, u32[]{:S(2)}) copy-start(bf16[256,17]{0,1:T(8,128)(2,1)} %param.38) | copy-start | bytes 26116
  228.4 76.9 %copy-start.6 = (f32[16,256]{1,0:T(8,128)S(1)}, f32[16,256]{1,0:T(8,128)}, u32[]{:S(2)}) copy-start(f32[16,256]{1,0:T(8,128)} %get-tuple-element.74) | copy-start | bytes 49156
  228.4 78.4 %copy-start = (bf16[2048,256]{1,0:T(8,128)(2,1)S(1)}, bf16[2048,256]{1,0:T(8,128)(2,1)}, u32[]{:S(2)}) copy-start(bf16[2048,256]{1,0:T(8,128)(2,1)} %pool_weight.1) | copy-start | bytes 3145732
  306.0 2.8 copy-start.3
  306.7 2.1 copy-start.10
  449.0 161.8 %copy-start.9 = (f32[8,128]{1,0:T(8,128)S(1)}, f32[8,128]{1,0:T(8,128)}, u32[]{:S(2)}) copy-start(f32[8,128]{1,0:T(8,128)} %get-tuple-element.96) | copy-start | bytes 12292
  611.4 14.7 %copy-start.12 = (f32[8,128]{1,0:T(8,128)S(1)}, f32[8,128]{1,0:T(8,128)}, u32[]{:S(2)}) copy-start(f32[8,128]{1,0:T(8,128)} %get-tuple-element.102) | copy-start | bytes 12292
  611.4 14.7 %copy-start.8 = (f32[16,128]{1,0:T(8,128)S(1)}, f32[16,128]{1,0:T(8,128)}, u32[]{:S(2)}) copy-start(f32[16,128]{1,0:T(8,128)} %get-tuple-element.101) | copy-start | bytes 24580
  611.4 15.3 %copy-start.2 = (f32[32,8,128]{2,1,0:T(8,128)S(1)}, f32[32,8,128]{2,1,0:T(8,128)}, u32[]{:S(2)}) copy-start(f32[32,8,128]{2,1,0:T(8,128)} %get-tuple-element.100) | copy-start | bytes 393220
  611.4 15.4 %copy-start.4 = (bf16[16,256]{1,0:T(8,128)(2,1)S(1)}, bf16[16,256]{1,0:T(8,128)(2,1)}, u32[]{:S(2)}) copy-start(bf16[16,256]{1,0:T(8,128)(2,1)} %copy-done.3) | copy-start | bytes 24580
  611.4 15.4 %copy-start.11 = (f32[16]{0:T(128)S(1)}, f32[16]{0:T(128)}, u32[]{:S(2)}) copy-start(f32[16]{0:T(128)} %copy-done.10) | copy-start | bytes 196
  630.8 5.2 copy-start.5

commit v6 on v5

--- a/solution.py
+++ b/solution.py
@@ -325,7 +325,9 @@
         )
 
     def flush(number):
-        index, way = 2 - number // 3, lax.rem(2 * lax.rem(number, 3), 3)
+        own = number // 6
+        index = (1 - own) * (2 - number // 2) + own * (8 - number)
+        way = (1 - own) * 2 * lax.rem(number, 2) + own
         side_copy(index, way).wait_recv()
 
         @pl.when(way == 1)
@@ -345,11 +347,11 @@
             def _():
                 main_copy(index, way).start()
 
-    for index in (2, 1, 0):
+    for index, own in ((2, 0), (1, 0), (0, 0), (2, 1), (1, 1), (0, 1)):
         rate = BASE_RATE * (index + 1)
 
         def one_way(turn, carry):
-            way = lax.rem(2 * turn, 3)
+            way = 1 if own else 2 * turn
             for sign in (0, 1, -1):
                 tap = depth[pl.ds(index * 9 + 3 * way + 1 - sign, 1), :].astype(low)
                 made = jnp.dot(trunk[...] * tap, sep_point[index], preferred_element_type=wide)
@@ -364,19 +366,15 @@
                         field[line, at : at + width, :] += part
             send_side[index, way] = field[:, pl.ds(side_from, PAD), :].astype(low)
 
-            @pl.when(way == 1)
-            def _():
+            if own:
                 for line in range(height):
                     pre[index + 1, line * width : (line + 1) * width, :] = field[
                         line, PAD : PAD + width, :
                     ]
-
-            @pl.when(way != 1)
-            def _():
+            else:
                 send_main[index, way] = field[:, PAD : PAD + width, :].astype(low)
-
             side_copy(index, way).start()
-            number = 3 * (2 - index) + turn
+            number = turn + (8 - index if own else 2 * (2 - index))
 
             @pl.when(number > 0)
             def _():
@@ -384,8 +382,8 @@
 
             return carry
 
-        lax.fori_loop(0, 3, one_way, 0)
-    flush(8)
+        lax.fori_loop(0, 1 if own else 2, one_way, 0)
+    flush(jnp.int32(8))
     crop_total.start_column()
 
     def lines(body, carry=0):
@@ -845,8 +843,10 @@
                 return carry
 
             lax.fori_loop(0, 2, collect, 0)
-        if way == 1 and index > 0:
-            send(index)
+        if way == 1 and index == 2:
+            send(1)
+        if way == 2 and index == 0:
+            send(2)
         if way == 1 and index == 0:
             crop_sum.start_column()
         if way == 0 and index == 0:
@@ -1997,21 +1997,18 @@
                 act_turned[...], moved[...], preferred_element_type=wide
             ).astype(low)
 
-    expand_sum.start_level(0)
     halo.wait_own()
     one_way(1)
     halo.pass_first()
-    expand_sum.start_level(1)
     lax.fori_loop(0, channels // width, turn_features, 0)
     halo.pass_rest()
-    expand_sum.start_back(1)
     halo.wait_edges()
     one_way(halo.pair_way)
-    expand_sum.start_back(0)
     halo.wait_relay()
+    expand_sum.start_level(0)
     one_way(halo.far_way)
     dilated_sum.start_half()
-    expand_sum.start_back_half()
+    expand_sum.start_level(1)
     shift_sum, gain_sum = jnp.zeros((1, middle), wide), jnp.zeros((1, middle), wide)
     for line in range(height):
         span = slice(line * width, (line + 1) * width)
@@ -2042,6 +2039,7 @@
         features_turned[...], reduced_low[...], preferred_element_type=wide
     ).astype(low)
     reduce_sum.start_half()
+    expand_sum.start_back(1)
     chunk = 2 * LANES
 
     def last(block, carry):
@@ -2052,8 +2050,10 @@
 
     lax.fori_loop(0, channels // chunk, last, 0)
     reduce_sum.start_level(0)
+    expand_sum.start_back(0)
     dilated_sum.start_level(1)
     reduce_sum.start_level(1)
+    expand_sum.start_back_half()
     dilated_sum.start_back(1)
     reduce_sum.start_back(1)
     dilated_sum.start_back(0)

time: 653 us -> 636 us (0.974)
  Pallas kernels: 614 us -> 598 us
    pallas_call x1, Pallas kernels: 140 us -> 133 us  [trunk_back(): pl.pallas_call(trunk_back_kernel, out_shape=outs, in_specs=[away] + [whol...]
where the time goes in v6:
time: 636 us; the launch traced here: 628 us
  Pallas kernels  598 us (94%)
  local copies, waits for them, and re-layouts  20.2 us (3%)
  other arithmetic  6.68 us (1%)
    pallas_call x1, Pallas kernels, tail(): pl.pallas_call(functools.partial(tail_kernel), out_shape=outs, in_specs=[...  157 us
    pallas_call x1, Pallas kernels, trunk_back(): pl.pallas_call(trunk_back_kernel, out_shape=outs, in_specs=[away] + [whol...  133 us
    pallas_call x1, Pallas kernels, pyramid(): pl.pallas_call(functools.partial(pyramid_kernel, height), out_shape=outs,...  124 us
    pallas_call x1, Pallas kernels, front(): pl.pallas_call(front_kernel, out_shape=outs, in_specs=[whole] * 12, out_s...  91.9 us
    pallas_call x1, Pallas kernels, pyramid_weights(): pl.pallas_call(pyramid_weights_kernel, out_shape=outs, in_specs=[whole] *...  77.9 us
    pallas_call x1, Pallas kernels, widen(): pl.pallas_call(widen_kernel, grid=(steps,), out_shape=(shape((3, channels...  14.6 us

profile of v6, /device:TPU:11, one launch (start us, length us, event | category | flops | bytes accessed | tf_op | source)
XLA Modules:
  0.0 628.1 jit_solution(5155125322505483248)
XLA Ops:
  0.7 91.9 %front.1 = (f32[1024,512]{1,0:T(8,128)}, bf16[1024,512]{1,0:T(8,128)(2,1)}, f32[1024,512]{1,0:T(8,128)}, bf16[1024,512]{1,0:T(8,128)(2,1)}, f32[1024,2048]{1,0:T...) custom-call(bf16[1024,2048]{1,0:T(8,128)(2,1)} %bitcast.67, ...), custom_call_target="tpu_custom_call" | custom-call | tf_op jit(solution)/shard_map/front/pallas_call | solution.py:1644
  92.7 0.6 fusion.11
  93.3 1.9 fusion.5
  95.2 0.6 select_maximum_fusion.weights
  96.0 0.7 pad.21.depth
  96.7 0.7 copy.49.head_raw
  97.4 123.7 %pyramid.1 = (bf16[4,1024,256]{2,1,0:T(8,128)(2,1)}, bf16[1280,256]{1,0:T(8,128)(2,1)}, bf16[256,128]{1,0:T(8,128)(2,1)}, f32[16,256]{1,0:T(8,128)}, f32[16,256]...) custom-call(bf16[1024,2048]{1,0:T(8,128)(2,1)} %get-tuple-element.61, ...), custom_call_target="tpu_custom_call" | custom-call | flops 53687091200 | bytes 134217728 | tf_op jit(solution)/shard_map/pyramid/pallas_call | solution.py:655
  221.5 1.0 pad.24.depth
  222.6 77.9 %pyramid_weights.1 = (bf16[3,3,4,352,256]{4,3,2,1,0:T(8,128)(2,1)}, bf16[5632,512]{1,0:T(8,128)(2,1)}, f32[16,256]{1,0:T(8,128)}) custom-call(bf16[4,4,256,256]{3,2,1,0:T(8,128)(2,1)} %bitcast.90, bf16[1024,2048]{1,0:T(8,128)(2,1)} %get-tuple-element.61.trunk, f32[2048,128]{1,0:T(8,128)} %pad.24.depth, bf16[3,2048,256]{2,1,0:T(8,128)(2,1)} %sep_point.5, ...), custom_call_target="tpu_custom_call" | custom-call | flops 53687091200 | bytes 134217728 | tf_op jit(solution)/shard_map/pyramid_weights/pallas_call | solution.py:904
  300.5 0.7 multiply_convert_fusion
  301.2 0.7 slice_bitcast_fusion.4
  302.3 0.9 fusion.crop_rest
  303.1 0.8 pad_convert_fusion.crop_high
  304.0 132.5 %trunk_back.1 = (bf16[1024,2048]{1,0:T(8,128)(2,1)}, bf16[2048,512]{1,0:T(8,128)(2,1)}, bf16[1024,512]{1,0:T(8,128)(2,1)}, f32[32,128]{1,0:T(8,128)}, f32[8,128]{1,0:T(8,128)}, /*index=5*/bf16[5632,512]{1,0:T(8,128)(2,1)}) custom-call(bf16[3,3,4,352,256]{4,3,2,1,0:T(8,128)(2,1)} %get-tuple-element.71.near, bf16[1024,256]{1,0:T(8,128)(2,1)} %get-tuple-element.72.own_low, ...), custom_call_target="tpu_custom_call" | custom-call | flops 42949672960 | bytes 134217728 | tf_op jit(solution)/shard_map/trunk_back/pallas_call | solution.py:1205
  436.5 157.2 %tail.1 = (bf16[1024,2048]{1,0:T(8,128)(2,1)}, bf16[2048,512]{1,0:T(8,128)(2,1)}, bf16[4608,512]{1,0:T(8,128)(2,1)}, bf16[2048,512]{1,0:T(8,128)(2,1)}, f32[8,128]{1,0:T(8,128)}) custom-call(bf16[1024,512]{1,0:T(8,128)(2,1)} %get-tuple-element.81.dilated_low, bf16[1024,512]{1,0:T(8,128)(2,1)} %get-tuple-element.82.first_act, ...), custom_call_target="tpu_custom_call" | custom-call | flops 107374182400 | bytes 536870912 | tf_op jit(solution)/shard_map/tail/pallas_call | solution.py:2106
  593.7 0.8 fusion.9
  594.5 0.6 pad_maximum_fusion.2
  595.1 14.6 %widen.1 = (f32[3,2048,256]{2,1,0:T(8,128)}, f32[2048,256]{1,0:T(8,128)}, f32[512,2048]{1,0:T(8,128)}, f32[4608,512]{1,0:T(8,128)}, f32[2048,512]{1,0:T(8,128)}) custom-call(bf16[5632,512]{1,0:T(8,128)(2,1)} %get-tuple-element.88.first.second, bf16[5632,512]{1,0:T(8,128)(2,1)} %get-tuple-element.88.first.second, bf16[4,512,512]{2,1,0:T(8,128)(2,1)} %bitcast.70, ...), custom_call_target="tpu_custom_call" | custom-call | tf_op jit(solution)/shard_map/widen/pallas_call | solution.py:2144
  609.8 0.6 pad_maximum_fusion
  610.5 1.9 fusion.2
  612.4 1.2 slice_convert_fusion
  613.6 0.8 reshape.193
  614.5 1.2 copy.54
  615.6 1.1 copy_bitcast_fusion
  617.2 0.9 copy.56
  618.1 0.9 copy_bitcast_fusion.1
  619.0 0.7 copy.57
  619.7 0.6 fusion.6
  620.3 1.2 slice.65
  621.5 1.2 slice_bitcast_fusion.2
  622.7 0.5 slice_bitcast_fusion.3
  623.2 4.8 copy.66
  (44 shorter events, 1.5 us)
Async XLA Ops:
  0.7 92.0 %copy-start.13 = (f32[3]{0:T(128)S(1)}, f32[3]{0:T(128)}, u32[]{:S(2)}) copy-start(f32[3]{0:T(128)} %param.40) | copy-start | bytes 40
  0.7 95.2 %copy-start.1 = (bf16[3,9,2048]{2,0,1:T(4,128)(2,1)S(1)}, bf16[3,9,2048]{2,0,1:T(4,128)(2,1)}, u32[]{:S(2)}) copy-start(bf16[3,9,2048]{2,0,1:T(4,128)(2,1)} %param.32) | copy-start | bytes 331780
  0.7 96.0 %copy-start.7 = (bf16[256,17]{0,1:T(8,128)(2,1)S(1)}, bf16[256,17]{0,1:T(8,128)(2,1)}, u32[]{:S(2)}) copy-start(bf16[256,17]{0,1:T(8,128)(2,1)} %param.38) | copy-start | bytes 26116
  222.6 77.9 %copy-start.6 = (f32[16,256]{1,0:T(8,128)S(1)}, f32[16,256]{1,0:T(8,128)}, u32[]{:S(2)}) copy-start(f32[16,256]{1,0:T(8,128)} %get-tuple-element.74) | copy-start | bytes 49156
  222.6 79.3 %copy-start = (bf16[2048,256]{1,0:T(8,128)(2,1)S(1)}, bf16[2048,256]{1,0:T(8,128)(2,1)}, u32[]{:S(2)}) copy-start(bf16[2048,256]{1,0:T(8,128)(2,1)} %pool_weight.1) | copy-start | bytes 3145732
  301.2 2.8 copy-start.3
  301.9 2.1 copy-start.10
  436.5 158.0 %copy-start.9 = (f32[8,128]{1,0:T(8,128)S(1)}, f32[8,128]{1,0:T(8,128)}, u32[]{:S(2)}) copy-start(f32[8,128]{1,0:T(8,128)} %get-tuple-element.96) | copy-start | bytes 12292
  595.1 14.7 %copy-start.12 = (f32[8,128]{1,0:T(8,128)S(1)}, f32[8,128]{1,0:T(8,128)}, u32[]{:S(2)}) copy-start(f32[8,128]{1,0:T(8,128)} %get-tuple-element.102) | copy-start | bytes 12292
  595.1 14.7 %copy-start.8 = (f32[16,128]{1,0:T(8,128)S(1)}, f32[16,128]{1,0:T(8,128)}, u32[]{:S(2)}) copy-start(f32[16,128]{1,0:T(8,128)} %get-tuple-element.101) | copy-start | bytes 24580
  595.1 15.3 %copy-start.2 = (f32[32,8,128]{2,1,0:T(8,128)S(1)}, f32[32,8,128]{2,1,0:T(8,128)}, u32[]{:S(2)}) copy-start(f32[32,8,128]{2,1,0:T(8,128)} %get-tuple-element.100) | copy-start | bytes 393220
  595.1 15.4 %copy-start.4 = (bf16[16,256]{1,0:T(8,128)(2,1)S(1)}, bf16[16,256]{1,0:T(8,128)(2,1)}, u32[]{:S(2)}) copy-start(bf16[16,256]{1,0:T(8,128)(2,1)} %copy-done.3) | copy-start | bytes 24580
  595.1 15.4 %copy-start.11 = (f32[16]{0:T(128)S(1)}, f32[16]{0:T(128)}, u32[]{:S(2)}) copy-start(f32[16]{0:T(128)} %copy-done.10) | copy-start | bytes 196
  614.5 5.2 copy-start.5

commit v7 on v6

--- a/solution.py
+++ b/solution.py
@@ -843,7 +843,7 @@
                 return carry
 
             lax.fori_loop(0, 2, collect, 0)
-        if way == 1 and index == 2:
+        if way == 1 and index == 1:
             send(1)
         if way == 2 and index == 0:
             send(2)
@@ -2135,7 +2135,7 @@
 def widen(early, expand, dilated, reduce, channels, aspp):
     middle = reduce.shape[1]
     wide = jnp.float32
-    steps = 8
+    steps = 16
     rows = channels // steps
     taps = 9 * middle // steps
     lines = middle // steps

time: 636 us -> 644 us (1.013)
  Pallas kernels: 598 us -> 606 us
    pallas_call x1, Pallas kernels: 77.9 us -> 86.1 us  [pyramid_weights(): pl.pallas_call(pyramid_weights_kernel, out_shape=outs, in_specs=[whole] *...]
where the time goes in v7:
time: 644 us; the launch traced here: 637 us
  Pallas kernels  606 us (94%)
  local copies, waits for them, and re-layouts  20.2 us (3%)
  other arithmetic  6.68 us (1%)
    pallas_call x1, Pallas kernels, tail(): pl.pallas_call(functools.partial(tail_kernel), out_shape=outs, in_specs=[...  155 us
    pallas_call x1, Pallas kernels, trunk_back(): pl.pallas_call(trunk_back_kernel, out_shape=outs, in_specs=[away] + [whol...  133 us
    pallas_call x1, Pallas kernels, pyramid(): pl.pallas_call(functools.partial(pyramid_kernel, height), out_shape=outs,...  124 us
    pallas_call x1, Pallas kernels, front(): pl.pallas_call(front_kernel, out_shape=outs, in_specs=[whole] * 12, out_s...  91.9 us
    pallas_call x1, Pallas kernels, pyramid_weights(): pl.pallas_call(pyramid_weights_kernel, out_shape=outs, in_specs=[whole] *...  86.1 us
    pallas_call x1, Pallas kernels, widen(): pl.pallas_call(widen_kernel, grid=(steps,), out_shape=(shape((3, channels...  16.7 us

profile of v7, /device:TPU:11, one launch (start us, length us, event | category | flops | bytes accessed | tf_op | source)
XLA Modules:
  0.0 636.5 jit_solution(2501297904358959988)
XLA Ops:
  0.7 91.9 %front.1 = (f32[1024,512]{1,0:T(8,128)}, bf16[1024,512]{1,0:T(8,128)(2,1)}, f32[1024,512]{1,0:T(8,128)}, bf16[1024,512]{1,0:T(8,128)(2,1)}, f32[1024,2048]{1,0:T...) custom-call(bf16[1024,2048]{1,0:T(8,128)(2,1)} %bitcast.67, ...), custom_call_target="tpu_custom_call" | custom-call | tf_op jit(solution)/shard_map/front/pallas_call | solution.py:1644
  92.7 0.6 fusion.11
  93.3 1.9 fusion.5
  95.2 0.6 select_maximum_fusion.weights
  96.0 0.7 pad.21.depth
  96.7 0.7 copy.49.head_raw
  97.4 123.7 %pyramid.1 = (bf16[4,1024,256]{2,1,0:T(8,128)(2,1)}, bf16[1280,256]{1,0:T(8,128)(2,1)}, bf16[256,128]{1,0:T(8,128)(2,1)}, f32[16,256]{1,0:T(8,128)}, f32[16,256]...) custom-call(bf16[1024,2048]{1,0:T(8,128)(2,1)} %get-tuple-element.61, ...), custom_call_target="tpu_custom_call" | custom-call | flops 53687091200 | bytes 134217728 | tf_op jit(solution)/shard_map/pyramid/pallas_call | solution.py:655
  221.5 1.0 pad.24.depth
  222.6 86.1 %pyramid_weights.1 = (bf16[3,3,4,352,256]{4,3,2,1,0:T(8,128)(2,1)}, bf16[5632,512]{1,0:T(8,128)(2,1)}, f32[16,256]{1,0:T(8,128)}) custom-call(bf16[4,4,256,256]{3,2,1,0:T(8,128)(2,1)} %bitcast.90, bf16[1024,2048]{1,0:T(8,128)(2,1)} %get-tuple-element.61.trunk, f32[2048,128]{1,0:T(8,128)} %pad.24.depth, bf16[3,2048,256]{2,1,0:T(8,128)(2,1)} %sep_point.5, ...), custom_call_target="tpu_custom_call" | custom-call | flops 53687091200 | bytes 134217728 | tf_op jit(solution)/shard_map/pyramid_weights/pallas_call | solution.py:904
  308.7 0.7 multiply_convert_fusion
  309.4 0.7 slice_bitcast_fusion.4
  310.5 0.9 fusion.crop_rest
  311.3 0.8 pad_convert_fusion.crop_high
  312.2 132.5 %trunk_back.1 = (bf16[1024,2048]{1,0:T(8,128)(2,1)}, bf16[2048,512]{1,0:T(8,128)(2,1)}, bf16[1024,512]{1,0:T(8,128)(2,1)}, f32[32,128]{1,0:T(8,128)}, f32[8,128]{1,0:T(8,128)}, /*index=5*/bf16[5632,512]{1,0:T(8,128)(2,1)}) custom-call(bf16[3,3,4,352,256]{4,3,2,1,0:T(8,128)(2,1)} %get-tuple-element.71.near, bf16[1024,256]{1,0:T(8,128)(2,1)} %get-tuple-element.72.own_low, ...), custom_call_target="tpu_custom_call" | custom-call | flops 42949672960 | bytes 134217728 | tf_op jit(solution)/shard_map/trunk_back/pallas_call | solution.py:1205
  444.7 155.3 %tail.1 = (bf16[1024,2048]{1,0:T(8,128)(2,1)}, bf16[2048,512]{1,0:T(8,128)(2,1)}, bf16[4608,512]{1,0:T(8,128)(2,1)}, bf16[2048,512]{1,0:T(8,128)(2,1)}, f32[8,128]{1,0:T(8,128)}) custom-call(bf16[1024,512]{1,0:T(8,128)(2,1)} %get-tuple-element.81.dilated_low, bf16[1024,512]{1,0:T(8,128)(2,1)} %get-tuple-element.82.first_act, ...), custom_call_target="tpu_custom_call" | custom-call | flops 107374182400 | bytes 536870912 | tf_op jit(solution)/shard_map/tail/pallas_call | solution.py:2106
  600.0 0.8 fusion.9
  600.8 0.6 pad_maximum_fusion.2
  601.4 16.7 %widen.1 = (f32[3,2048,256]{2,1,0:T(8,128)}, f32[2048,256]{1,0:T(8,128)}, f32[512,2048]{1,0:T(8,128)}, f32[4608,512]{1,0:T(8,128)}, f32[2048,512]{1,0:T(8,128)}) custom-call(bf16[5632,512]{1,0:T(8,128)(2,1)} %get-tuple-element.88.first.second, bf16[5632,512]{1,0:T(8,128)(2,1)} %get-tuple-element.88.first.second, bf16[4,512,512]{2,1,0:T(8,128)(2,1)} %bitcast.70, ...), custom_call_target="tpu_custom_call" | custom-call | tf_op jit(solution)/shard_map/widen/pallas_call | solution.py:2144
  618.2 0.6 pad_maximum_fusion
  618.9 1.9 fusion.2
  620.7 1.2 slice_convert_fusion
  622.0 0.8 reshape.193
  622.9 1.2 copy.54
  624.0 1.1 copy_bitcast_fusion
  625.6 0.9 copy.56
  626.5 0.9 copy_bitcast_fusion.1
  627.4 0.7 copy.57
  628.0 0.6 fusion.6
  628.7 1.2 slice.65
  629.8 1.2 slice_bitcast_fusion.2
  631.0 0.5 slice_bitcast_fusion.3
  631.6 4.8 copy.66
  (44 shorter events, 1.5 us)
Async XLA Ops:
  0.7 92.0 %copy-start.13 = (f32[3]{0:T(128)S(1)}, f32[3]{0:T(128)}, u32[]{:S(2)}) copy-start(f32[3]{0:T(128)} %param.40) | copy-start | bytes 40
  0.7 95.2 %copy-start.1 = (bf16[3,9,2048]{2,0,1:T(4,128)(2,1)S(1)}, bf16[3,9,2048]{2,0,1:T(4,128)(2,1)}, u32[]{:S(2)}) copy-start(bf16[3,9,2048]{2,0,1:T(4,128)(2,1)} %param.32) | copy-start | bytes 331780
  0.7 96.0 %copy-start.7 = (bf16[256,17]{0,1:T(8,128)(2,1)S(1)}, bf16[256,17]{0,1:T(8,128)(2,1)}, u32[]{:S(2)}) copy-start(bf16[256,17]{0,1:T(8,128)(2,1)} %param.38) | copy-start | bytes 26116
  222.6 86.1 %copy-start.6 = (f32[16,256]{1,0:T(8,128)S(1)}, f32[16,256]{1,0:T(8,128)}, u32[]{:S(2)}) copy-start(f32[16,256]{1,0:T(8,128)} %get-tuple-element.74) | copy-start | bytes 49156
  222.6 87.5 %copy-start = (bf16[2048,256]{1,0:T(8,128)(2,1)S(1)}, bf16[2048,256]{1,0:T(8,128)(2,1)}, u32[]{:S(2)}) copy-start(bf16[2048,256]{1,0:T(8,128)(2,1)} %pool_weight.1) | copy-start | bytes 3145732
  309.4 2.8 copy-start.3
  310.1 2.1 copy-start.10
  444.7 156.1 %copy-start.9 = (f32[8,128]{1,0:T(8,128)S(1)}, f32[8,128]{1,0:T(8,128)}, u32[]{:S(2)}) copy-start(f32[8,128]{1,0:T(8,128)} %get-tuple-element.96) | copy-start | bytes 12292
  601.4 16.7 %copy-start.12 = (f32[8,128]{1,0:T(8,128)S(1)}, f32[8,128]{1,0:T(8,128)}, u32[]{:S(2)}) copy-start(f32[8,128]{1,0:T(8,128)} %get-tuple-element.102) | copy-start | bytes 12292
  601.4 16.7 %copy-start.8 = (f32[16,128]{1,0:T(8,128)S(1)}, f32[16,128]{1,0:T(8,128)}, u32[]{:S(2)}) copy-start(f32[16,128]{1,0:T(8,128)} %get-tuple-element.101) | copy-start | bytes 24580
  601.4 17.4 %copy-start.2 = (f32[32,8,128]{2,1,0:T(8,128)S(1)}, f32[32,8,128]{2,1,0:T(8,128)}, u32[]{:S(2)}) copy-start(f32[32,8,128]{2,1,0:T(8,128)} %get-tuple-element.100) | copy-start | bytes 393220
  601.4 17.4 %copy-start.4 = (bf16[16,256]{1,0:T(8,128)(2,1)S(1)}, bf16[16,256]{1,0:T(8,128)(2,1)}, u32[]{:S(2)}) copy-start(bf16[16,256]{1,0:T(8,128)(2,1)} %copy-done.3) | copy-start | bytes 24580
  601.4 17.4 %copy-start.11 = (f32[16]{0:T(128)S(1)}, f32[16]{0:T(128)}, u32[]{:S(2)}) copy-start(f32[16]{0:T(128)} %copy-done.10) | copy-start | bytes 196
  622.8 5.2 copy-start.5
